TPU v7x, 32 devices: a whole 2x2x4 slice. The times are simulated.
32 devices in a mesh: groups: 2 (over x), gx: 16 (over z, y, core).
Axes of the slice: x: 2, y: 2, z: 4, core: 2. Of those that a mesh axis runs over, the one named last changes fastest.
Arguments:
- activations: bfloat16 [256, 16384], P('groups', 'gx'), parts along dimension 0, may hold values from -400 to 400
- norm_gain: bfloat16 [16384], P('gx'), may hold values from 0.099609375 to 1.8984375
- w_qkv: bfloat16 [16384, 9216], P('gx'), may hold values from -0.046875 to 0.046875
- w_out: bfloat16 [8192, 16384], P(None, 'gx'), may hold values from -0.0625 to 0.0625
- cache_keys: bfloat16 [256, 256, 4, 128], P(('groups', 'gx')), parts along dimension 0, may hold values from -420 to 420
- value_cache_rows: bfloat16 [256, 256, 4, 128], P(('groups', 'gx')), parts along dimension 0, may hold values from -6 to 6
Outputs:
- attention_out: bfloat16 [256, 16384], P('groups', 'gx'), parts along dimension 0
There are 2 independent parts, one for each index of `groups`. A program takes and returns all parts, laid end to end along the dimension named above; an argument that names none is the same for every part. Nothing has to cross between parts.
All inputs are finite; a program needn't handle non-finite values.
Results may differ from a plain program's by a relative error of at most 0.012.
Values may be sent and summed in bfloat16 or wider, within the bound.
No kernel may reach another device: no remote copies, remote signals or barrier semaphores. Data moves between devices by JAX's collectives and lax.ppermute only.
A program may use at most 128 MiB of HBM per device.

v0:
```python
import jax
import jax.numpy as jnp
from jax import lax
from jax.sharding import PartitionSpec as P

D = 16384
QUERY_HEADS = 64
KEY_VALUE_HEADS = 4
HEAD_SIZE = 128
CONTEXT_LENGTH = 256


def apply_rotary(tensor):
    half_dim = HEAD_SIZE // 2
    frequency = jnp.float32(500000.0) ** (
        -jnp.arange(half_dim, dtype=jnp.float32) * 2.0 / HEAD_SIZE
    )
    angles = jnp.float32(CONTEXT_LENGTH) * frequency
    cosine = jnp.cos(angles)
    sine_part = jnp.sin(angles)
    first_half = tensor[..., :half_dim]
    second_half = tensor[..., half_dim:]
    return jnp.concatenate(
        [
            first_half * cosine - second_half * sine_part,
            second_half * cosine + first_half * sine_part,
        ],
        axis=-1,
    )


def attend(query_rows, fresh_keys, fresh_values, cache_keys, value_cache_rows):
    count_of_rows = query_rows.shape[0]
    grouped_queries = query_rows.reshape(
        count_of_rows, KEY_VALUE_HEADS, QUERY_HEADS // KEY_VALUE_HEADS, HEAD_SIZE
    )
    scaling = 1.0 / jnp.sqrt(jnp.float32(HEAD_SIZE))
    cached_scores = (
        jnp.einsum(
            "rkgd,rtkd->rkgt", grouped_queries, cache_keys, preferred_element_type=jnp.float32
        )
        * scaling
    )
    own_scores = (
        jnp.einsum("rkgd,rkd->rkg", grouped_queries, fresh_keys, preferred_element_type=jnp.float32)
        * scaling
    )
    highest = jnp.maximum(jnp.max(cached_scores, axis=-1), own_scores)
    cached_exp = jnp.exp(cached_scores - highest[..., None])
    own_exp = jnp.exp(own_scores - highest)
    denominator = jnp.sum(cached_exp, axis=-1) + own_exp
    cached_weights = (cached_exp / denominator[..., None]).astype(jnp.bfloat16)
    own_weights = (own_exp / denominator).astype(jnp.bfloat16)
    combined = jnp.einsum(
        "rkgt,rtkd->rkgd", cached_weights, value_cache_rows, preferred_element_type=jnp.float32
    )
    combined = (
        combined
        + own_weights.astype(jnp.float32)[..., None]
        * fresh_values.astype(jnp.float32)[:, :, None, :]
    )
    return combined.reshape(count_of_rows, QUERY_HEADS * HEAD_SIZE).astype(jnp.bfloat16)


def body(activations, norm_gain, w_qkv, w_out, cache_keys, value_cache_rows):
    count_of_rows = cache_keys.shape[0]
    query_width = QUERY_HEADS * HEAD_SIZE
    wide_acts = activations.astype(jnp.float32)
    local_squares = jnp.sum(wide_acts * wide_acts, axis=1)
    scaled = (wide_acts * norm_gain.astype(jnp.float32)).astype(jnp.bfloat16)
    partial_sums = jnp.dot(scaled, w_qkv, preferred_element_type=jnp.float32)
    own_sums, own_squares = (
        lax.psum_scatter(partial_sums, "gx", scatter_dimension=0, tiled=True),
        lax.psum_scatter(local_squares, "gx", scatter_dimension=0, tiled=True),
    )
    query_sums = own_sums[:, :query_width]
    other_sums = own_sums[:, query_width:]
    inverse_rms = lax.rsqrt(own_squares / D + 1e-05)[:, None]
    query_rows = apply_rotary(
        (query_sums * inverse_rms).reshape(count_of_rows, QUERY_HEADS, HEAD_SIZE)
    ).astype(jnp.bfloat16)
    other_rescaled = other_sums * inverse_rms
    fresh_keys = apply_rotary(
        other_rescaled[:, : KEY_VALUE_HEADS * HEAD_SIZE].reshape(
            count_of_rows, KEY_VALUE_HEADS, HEAD_SIZE
        )
    ).astype(jnp.bfloat16)
    fresh_values = (
        other_rescaled[:, KEY_VALUE_HEADS * HEAD_SIZE :]
        .reshape(count_of_rows, KEY_VALUE_HEADS, HEAD_SIZE)
        .astype(jnp.bfloat16)
    )
    attended = attend(query_rows, fresh_keys, fresh_values, cache_keys, value_cache_rows)
    projected_out = jnp.dot(
        lax.all_gather(attended, "gx", axis=0, tiled=True),
        w_out,
        preferred_element_type=jnp.float32,
    )
    return projected_out.astype(jnp.bfloat16)


def solution(mesh):
    return jax.shard_map(
        body,
        mesh=mesh,
        in_specs=(
            P("groups", "gx"),
            P("gx"),
            P("gx", None),
            P(None, "gx"),
            P(("groups", "gx"), None, None, None),
            P(("groups", "gx"), None, None, None),
        ),
        out_specs=P("groups", "gx"),
        check_vma=False,
    )
```

profile of v0, /device:TPU:0, one launch (start us, length us, event | category | flops | bytes accessed | tf_op | source)
XLA Modules:
  0.0 158.9 jit_solution(11669009872884582651)
XLA Ops:
  6.5 0.0 copy-start
  6.5 0.0 reduce-scatter.2.cloned.1.call-start
  6.5 0.8 convert_element_type.47
  7.4 11.2 %fusion.16 = f32[128,9216]{1,0:T(8,128)} fusion(bf16[1024,9216]{1,0:T(8,128)(2,1)} %param.8, bf16[128,1024]{1,0:T(8,128)(2,1)} %param.6, f32[1024]{0:T(1024)S(1)} %convert_element_type.47), kind=kOutput, calls=%fused_computation.15 | convolution fusion | flops 2416312320 | bytes 23859200 | tf_op jit(solution)/shard_map/dot_general | solution.py:71
  18.6 0.0 copy-start.3
  18.6 0.0 copy-start.1
  18.6 0.0 reduce-scatter.2.cloned.1.call-update
  18.6 0.0 all-gather.2.cloned.1.call-start
  18.7 0.6 copy-done.3
  19.2 0.6 dynamic-slice
  20.5 0.0 copy-done.1
  20.5 0.1 fusion.14
  20.6 35.1 %all-reduce = f32[128]{0:T(128)S(1)} all-reduce(f32[128]{0:T(128)S(1)} %fusion.14), channel_id=3, replica_groups=mesh['groups'=2,'gx'=16] {'gx'}, use_global_device_ids=true, to_apply=%region_2.0.clone | all-reduce | flops 128 | bytes 1024
  55.7 0.1 fusion.29
  55.8 0.1 fusion.30
  55.9 41.1 %reduce-scatter.2.cloned.1.call-done = f32[8,9216]{1,0:T(8,128)} async-done(((f32[128,9216]{1,0:T(8,128)}), f32[8,9216]{1,0:T(8,128)}) %reduce-scatter.2.cloned.1.call-update) | async-done | bytes 294928 | tf_op jit(solution)/shard_map/reduce_scatter | solution.py:73
  97.0 0.8 slice_multiply_fusion.1
  97.8 0.1 subtract_convert_fusion.1
  97.9 1.0 fusion.18
  98.9 0.1 subtract_convert_fusion
  99.1 0.0 copy-start.2
  99.2 0.1 maximum_bitcast_fusion
  99.2 0.2 fusion.22
  99.5 0.0 copy-done
  99.5 0.8 fusion.34
  100.3 0.3 fusion.15
  100.7 0.1 copy-done.2
  100.7 0.5 fusion.10
  101.2 0.8 copy.35
  102.0 0.0 all-gather.2.cloned.1.call-update
  102.0 40.6 %all-gather.2.cloned.1.call-done = bf16[128,8192]{1,0:T(8,128)(2,1)} async-done(((bf16[8,8192]{1,0:T(8,128)(2,1)}), bf16[128,8192]{1,0:T(8,128)(2,1)}) %all-gather.2.cloned.1.call-update) | async-done | bytes 2097168 | tf_op jit(solution)/shard_map/all_gather | solution.py:95
  142.6 9.4 %convolution_convert_fusion = bf16[128,1024]{1,0:T(8,128)(2,1)} fusion(bf16[128,8192]{1,0:T(8,128)(2,1)} %all-gather.2.cloned.1.call-done, bf16[8192,1024]{1,0:T(8,128)(2,1)} %param.9), kind=kOutput, calls=%fused_computation.5 | convolution fusion | flops 2147614720 | bytes 19136512 | tf_op jit(solution)/shard_map/dot_general | solution.py:94
  (7 shorter events, 0.1 us)
Async XLA Ops:
  6.5 93.0 %copy-start = (bf16[8,256,4,128]{3,2,1,0:T(4,128)(2,1)S(1)}, bf16[8,256,4,128]{3,2,1,0:T(4,128)(2,1)}, u32[]{:S(2)}) copy-start(bf16[8,256,4,128]{3,2,1,0:T(4,128)(2,1)} %param.10) | copy-start | bytes 6291460
  6.5 90.5 %reduce-scatter.2.cloned.1.call-start = ((), (), s32[]{:S(2)}) async-start(), calls=%async_computation.1 | async-start | bytes 5013504 | tf_op jit(solution)/shard_map/reduce_scatter | solution.py:73
  18.6 0.7 copy-start.3
  18.6 1.9 %copy-start.1 = (bf16[128,1024]{1,0:T(8,128)(2,1)S(1)}, bf16[128,1024]{1,0:T(8,128)(2,1)}, u32[]{:S(2)}) copy-start(bf16[128,1024]{1,0:T(8,128)(2,1)} %param.6) | copy-start | bytes 786436
  18.6 124.0 %all-gather.2.cloned.1.call-start = ((), (), s32[]{:S(2)}) async-start(), calls=%async_computation.2 | async-start | bytes 2228224 | tf_op jit(solution)/shard_map/all_gather | solution.py:95
  99.1 1.6 %copy-start.2 = (bf16[8,256,4,128]{3,2,1,0:T(4,128)(2,1)S(1)}, bf16[8,256,4,128]{3,2,1,0:T(4,128)(2,1)}, u32[]{:S(2)}) copy-start(bf16[8,256,4,128]{3,2,1,0:T(4,128)(2,1)} %param.11) | copy-start | bytes 6291460
Sparse Core Ops, SparseCore 0:
  18.7 78.2 reduce-scatter.1
  102.1 40.4 all-gather.1
where the time goes:
time: 159 us
  waiting for transfers between devices  81.7 us (51%)
  blocking collectives  35.1 us (22%)
  matrix products  22.2 us (14%)
  between operations  14.2 us (9%)
  other arithmetic  3.59 us (2%)
  local copies, waits for them, and re-layouts  2.04 us (1%)
    reduce_scatter x1, waiting for transfers between devices, body(): lax.psum_scatter(partial_sums, 'gx', scatter_dimension=0, tiled=True)  41.1 us
    all_gather x1, waiting for transfers between devices, body(): lax.all_gather(attended, 'gx', axis=0, tiled=True)  40.6 us
    unnamed x1, blocking collectives  35.1 us
    dot_general x1, matrix products, body(): partial_sums = jnp.dot(scaled, w_qkv, preferred_element_type=jnp.float32)  11.2 us
    dot_general x1, matrix products, body(): jnp.dot(lax.all_gather(attended, 'gx', axis=0, tiled=True), w_out, prefer...  9.44 us
  transfers between devices with their start and end apart: 2, of which 2 were waited for; matrix products, arithmetic and copies ran while one was open for 1% of the time, Pallas kernels for 0%

commit v1 on v0

v1 whole, which is shorter than its diff:
```python
import functools

import jax
import jax.numpy as jnp
from jax import lax
from jax.experimental import pallas as pl
from jax.experimental.pallas import tpu as pltpu
from jax.sharding import PartitionSpec as P

D = 16384
QUERY_HEADS = 64
KEY_VALUE_HEADS = 4
HEAD_SIZE = 128
CONTEXT_LENGTH = 256
GROUP = QUERY_HEADS // KEY_VALUE_HEADS
QUERY_WIDTH = QUERY_HEADS * HEAD_SIZE
QKVW = QUERY_WIDTH + 2 * KEY_VALUE_HEADS * HEAD_SIZE
TILE = 1024
LANES = 128
MIB = 1024 * 1024
CHUNKS = ((2, 4), (0, 2))


def bit_reverse(position, count):
    result = 0
    while count > 1:
        result = result * 2 + position % 2
        position //= 2
        count //= 2
    return result


def projection_kernel(
    count, rows, tiles, with_squares,
    me_ref, acts_ref, gain_ref, w_ref, send_ref, keep_ref, wide, scaled,
):
    step = pl.program_id(0)
    half = count * rows // 2
    me = me_ref[0]

    @pl.when(step == 0)
    def _():
        wide[...] = acts_ref[...].astype(jnp.float32)
        gain = gain_ref[...].astype(jnp.float32)
        for pair in range(count // 2):
            parts = []
            for position in (2 * pair, 2 * pair + 1):
                source = jnp.bitwise_xor(me, bit_reverse(position, count))
                start = pl.multiple_of(source * rows, rows)
                parts.append(wide[pl.ds(start, rows), :])
            both = jnp.concatenate(parts, axis=0)
            where = pl.ds(2 * pair * rows, 2 * rows)
            scaled[where, :] = (both * gain).astype(jnp.bfloat16)
            if with_squares:
                squares = jnp.sum(both * both, axis=1, keepdims=True)
                high = squares.astype(jnp.bfloat16).astype(jnp.float32)
                lane = lax.broadcasted_iota(jnp.int32, (2 * rows, LANES), 1)
                lanes = jnp.where(lane == 2 * me, high, 0.0)
                lanes = jnp.where(lane == 2 * me + 1, squares - high, lanes)
                if 2 * pair < count // 2:
                    keep_ref[where, tiles * TILE :] = lanes
                else:
                    send_ref[pl.ds(2 * pair * rows - half, 2 * rows), tiles * TILE :] = (
                        lanes.astype(jnp.bfloat16)
                    )

    product = jnp.dot(scaled[...], w_ref[...], preferred_element_type=jnp.float32)
    columns = pl.ds(pl.multiple_of(step * TILE, TILE), TILE)
    keep_ref[:, columns] = product[:half]
    send_ref[:, columns] = product[half:].astype(jnp.bfloat16)


def project(me, activations, gain, w_qkv, count, rows, start, width, with_squares):
    tiles = width // TILE
    depth = w_qkv.shape[0]
    half = count * rows // 2
    whole = width + (LANES if with_squares else 0)
    return pl.pallas_call(
        functools.partial(projection_kernel, count, rows, tiles, with_squares),
        grid_spec=pltpu.PrefetchScalarGridSpec(
            num_scalar_prefetch=1,
            grid=(tiles,),
            in_specs=[
                pl.BlockSpec(activations.shape, lambda j, me: (0, 0)),
                pl.BlockSpec((1, depth), lambda j, me: (0, 0)),
                pl.BlockSpec((depth, TILE), lambda j, me: (0, start // TILE + j)),
            ],
            out_specs=[
                pl.BlockSpec((half, whole), lambda j, me: (0, 0)),
                pl.BlockSpec((half, whole), lambda j, me: (0, 0)),
            ],
            scratch_shapes=[
                pltpu.VMEM(activations.shape, jnp.float32),
                pltpu.VMEM(activations.shape, jnp.bfloat16),
            ],
        ),
        out_shape=[
            jax.ShapeDtypeStruct((half, whole), jnp.bfloat16),
            jax.ShapeDtypeStruct((half, whole), jnp.float32),
        ],
        compiler_params=pltpu.CompilerParams(vmem_limit_bytes=32 * MIB),
        cost_estimate=pl.CostEstimate(
            flops=4 * half * depth * width,
            bytes_accessed=2 * depth * width + 6 * half * whole,
            transcendentals=0,
        ),
    )(me, activations, gain, w_qkv)


def output_kernel(
    count, rows, tiles, first, last, me_ref, *refs
):
    mine_ref, other_ref, w_ref = refs[:3]
    refs = refs[3:]
    if not first:
        before_ref, refs = refs[0], refs[1:]
    out_ref, total = refs[0], refs[1]
    step = pl.program_id(0)
    columns = pl.ds(pl.multiple_of(step * TILE, TILE), TILE)
    left = jnp.concatenate([mine_ref[:, columns], other_ref[:, columns]], axis=0)
    product = jnp.dot(left, w_ref[...], preferred_element_type=jnp.float32)

    @pl.when(step == 0)
    def _():
        total[...] = product if first else before_ref[...] + product

    @pl.when(step > 0)
    def _():
        total[...] += product

    @pl.when(step == tiles - 1)
    def _():
        if not last:
            out_ref[...] = total[...]
            return
        reversed_me = me_ref[1]
        for pair in range(count // 2):
            parts = []
            for block in (2 * pair, 2 * pair + 1):
                reversed_block = bit_reverse(block, count)
                position = jnp.bitwise_xor(reversed_me, reversed_block)
                parts.append(total[pl.ds(pl.multiple_of(position * rows, rows), rows), :])
            out_ref[pl.ds(2 * pair * rows, 2 * rows), :] = jnp.concatenate(
                parts, axis=0
            ).astype(jnp.bfloat16)


def output_part(me, mine, other, w_out, before, count, rows, start, last):
    width = mine.shape[1]
    tiles = width // TILE
    columns = w_out.shape[1]
    whole = lambda j, me: (0, 0)
    in_specs = [
        pl.BlockSpec(mine.shape, whole),
        pl.BlockSpec(other.shape, whole),
        pl.BlockSpec((TILE, columns), lambda j, me: (start // TILE + j, 0)),
    ]
    operands = [mine, other, w_out]
    first = before is None
    if not first:
        in_specs.append(pl.BlockSpec(before.shape, whole))
        operands.append(before)
    shape = (count * rows, columns)
    return pl.pallas_call(
        functools.partial(output_kernel, count, rows, tiles, first, last),
        grid_spec=pltpu.PrefetchScalarGridSpec(
            num_scalar_prefetch=1,
            grid=(tiles,),
            in_specs=in_specs,
            out_specs=pl.BlockSpec(shape, whole),
            scratch_shapes=[pltpu.VMEM(shape, jnp.float32)],
        ),
        out_shape=jax.ShapeDtypeStruct(shape, jnp.bfloat16 if last else jnp.float32),
        compiler_params=pltpu.CompilerParams(vmem_limit_bytes=32 * MIB),
        cost_estimate=pl.CostEstimate(
            flops=2 * shape[0] * width * columns,
            bytes_accessed=2 * width * columns + 2 * shape[0] * (width + columns),
            transcendentals=0,
        ),
    )(me, *operands)


def rotation():
    half_dim = HEAD_SIZE // 2
    frequency = jnp.float32(500000.0) ** (
        -jnp.arange(half_dim, dtype=jnp.float32) * 2.0 / HEAD_SIZE
    )
    angles = jnp.float32(CONTEXT_LENGTH) * frequency
    return jnp.cos(angles), jnp.sin(angles)


def apply_rotary(tensor):
    half_dim = HEAD_SIZE // 2
    cosine, sine_part = rotation()
    first_half = tensor[..., :half_dim]
    second_half = tensor[..., half_dim:]
    return jnp.concatenate(
        [
            first_half * cosine - second_half * sine_part,
            second_half * cosine + first_half * sine_part,
        ],
        axis=-1,
    )


def attend(query_rows, fresh_keys, fresh_values, cache_keys, value_cache_rows):
    count_of_rows, heads = fresh_keys.shape[:2]
    grouped_queries = query_rows.reshape(count_of_rows, heads, GROUP, HEAD_SIZE)
    scaling = 1.0 / jnp.sqrt(jnp.float32(HEAD_SIZE))
    cached_scores = (
        jnp.einsum(
            "rkgd,rtkd->rkgt", grouped_queries, cache_keys, preferred_element_type=jnp.float32
        )
        * scaling
    )
    own_scores = (
        jnp.einsum("rkgd,rkd->rkg", grouped_queries, fresh_keys, preferred_element_type=jnp.float32)
        * scaling
    )
    highest = jnp.maximum(jnp.max(cached_scores, axis=-1), own_scores)
    cached_exp = jnp.exp(cached_scores - highest[..., None])
    own_exp = jnp.exp(own_scores - highest)
    denominator = jnp.sum(cached_exp, axis=-1) + own_exp
    cached_weights = (cached_exp / denominator[..., None]).astype(jnp.bfloat16)
    own_weights = (own_exp / denominator).astype(jnp.bfloat16)
    combined = jnp.einsum(
        "rkgt,rtkd->rkgd", cached_weights, value_cache_rows, preferred_element_type=jnp.float32
    )
    combined = (
        combined
        + own_weights.astype(jnp.float32)[..., None]
        * fresh_values.astype(jnp.float32)[:, :, None, :]
    )
    return combined.reshape(count_of_rows, heads * GROUP * HEAD_SIZE).astype(jnp.bfloat16)


def swap(value, count, bit):
    return lax.ppermute(value, "gx", [(i, i ^ bit) for i in range(count)])


def reduce_rows(send, keep, count, rows):
    size, bit = count // 2, 1
    received = [swap(send, count, bit)]
    while size > 1:
        size, bit = size // 2, bit * 2
        part = slice(size * rows, 2 * size * rows)
        total = keep[part]
        for piece in received:
            total = total + piece[part].astype(jnp.float32)
        received.append(swap(total.astype(jnp.bfloat16), count, bit))
    total = keep[:rows]
    for piece in received:
        total = total + piece[:rows].astype(jnp.float32)
    return total


def gather_rows(own, count):
    bit = count // 2
    mine = own
    while bit > 1:
        mine = jnp.concatenate([mine, swap(mine, count, bit)], axis=0)
        bit //= 2
    return mine, swap(mine, count, 1)


def body(count, activations, norm_gain, w_qkv, w_out, cache_keys, value_cache_rows):
    rows = cache_keys.shape[0]
    index = lax.axis_index("gx").astype(jnp.int32)
    reversed_index = jnp.int32(0)
    bit = 1
    while bit < count:
        reversed_index = reversed_index * 2 + (index // bit) % 2
        bit *= 2
    me = jnp.stack([index, reversed_index])
    gain = norm_gain[None, :]
    per_head = GROUP * HEAD_SIZE

    sums = []
    for order, (low, high) in enumerate(CHUNKS):
        first = order == 0
        start = low * per_head
        width = (QKVW if first else high * per_head) - start
        send, keep = project(
            me, activations, gain, w_qkv, count, rows, start, width, first
        )
        sums.append(reduce_rows(send, keep, count, rows))

    lead = sums[0]
    width = (CHUNKS[0][1] - CHUNKS[0][0]) * per_head
    own_squares = jnp.sum(lead[:, -LANES:], axis=1)
    inverse_rms = lax.rsqrt(own_squares / D + 1e-05)[:, None]
    fresh = lead[:, width:-LANES] * inverse_rms
    kv_width = KEY_VALUE_HEADS * HEAD_SIZE
    shape = (rows, KEY_VALUE_HEADS, HEAD_SIZE)
    fresh_keys = apply_rotary(fresh[:, :kv_width].reshape(shape)).astype(jnp.bfloat16)
    fresh_values = fresh[:, kv_width:].reshape(shape).astype(jnp.bfloat16)

    total = None
    for order, (low, high) in enumerate(CHUNKS):
        width = (high - low) * per_head
        queries = apply_rotary(
            (sums[order][:, :width] * inverse_rms).reshape(rows, width // HEAD_SIZE, HEAD_SIZE)
        ).astype(jnp.bfloat16)
        attended = attend(
            queries,
            fresh_keys[:, low:high],
            fresh_values[:, low:high],
            cache_keys[:, :, low:high],
            value_cache_rows[:, :, low:high],
        )
        mine, other = gather_rows(attended, count)
        total = output_part(
            me, mine, other, w_out, total, count, rows, low * per_head,
            order == len(CHUNKS) - 1,
        )
    return total


def solution(mesh):
    return jax.shard_map(
        functools.partial(body, mesh.shape["gx"]),
        mesh=mesh,
        in_specs=(
            P("groups", "gx"),
            P("gx"),
            P("gx", None),
            P(None, "gx"),
            P(("groups", "gx"), None, None, None),
            P(("groups", "gx"), None, None, None),
        ),
        out_specs=P("groups", "gx"),
        check_vma=False,
    )
```

time: 159 us -> 89.3 us (0.56)
  waiting for transfers between devices: 81.7 us -> 26 us
  blocking collectives: 35.1 us -> 0 us
  starting transfers between devices: 0.04 us -> 23.4 us
  local copies, waits for them, and re-layouts: 2.04 us -> 22.8 us
  matrix products: 22.2 us -> 2.1 us
  between operations: 14.2 us -> 0.37 us
  Pallas kernels: 0 us -> 12.7 us
  other arithmetic: 3.59 us -> 1.64 us
    reduce_scatter x1 -> x0, waiting for transfers between devices: 41.1 us -> none  [body(): lax.psum_scatter(partial_sums, 'gx', scatter_dimension=0, tiled=True)]
    all_gather x1 -> x0, waiting for transfers between devices: 40.6 us -> none  [body(): lax.all_gather(attended, 'gx', axis=0, tiled=True)]
    unnamed x1 -> x0, blocking collectives: 35.1 us -> none
    ppermute x0 -> x16, waiting for transfers between devices: none -> 26 us  [swap(): return lax.ppermute(value, 'gx', [(i, i ^ bit) for i in range(count)])]
    ppermute x0 -> x16, starting transfers between devices: none -> 23.4 us  [swap(): return lax.ppermute(value, 'gx', [(i, i ^ bit) for i in range(count)])]
    dot_general x2 -> x0, matrix products: 20.7 us -> none  [the longest x1 11.2 us: body(): partial_sums = jnp.dot(scaled, w_qkv, preferred_element_type=jnp.float32)]
    unnamed x10 -> x20, local copies, waits for them, and re-layouts: 1.99 us -> 19 us
    pallas_call x0 -> x4, Pallas kernels: none -> 12.7 us  [the longest x2 6.78 us: project(): pl.pallas_call(functools.partial(projection_kernel, count, rows, tiles, w...]
  transfers between devices with their start and end apart: 2 -> 16, of which waited for: 2 -> 11; matrix products, arithmetic and copies ran while one was open for 1% -> 6% of each run, Pallas kernels for 0% -> 6%
where the time goes in v1:
time: 89.3 us; the launch traced here: 89 us
  waiting for transfers between devices  26 us (29%)
  starting transfers between devices  23.4 us (26%)
  local copies, waits for them, and re-layouts  22.8 us (26%)
  Pallas kernels  12.7 us (14%)
  matrix products  2.1 us (2%)
  other arithmetic  1.64 us (2%)
    ppermute x16, waiting for transfers between devices, swap(): return lax.ppermute(value, 'gx', [(i, i ^ bit) for i in range(count)])  26 us
    ppermute x16, starting transfers between devices, swap(): return lax.ppermute(value, 'gx', [(i, i ^ bit) for i in range(count)])  23.4 us
    unnamed x20, local copies, waits for them, and re-layouts  19 us
    pallas_call x2, Pallas kernels, project(): pl.pallas_call(functools.partial(projection_kernel, count, rows, tiles, w...  6.78 us
    pallas_call x2, Pallas kernels, output_part(): pl.pallas_call(functools.partial(output_kernel, count, rows, tiles, first...  5.96 us
  transfers between devices with their start and end apart: 16, of which 11 were waited for; matrix products, arithmetic and copies ran while one was open for 6% of the time, Pallas kernels for 6%

profile of v1, /device:TPU:0, one launch (start us, length us, event | category | flops | bytes accessed | tf_op | source)
XLA Modules:
  0.0 89.0 jit_solution(11505121521211543478)
XLA Ops:
  0.0 0.7 broadcast_in_dim.2.gain_ref
  0.7 0.1 pad_add_fusion.me_ref
  0.8 6.4 %copy-done = bf16[1024,9216]{1,0:T(8,128)(2,1)S(1)} copy-done((bf16[1024,9216]{1,0:T(8,128)(2,1)S(1)}, bf16[1024,9216]{1,0:T(8,128)(2,1)}, u32[]{:S(2)}) %copy-start) | copy-done | bytes 18874392
  7.1 0.9 %copy-done.3 = bf16[128,1024]{1,0:T(8,128)(2,1)S(1)} copy-done((bf16[128,1024]{1,0:T(8,128)(2,1)S(1)}, bf16[128,1024]{1,0:T(8,128)(2,1)}, u32[]{:S(2)}) %copy-start.3) | copy-done | bytes 262168
  8.1 3.8 %shard_map.65 = (bf16[64,5248]{1,0:T(8,128)(2,1)S(1)}, f32[64,5248]{1,0:T(8,128)S(1)}) custom-call(s32[2]{0:T(128)S(1)} %pad_add_fusion.me_ref, bf16[128,1024]{1,0:T(8,128)(2,1)S(1)} %copy-done.3, bf16[1,1024]{1,0:T(2,128)(2,1)S(1)} %broadcast_in_dim.2.gain_ref, bf16[1024,9216]{1,0:T(8,128)(2,1)S(1)} %copy-done), custom_call_target="tpu_custom_call" | custom-call | flops 1342177280 | bytes 12500992 | tf_op jit(solution)/shard_map/pallas_call | solution.py:78
  11.8 0.0 copy-start.4
  11.8 0.5 collective-permute-start.4
  12.4 3.0 %shard_map.64 = (bf16[64,4096]{1,0:T(8,128)(2,1)S(1)}, f32[64,4096]{1,0:T(8,128)S(1)}) custom-call(s32[2]{0:T(128)S(1)} %pad_add_fusion.me_ref, bf16[128,1024]{1,0:T(8,128)(2,1)S(1)} %copy-done.3, bf16[1,1024]{1,0:T(2,128)(2,1)S(1)} %broadcast_in_dim.2.gain_ref, bf16[1024,9216]{1,0:T(8,128)(2,1)S(1)} %copy-done), custom_call_target="tpu_custom_call" | custom-call | flops 1073741824 | bytes 9961472 | tf_op jit(solution)/shard_map/pallas_call | solution.py:78
  15.4 0.0 copy-start.5
  15.4 0.1 collective-permute-start
  15.5 1.5 %fusion.31 = (bf16[8,256,2,128]{3,2,1,0:T(2,128)(2,1)S(1)}, bf16[8,256,2,128]{3,2,1,0:T(2,128)(2,1)S(1)}) fusion(bf16[8,256,4,128]{3,2,1,0:T(4,128)(2,1)S(1)} %copy-done.4), kind=kLoop, calls=%fused_computation.88 | loop fusion | bytes 4194304 | tf_op jit(solution)/shard_map/slice | solution.py:308
  17.1 1.5 %fusion.32 = (bf16[8,256,2,128]{3,2,1,0:T(2,128)(2,1)S(1)}, bf16[8,256,2,128]{3,2,1,0:T(2,128)(2,1)S(1)}) fusion(bf16[8,256,4,128]{3,2,1,0:T(4,128)(2,1)S(1)} %copy-done.5), kind=kLoop, calls=%fused_computation.89 | loop fusion | bytes 4194304 | tf_op jit(solution)/shard_map/slice | solution.py:309
  18.6 0.0 collective-permute-done.4
  18.6 0.1 add_convert_fusion
  18.7 3.0 %collective-permute-start.5 = (bf16[32,5248]{1,0:T(8,128)(2,1)S(1)}, bf16[32,5248]{1,0:T(8,128)(2,1)S(1)}, u32[]{:S(2)}, u32[]{:S(2)}) collective-permute-start(bf16[32,5248]{1,0:T(8,128)(2,1)S(1)} %add_convert_fusion), channel_id=1, source_target_pairs={{0,2},{1,3},{2,0},{3,1},{4,6},{5,7},{6,4},{7,5},{8,10},{9,11},{10,... | collective-permute-start | bytes 1007624 | tf_op jit(solution)/shard_map/ppermute | solution.py:238
  21.7 0.0 collective-permute-done
  21.8 0.1 collective-permute-start.1
  21.9 8.5 %collective-permute-done.5 = bf16[32,5248]{1,0:T(8,128)(2,1)S(1)} collective-permute-done((bf16[32,5248]{1,0:T(8,128)(2,1)S(1)}, bf16[32,5248]{1,0:T(8,128)(2,1)S(1)}, u32[]{:S(2)}, u32[]{:S(2)}) %collective-permute-start.5) | collective-permute-done | bytes 335904 | tf_op jit(solution)/shard_map/ppermute | solution.py:238
  30.4 0.1 add_convert_fusion.2
  30.5 2.2 %collective-permute-start.6 = (bf16[16,5248]{1,0:T(8,128)(2,1)S(1)}, bf16[16,5248]{1,0:T(8,128)(2,1)S(1)}, u32[]{:S(2)}, u32[]{:S(2)}) collective-permute-start(bf16[16,5248]{1,0:T(8,128)(2,1)S(1)} %add_convert_fusion.2), channel_id=1, source_target_pairs={{0,4},{1,5},{2,6},{3,7},{4,0},{5,1},{6,2},{7,3},{8,12},{9,13},{10,... | collective-permute-start | bytes 503816 | tf_op jit(solution)/shard_map/ppermute | solution.py:238
  32.7 2.8 %collective-permute-done.1 = bf16[32,4096]{1,0:T(8,128)(2,1)S(1)} collective-permute-done((bf16[32,4096]{1,0:T(8,128)(2,1)S(1)}, bf16[32,4096]{1,0:T(8,128)(2,1)S(1)}, u32[]{:S(2)}, u32[]{:S(2)}) %collective-permute-start.1) | collective-permute-done | bytes 262176 | tf_op jit(solution)/shard_map/ppermute | solution.py:238
  35.5 1.9 %collective-permute-start.2 = (bf16[16,4096]{1,0:T(8,128)(2,1)S(1)}, bf16[16,4096]{1,0:T(8,128)(2,1)S(1)}, u32[]{:S(2)}, u32[]{:S(2)}) collective-permute-start(bf16[16,4096]{1,0:T(8,128)(2,1)S(1)} %add_convert_fusion.3), channel_id=1, source_target_pairs={{0,4},{1,5},{2,6},{3,7},{4,0},{5,1},{6,2},{7,3},{8,12},{9,13},{10,... | collective-permute-start | bytes 393224 | tf_op jit(solution)/shard_map/ppermute | solution.py:238
  37.4 0.0 collective-permute-done.6
  37.4 2.7 %collective-permute-start.7 = (bf16[8,5248]{1,0:T(8,128)(2,1)S(1)}, bf16[8,5248]{1,0:T(8,128)(2,1)S(1)}, u32[]{:S(2)}, u32[]{:S(2)}) collective-permute-start(bf16[8,5248]{1,0:T(8,128)(2,1)S(1)} %add_convert_fusion.4), channel_id=1, source_target_pairs={{0,8},{1,9},{2,10},{3,11},{4,12},{5,13},{6,14},{7,15},{8,0},{9,1},... | collective-permute-start | bytes 251912 | tf_op jit(solution)/shard_map/ppermute | solution.py:238
  40.1 1.4 %collective-permute-done.2 = bf16[16,4096]{1,0:T(8,128)(2,1)S(1)} collective-permute-done((bf16[16,4096]{1,0:T(8,128)(2,1)S(1)}, bf16[16,4096]{1,0:T(8,128)(2,1)S(1)}, u32[]{:S(2)}, u32[]{:S(2)}) %collective-permute-start.2) | collective-permute-done | bytes 131104 | tf_op jit(solution)/shard_map/ppermute | solution.py:238
  41.5 2.5 %collective-permute-start.3 = (bf16[8,4096]{1,0:T(8,128)(2,1)S(1)}, bf16[8,4096]{1,0:T(8,128)(2,1)S(1)}, u32[]{:S(2)}, u32[]{:S(2)}) collective-permute-start(bf16[8,4096]{1,0:T(8,128)(2,1)S(1)} %add_convert_fusion.7), channel_id=1, source_target_pairs={{0,8},{1,9},{2,10},{3,11},{4,12},{5,13},{6,14},{7,15},{8,0},{9,1},... | collective-permute-start | bytes 196616 | tf_op jit(solution)/shard_map/ppermute | solution.py:238
  44.0 0.5 collective-permute-done.7
  44.5 0.1 convert_add_fusion
  44.6 0.1 slice_reduce_fusion
  44.7 0.1 slice_multiply_fusion.1
  44.8 0.1 add_convert_fusion.8
  44.9 1.8 %collective-permute-done.3 = bf16[8,4096]{1,0:T(8,128)(2,1)S(1)} collective-permute-done((bf16[8,4096]{1,0:T(8,128)(2,1)S(1)}, bf16[8,4096]{1,0:T(8,128)(2,1)S(1)}, u32[]{:S(2)}, u32[]{:S(2)}) %collective-permute-start.3) | collective-permute-done | bytes 65568 | tf_op jit(solution)/shard_map/ppermute | solution.py:238
  46.7 0.1 fusion.8
  46.8 0.1 subtract_convert_fusion
  47.0 0.1 fusion.20
  47.1 0.2 fusion.13
  47.3 0.5 fusion.34
  47.8 0.2 fusion.7
  48.1 0.3 fusion.1
  48.5 2.5 %collective-permute-start.12 = (bf16[8,4096]{1,0:T(8,128)(2,1)S(1)}, bf16[8,4096]{1,0:T(8,128)(2,1)S(1)}, u32[]{:S(2)}, u32[]{:S(2)}) collective-permute-start(bf16[8,4096]{1,0:T(8,128)(2,1)S(1)} %bitcast.36), channel_id=1, source_target_pairs={{0,8},{1,9},{2,10},{3,11},{4,12},{5,13},{6,14},{7,15},{8,0},{9,1},... | collective-permute-start | bytes 196616 | tf_op jit(solution)/shard_map/ppermute | solution.py:238
  51.1 0.2 fusion.14
  51.3 0.5 fusion.33
  51.8 0.2 fusion.6
  52.1 0.3 fusion
  52.5 0.5 collective-permute-start.8
  53.0 1.1 %collective-permute-done.12 = bf16[8,4096]{1,0:T(8,128)(2,1)S(1)} collective-permute-done((bf16[8,4096]{1,0:T(8,128)(2,1)S(1)}, bf16[8,4096]{1,0:T(8,128)(2,1)S(1)}, u32[]{:S(2)}, u32[]{:S(2)}) %collective-permute-start.12) | collective-permute-done | bytes 65568 | tf_op jit(solution)/shard_map/ppermute | solution.py:238
  54.1 1.8 %collective-permute-start.13 = (bf16[16,4096]{1,0:T(8,128)(2,1)S(1)}, bf16[16,4096]{1,0:T(8,128)(2,1)S(1)}, u32[]{:S(2)}, u32[]{:S(2)}) collective-permute-start(bf16[16,4096]{1,0:T(8,128)(2,1)S(1)} %pad_maximum_fusion.3), channel_id=1, source_target_pairs={{0,4},{1,5},{2,6},{3,7},{4,0},{5,1},{6,2},{7,3},{8,12},{9,13},{10,... | collective-permute-start | bytes 393224 | tf_op jit(solution)/shard_map/ppermute | solution.py:238
  55.9 2.0 %collective-permute-done.8 = bf16[8,4096]{1,0:T(8,128)(2,1)S(1)} collective-permute-done((bf16[8,4096]{1,0:T(8,128)(2,1)S(1)}, bf16[8,4096]{1,0:T(8,128)(2,1)S(1)}, u32[]{:S(2)}, u32[]{:S(2)}) %collective-permute-start.8) | collective-permute-done | bytes 65568 | tf_op jit(solution)/shard_map/ppermute | solution.py:238
  57.9 2.2 %collective-permute-start.9 = (bf16[16,4096]{1,0:T(8,128)(2,1)S(1)}, bf16[16,4096]{1,0:T(8,128)(2,1)S(1)}, u32[]{:S(2)}, u32[]{:S(2)}) collective-permute-start(bf16[16,4096]{1,0:T(8,128)(2,1)S(1)} %pad_maximum_fusion.2), channel_id=1, source_target_pairs={{0,4},{1,5},{2,6},{3,7},{4,0},{5,1},{6,2},{7,3},{8,12},{9,13},{10,... | collective-permute-start | bytes 393224 | tf_op jit(solution)/shard_map/ppermute | solution.py:238
  60.1 0.3 collective-permute-done.13
  60.4 1.6 %collective-permute-start.14 = (bf16[32,4096]{1,0:T(8,128)(2,1)S(1)}, bf16[32,4096]{1,0:T(8,128)(2,1)S(1)}, u32[]{:S(2)}, u32[]{:S(2)}) collective-permute-start(bf16[32,4096]{1,0:T(8,128)(2,1)S(1)} %pad_maximum_fusion.1), channel_id=1, source_target_pairs={{0,2},{1,3},{2,0},{3,1},{4,6},{5,7},{6,4},{7,5},{8,10},{9,11},{10,... | collective-permute-start | bytes 786440 | tf_op jit(solution)/shard_map/ppermute | solution.py:238
  62.0 1.0 %collective-permute-done.9 = bf16[16,4096]{1,0:T(8,128)(2,1)S(1)} collective-permute-done((bf16[16,4096]{1,0:T(8,128)(2,1)S(1)}, bf16[16,4096]{1,0:T(8,128)(2,1)S(1)}, u32[]{:S(2)}, u32[]{:S(2)}) %collective-permute-start.9) | collective-permute-done | bytes 131104 | tf_op jit(solution)/shard_map/ppermute | solution.py:238
  63.1 1.6 %collective-permute-start.10 = (bf16[32,4096]{1,0:T(8,128)(2,1)S(1)}, bf16[32,4096]{1,0:T(8,128)(2,1)S(1)}, u32[]{:S(2)}, u32[]{:S(2)}) collective-permute-start(bf16[32,4096]{1,0:T(8,128)(2,1)S(1)} %pad_maximum_fusion), channel_id=1, source_target_pairs={{0,2},{1,3},{2,0},{3,1},{4,6},{5,7},{6,4},{7,5},{8,10},{9,11},{10,... | collective-permute-start | bytes 786440 | tf_op jit(solution)/shard_map/ppermute | solution.py:238
  64.7 3.9 %collective-permute-done.14 = bf16[32,4096]{1,0:T(8,128)(2,1)S(1)} collective-permute-done((bf16[32,4096]{1,0:T(8,128)(2,1)S(1)}, bf16[32,4096]{1,0:T(8,128)(2,1)S(1)}, u32[]{:S(2)}, u32[]{:S(2)}) %collective-permute-start.14) | collective-permute-done | bytes 262176 | tf_op jit(solution)/shard_map/ppermute | solution.py:238
  68.6 0.1 collective-permute-start.15
  68.7 2.7 %collective-permute-done.10 = bf16[32,4096]{1,0:T(8,128)(2,1)S(1)} collective-permute-done((bf16[32,4096]{1,0:T(8,128)(2,1)S(1)}, bf16[32,4096]{1,0:T(8,128)(2,1)S(1)}, u32[]{:S(2)}, u32[]{:S(2)}) %collective-permute-start.10) | collective-permute-done | bytes 262176 | tf_op jit(solution)/shard_map/ppermute | solution.py:238
  71.4 0.1 collective-permute-start.11
  71.5 0.0 collective-permute-done.15.refs_1_
  71.5 0.0 copy-start.1
  71.5 5.8 %copy-done.1 = bf16[8192,1024]{1,0:T(8,128)(2,1)S(1)} copy-done((bf16[8192,1024]{1,0:T(8,128)(2,1)S(1)}, bf16[8192,1024]{1,0:T(8,128)(2,1)}, u32[]{:S(2)}) %copy-start.1) | copy-done | bytes 16777240
  77.2 2.6 %shard_map.66.refs_3_ = f32[128,1024]{1,0:T(8,128)S(1)} custom-call(s32[2]{0:T(128)S(1)} %pad_add_fusion.me_ref, bf16[64,4096]{1,0:T(8,128)(2,1)S(1)} %constant_dynamic-update-slice_fusion.4.refs_0_, bf16[64,4096]{1,0:T(8,128)(2,1)S(1)} %collective-permute-done.15.refs_1_, bf16[8192,1024]{1,0:T(8,128)(2,1)S(1)} %copy-done.1), custom_call_target="tpu_custom_call" | custom-call | flops 1073741824 | bytes 9699328 | tf_op jit(solution)/shard_map/pallas_call | solution.py:164
  79.9 0.0 copy-start.2
  79.9 5.8 %copy-done.2 = bf16[8192,1024]{1,0:T(8,128)(2,1)S(1)} copy-done((bf16[8192,1024]{1,0:T(8,128)(2,1)S(1)}, bf16[8192,1024]{1,0:T(8,128)(2,1)}, u32[]{:S(2)}) %copy-start.2) | copy-done | bytes 16777240
  85.7 3.3 %shard_map.67 = bf16[128,1024]{1,0:T(8,128)(2,1)} custom-call(s32[2]{0:T(128)S(1)} %pad_add_fusion.me_ref, bf16[64,4096]{1,0:T(8,128)(2,1)S(1)} %constant_dynamic-update-slice_fusion.refs_0_, bf16[64,4096]{1,0:T(8,128)(2,1)S(1)} %collective-permute-done.11.refs_1_, bf16[8192,1024]{1,0:T(8,128)(2,1)S(1)} %copy-done.2, f32[128,1024]{1,0:T(8,128)S(1)} %shard_map.66.refs_3_), custom_call_target="tpu_custom_call" | custom-call | flops 1073741824 | bytes 9699328 | tf_op jit(solution)/shard_map/pallas_call | solution.py:164
  (38 shorter events, 0.6 us)
Async XLA Ops:
  0.8 6.4 %copy-start = (bf16[1024,9216]{1,0:T(8,128)(2,1)S(1)}, bf16[1024,9216]{1,0:T(8,128)(2,1)}, u32[]{:S(2)}) copy-start(bf16[1024,9216]{1,0:T(8,128)(2,1)} %w_ref.3) | copy-start | bytes 56623108
  7.1 0.9 %copy-start.3 = (bf16[128,1024]{1,0:T(8,128)(2,1)S(1)}, bf16[128,1024]{1,0:T(8,128)(2,1)}, u32[]{:S(2)}) copy-start(bf16[128,1024]{1,0:T(8,128)(2,1)} %acts_ref.3) | copy-start | bytes 786436
  11.8 3.7 %copy-start.4 = (bf16[8,256,4,128]{3,2,1,0:T(4,128)(2,1)S(1)}, bf16[8,256,4,128]{3,2,1,0:T(4,128)(2,1)}, u32[]{:S(2)}) copy-start(bf16[8,256,4,128]{3,2,1,0:T(4,128)(2,1)} %param.10) | copy-start | bytes 6291460
  11.8 6.8 %collective-permute-start.4 = (bf16[64,5248]{1,0:T(8,128)(2,1)S(1)}, bf16[64,5248]{1,0:T(8,128)(2,1)S(1)}, u32[]{:S(2)}, u32[]{:S(2)}) collective-permute-start(bf16[64,5248]{1,0:T(8,128)(2,1)S(1)} %get-tuple-element.12), channel_id=1, source_target_pairs={{0,1},{1,0},{2,3},{3,2},{4,5},{5,4},{6,7},{7,6},{8,9},{9,8},{10,11... | collective-permute-start | bytes 2015240 | tf_op jit(solution)/shard_map/ppermute | solution.py:238
  15.4 1.7 %copy-start.5 = (bf16[8,256,4,128]{3,2,1,0:T(4,128)(2,1)S(1)}, bf16[8,256,4,128]{3,2,1,0:T(4,128)(2,1)}, u32[]{:S(2)}) copy-start(bf16[8,256,4,128]{3,2,1,0:T(4,128)(2,1)} %param.11) | copy-start | bytes 6291460
  15.4 6.3 %collective-permute-start = (bf16[64,4096]{1,0:T(8,128)(2,1)S(1)}, bf16[64,4096]{1,0:T(8,128)(2,1)S(1)}, u32[]{:S(2)}, u32[]{:S(2)}) collective-permute-start(bf16[64,4096]{1,0:T(8,128)(2,1)S(1)} %get-tuple-element.10), channel_id=1, source_target_pairs={{0,1},{1,0},{2,3},{3,2},{4,5},{5,4},{6,7},{7,6},{8,9},{9,8},{10,11... | collective-permute-start | bytes 1572872 | tf_op jit(solution)/shard_map/ppermute | solution.py:238
  18.7 11.7 %collective-permute-start.5 = (bf16[32,5248]{1,0:T(8,128)(2,1)S(1)}, bf16[32,5248]{1,0:T(8,128)(2,1)S(1)}, u32[]{:S(2)}, u32[]{:S(2)}) collective-permute-start(bf16[32,5248]{1,0:T(8,128)(2,1)S(1)} %add_convert_fusion), channel_id=1, source_target_pairs={{0,2},{1,3},{2,0},{3,1},{4,6},{5,7},{6,4},{7,5},{8,10},{9,11},{10,... | collective-permute-start | bytes 1007624 | tf_op jit(solution)/shard_map/ppermute | solution.py:238
  21.8 13.7 %collective-permute-start.1 = (bf16[32,4096]{1,0:T(8,128)(2,1)S(1)}, bf16[32,4096]{1,0:T(8,128)(2,1)S(1)}, u32[]{:S(2)}, u32[]{:S(2)}) collective-permute-start(bf16[32,4096]{1,0:T(8,128)(2,1)S(1)} %add_convert_fusion.1), channel_id=1, source_target_pairs={{0,2},{1,3},{2,0},{3,1},{4,6},{5,7},{6,4},{7,5},{8,10},{9,11},{10,... | collective-permute-start | bytes 786440 | tf_op jit(solution)/shard_map/ppermute | solution.py:238
  30.5 6.9 %collective-permute-start.6 = (bf16[16,5248]{1,0:T(8,128)(2,1)S(1)}, bf16[16,5248]{1,0:T(8,128)(2,1)S(1)}, u32[]{:S(2)}, u32[]{:S(2)}) collective-permute-start(bf16[16,5248]{1,0:T(8,128)(2,1)S(1)} %add_convert_fusion.2), channel_id=1, source_target_pairs={{0,4},{1,5},{2,6},{3,7},{4,0},{5,1},{6,2},{7,3},{8,12},{9,13},{10,... | collective-permute-start | bytes 503816 | tf_op jit(solution)/shard_map/ppermute | solution.py:238
  35.5 5.9 %collective-permute-start.2 = (bf16[16,4096]{1,0:T(8,128)(2,1)S(1)}, bf16[16,4096]{1,0:T(8,128)(2,1)S(1)}, u32[]{:S(2)}, u32[]{:S(2)}) collective-permute-start(bf16[16,4096]{1,0:T(8,128)(2,1)S(1)} %add_convert_fusion.3), channel_id=1, source_target_pairs={{0,4},{1,5},{2,6},{3,7},{4,0},{5,1},{6,2},{7,3},{8,12},{9,13},{10,... | collective-permute-start | bytes 393224 | tf_op jit(solution)/shard_map/ppermute | solution.py:238
  37.4 7.1 %collective-permute-start.7 = (bf16[8,5248]{1,0:T(8,128)(2,1)S(1)}, bf16[8,5248]{1,0:T(8,128)(2,1)S(1)}, u32[]{:S(2)}, u32[]{:S(2)}) collective-permute-start(bf16[8,5248]{1,0:T(8,128)(2,1)S(1)} %add_convert_fusion.4), channel_id=1, source_target_pairs={{0,8},{1,9},{2,10},{3,11},{4,12},{5,13},{6,14},{7,15},{8,0},{9,1},... | collective-permute-start | bytes 251912 | tf_op jit(solution)/shard_map/ppermute | solution.py:238
  41.5 5.2 %collective-permute-start.3 = (bf16[8,4096]{1,0:T(8,128)(2,1)S(1)}, bf16[8,4096]{1,0:T(8,128)(2,1)S(1)}, u32[]{:S(2)}, u32[]{:S(2)}) collective-permute-start(bf16[8,4096]{1,0:T(8,128)(2,1)S(1)} %add_convert_fusion.7), channel_id=1, source_target_pairs={{0,8},{1,9},{2,10},{3,11},{4,12},{5,13},{6,14},{7,15},{8,0},{9,1},... | collective-permute-start | bytes 196616 | tf_op jit(solution)/shard_map/ppermute | solution.py:238
  48.5 5.6 %collective-permute-start.12 = (bf16[8,4096]{1,0:T(8,128)(2,1)S(1)}, bf16[8,4096]{1,0:T(8,128)(2,1)S(1)}, u32[]{:S(2)}, u32[]{:S(2)}) collective-permute-start(bf16[8,4096]{1,0:T(8,128)(2,1)S(1)} %bitcast.36), channel_id=1, source_target_pairs={{0,8},{1,9},{2,10},{3,11},{4,12},{5,13},{6,14},{7,15},{8,0},{9,1},... | collective-permute-start | bytes 196616 | tf_op jit(solution)/shard_map/ppermute | solution.py:238
  52.5 5.3 %collective-permute-start.8 = (bf16[8,4096]{1,0:T(8,128)(2,1)S(1)}, bf16[8,4096]{1,0:T(8,128)(2,1)S(1)}, u32[]{:S(2)}, u32[]{:S(2)}) collective-permute-start(bf16[8,4096]{1,0:T(8,128)(2,1)S(1)} %bitcast.39), channel_id=1, source_target_pairs={{0,8},{1,9},{2,10},{3,11},{4,12},{5,13},{6,14},{7,15},{8,0},{9,1},... | collective-permute-start | bytes 196616 | tf_op jit(solution)/shard_map/ppermute | solution.py:238
  54.1 6.3 %collective-permute-start.13 = (bf16[16,4096]{1,0:T(8,128)(2,1)S(1)}, bf16[16,4096]{1,0:T(8,128)(2,1)S(1)}, u32[]{:S(2)}, u32[]{:S(2)}) collective-permute-start(bf16[16,4096]{1,0:T(8,128)(2,1)S(1)} %pad_maximum_fusion.3), channel_id=1, source_target_pairs={{0,4},{1,5},{2,6},{3,7},{4,0},{5,1},{6,2},{7,3},{8,12},{9,13},{10,... | collective-permute-start | bytes 393224 | tf_op jit(solution)/shard_map/ppermute | solution.py:238
  57.9 5.2 %collective-permute-start.9 = (bf16[16,4096]{1,0:T(8,128)(2,1)S(1)}, bf16[16,4096]{1,0:T(8,128)(2,1)S(1)}, u32[]{:S(2)}, u32[]{:S(2)}) collective-permute-start(bf16[16,4096]{1,0:T(8,128)(2,1)S(1)} %pad_maximum_fusion.2), channel_id=1, source_target_pairs={{0,4},{1,5},{2,6},{3,7},{4,0},{5,1},{6,2},{7,3},{8,12},{9,13},{10,... | collective-permute-start | bytes 393224 | tf_op jit(solution)/shard_map/ppermute | solution.py:238
  60.4 8.1 %collective-permute-start.14 = (bf16[32,4096]{1,0:T(8,128)(2,1)S(1)}, bf16[32,4096]{1,0:T(8,128)(2,1)S(1)}, u32[]{:S(2)}, u32[]{:S(2)}) collective-permute-start(bf16[32,4096]{1,0:T(8,128)(2,1)S(1)} %pad_maximum_fusion.1), channel_id=1, source_target_pairs={{0,2},{1,3},{2,0},{3,1},{4,6},{5,7},{6,4},{7,5},{8,10},{9,11},{10,... | collective-permute-start | bytes 786440 | tf_op jit(solution)/shard_map/ppermute | solution.py:238
  63.1 8.3 %collective-permute-start.10 = (bf16[32,4096]{1,0:T(8,128)(2,1)S(1)}, bf16[32,4096]{1,0:T(8,128)(2,1)S(1)}, u32[]{:S(2)}, u32[]{:S(2)}) collective-permute-start(bf16[32,4096]{1,0:T(8,128)(2,1)S(1)} %pad_maximum_fusion), channel_id=1, source_target_pairs={{0,2},{1,3},{2,0},{3,1},{4,6},{5,7},{6,4},{7,5},{8,10},{9,11},{10,... | collective-permute-start | bytes 786440 | tf_op jit(solution)/shard_map/ppermute | solution.py:238
  68.6 2.9 %collective-permute-start.15 = (bf16[64,4096]{1,0:T(8,128)(2,1)S(1)}, bf16[64,4096]{1,0:T(8,128)(2,1)S(1)}, u32[]{:S(2)}, u32[]{:S(2)}) collective-permute-start(bf16[64,4096]{1,0:T(8,128)(2,1)S(1)} %constant_dynamic-update-slice_fusion.4.refs_0_), channel_id=1, source_target_pairs={{0,1},{1,0},{2,3},{3,2},{4,5},{5,4},{6,7},{7,6},{8,9},{9,8},{10,11... | collective-permute-start | bytes 1572872 | tf_op jit(solution)/shard_map/ppermute | solution.py:238
  71.4 8.5 %collective-permute-start.11 = (bf16[64,4096]{1,0:T(8,128)(2,1)S(1)}, bf16[64,4096]{1,0:T(8,128)(2,1)S(1)}, u32[]{:S(2)}, u32[]{:S(2)}) collective-permute-start(bf16[64,4096]{1,0:T(8,128)(2,1)S(1)} %constant_dynamic-update-slice_fusion.refs_0_), channel_id=1, source_target_pairs={{0,1},{1,0},{2,3},{3,2},{4,5},{5,4},{6,7},{7,6},{8,9},{9,8},{10,11... | collective-permute-start | bytes 1572872 | tf_op jit(solution)/shard_map/ppermute | solution.py:238
  71.5 5.8 %copy-start.1 = (bf16[8192,1024]{1,0:T(8,128)(2,1)S(1)}, bf16[8192,1024]{1,0:T(8,128)(2,1)}, u32[]{:S(2)}) copy-start(bf16[8192,1024]{1,0:T(8,128)(2,1)} %refs_2_.3) | copy-start | bytes 50331652
  79.9 5.8 %copy-start.2 = (bf16[8192,1024]{1,0:T(8,128)(2,1)S(1)}, bf16[8192,1024]{1,0:T(8,128)(2,1)}, u32[]{:S(2)}) copy-start(bf16[8192,1024]{1,0:T(8,128)(2,1)} %refs_2_.3) | copy-start | bytes 50331652

commit v2 on v1

--- a/solution.py
+++ b/solution.py
@@ -21,17 +21,37 @@
 CHUNKS = ((2, 4), (0, 2))
 
 
-def bit_reverse(position, count):
-    result = 0
-    while count > 1:
-        result = result * 2 + position % 2
-        position //= 2
-        count //= 2
+def stage_bits(count, order):
+    bits = []
+    bit = 1
+    while bit < count:
+        bits.append(bit)
+        bit *= 2
+    if order % 2 and len(bits) > 2:
+        bits = bits[:1] + bits[2:] + bits[1:2]
+    return bits
+
+
+def relative(position, count, bits):
+    result, size = 0, count
+    for bit in bits:
+        size //= 2
+        if position & size:
+            result |= bit
     return result
 
 
+def position_of(index, count, bits):
+    result, size = 0, count
+    for bit in bits:
+        size //= 2
+        shift = bit.bit_length() - 1
+        result = result | ((index >> shift) & 1) * size
+    return result
+
+
 def projection_kernel(
-    count, rows, tiles, with_squares,
+    count, rows, bits, tiles, with_squares,
     me_ref, acts_ref, gain_ref, w_ref, send_ref, keep_ref, wide, scaled,
 ):
     step = pl.program_id(0)
@@ -45,7 +65,7 @@
         for pair in range(count // 2):
             parts = []
             for position in (2 * pair, 2 * pair + 1):
-                source = jnp.bitwise_xor(me, bit_reverse(position, count))
+                source = jnp.bitwise_xor(me, relative(position, count, bits))
                 start = pl.multiple_of(source * rows, rows)
                 parts.append(wide[pl.ds(start, rows), :])
             both = jnp.concatenate(parts, axis=0)
@@ -70,13 +90,13 @@
     send_ref[:, columns] = product[half:].astype(jnp.bfloat16)
 
 
-def project(me, activations, gain, w_qkv, count, rows, start, width, with_squares):
+def project(me, activations, gain, w_qkv, count, rows, bits, start, width, with_squares):
     tiles = width // TILE
     depth = w_qkv.shape[0]
     half = count * rows // 2
     whole = width + (LANES if with_squares else 0)
     return pl.pallas_call(
-        functools.partial(projection_kernel, count, rows, tiles, with_squares),
+        functools.partial(projection_kernel, count, rows, bits, tiles, with_squares),
         grid_spec=pltpu.PrefetchScalarGridSpec(
             num_scalar_prefetch=1,
             grid=(tiles,),
@@ -98,7 +118,7 @@
             jax.ShapeDtypeStruct((half, whole), jnp.bfloat16),
             jax.ShapeDtypeStruct((half, whole), jnp.float32),
         ],
-        compiler_params=pltpu.CompilerParams(vmem_limit_bytes=32 * MIB),
+        compiler_params=pltpu.CompilerParams(vmem_limit_bytes=20 * MIB),
         cost_estimate=pl.CostEstimate(
             flops=4 * half * depth * width,
             bytes_accessed=2 * depth * width + 6 * half * whole,
@@ -107,14 +127,9 @@
     )(me, activations, gain, w_qkv)
 
 
-def output_kernel(
-    count, rows, tiles, first, last, me_ref, *refs
-):
+def output_kernel(count, rows, bits, tiles, first, last, me_ref, *refs):
     mine_ref, other_ref, w_ref = refs[:3]
-    refs = refs[3:]
-    if not first:
-        before_ref, refs = refs[0], refs[1:]
-    out_ref, total = refs[0], refs[1]
+    out_ref, total = refs[-2:]
     step = pl.program_id(0)
     columns = pl.ds(pl.multiple_of(step * TILE, TILE), TILE)
     left = jnp.concatenate([mine_ref[:, columns], other_ref[:, columns]], axis=0)
@@ -122,7 +137,7 @@
 
     @pl.when(step == 0)
     def _():
-        total[...] = product if first else before_ref[...] + product
+        total[...] = product
 
     @pl.when(step > 0)
     def _():
@@ -130,22 +145,20 @@
 
     @pl.when(step == tiles - 1)
     def _():
-        if not last:
-            out_ref[...] = total[...]
-            return
-        reversed_me = me_ref[1]
+        mine = position_of(me_ref[0], count, bits)
         for pair in range(count // 2):
             parts = []
             for block in (2 * pair, 2 * pair + 1):
-                reversed_block = bit_reverse(block, count)
-                position = jnp.bitwise_xor(reversed_me, reversed_block)
+                position = jnp.bitwise_xor(mine, position_of(block, count, bits))
                 parts.append(total[pl.ds(pl.multiple_of(position * rows, rows), rows), :])
-            out_ref[pl.ds(2 * pair * rows, 2 * rows), :] = jnp.concatenate(
-                parts, axis=0
-            ).astype(jnp.bfloat16)
-
-
-def output_part(me, mine, other, w_out, before, count, rows, start, last):
+            both = jnp.concatenate(parts, axis=0)
+            where = pl.ds(2 * pair * rows, 2 * rows)
+            if not first:
+                both += refs[3][where, :]
+            out_ref[where, :] = both.astype(out_ref.dtype)
+
+
+def output_part(me, mine, other, w_out, before, count, rows, bits, start, last):
     width = mine.shape[1]
     tiles = width // TILE
     columns = w_out.shape[1]
@@ -162,7 +175,7 @@
         operands.append(before)
     shape = (count * rows, columns)
     return pl.pallas_call(
-        functools.partial(output_kernel, count, rows, tiles, first, last),
+        functools.partial(output_kernel, count, rows, bits, tiles, first, last),
         grid_spec=pltpu.PrefetchScalarGridSpec(
             num_scalar_prefetch=1,
             grid=(tiles,),
@@ -171,7 +184,7 @@
             scratch_shapes=[pltpu.VMEM(shape, jnp.float32)],
         ),
         out_shape=jax.ShapeDtypeStruct(shape, jnp.bfloat16 if last else jnp.float32),
-        compiler_params=pltpu.CompilerParams(vmem_limit_bytes=32 * MIB),
+        compiler_params=pltpu.CompilerParams(vmem_limit_bytes=20 * MIB),
         cost_estimate=pl.CostEstimate(
             flops=2 * shape[0] * width * columns,
             bytes_accessed=2 * width * columns + 2 * shape[0] * (width + columns),
@@ -238,11 +251,11 @@
     return lax.ppermute(value, "gx", [(i, i ^ bit) for i in range(count)])
 
 
-def reduce_rows(send, keep, count, rows):
-    size, bit = count // 2, 1
-    received = [swap(send, count, bit)]
-    while size > 1:
-        size, bit = size // 2, bit * 2
+def reduce_rows(send, keep, count, rows, bits):
+    size = count // 2
+    received = [swap(send, count, bits[0])]
+    for bit in bits[1:]:
+        size //= 2
         part = slice(size * rows, 2 * size * rows)
         total = keep[part]
         for piece in received:
@@ -254,36 +267,32 @@
     return total
 
 
-def gather_rows(own, count):
-    bit = count // 2
+def gather_rows(own, count, bits):
     mine = own
-    while bit > 1:
+    for bit in bits[:0:-1]:
         mine = jnp.concatenate([mine, swap(mine, count, bit)], axis=0)
-        bit //= 2
-    return mine, swap(mine, count, 1)
+    return mine, swap(mine, count, bits[0])
 
 
 def body(count, activations, norm_gain, w_qkv, w_out, cache_keys, value_cache_rows):
     rows = cache_keys.shape[0]
-    index = lax.axis_index("gx").astype(jnp.int32)
-    reversed_index = jnp.int32(0)
-    bit = 1
-    while bit < count:
-        reversed_index = reversed_index * 2 + (index // bit) % 2
-        bit *= 2
-    me = jnp.stack([index, reversed_index])
+    me = lax.axis_index("gx").astype(jnp.int32)[None]
+    w_qkv = pltpu.with_memory_space_constraint(w_qkv, pltpu.HBM)
     gain = norm_gain[None, :]
     per_head = GROUP * HEAD_SIZE
 
     sums = []
     for order, (low, high) in enumerate(CHUNKS):
         first = order == 0
+        bits = stage_bits(count, order)
         start = low * per_head
         width = (QKVW if first else high * per_head) - start
         send, keep = project(
-            me, activations, gain, w_qkv, count, rows, start, width, first
+            me, activations, gain, w_qkv, count, rows, bits, start, width, first
         )
-        sums.append(reduce_rows(send, keep, count, rows))
+        if order == len(CHUNKS) - 1:
+            w_out, send = lax.optimization_barrier((w_out, send))
+        sums.append(reduce_rows(send, keep, count, rows, bits))
 
     lead = sums[0]
     width = (CHUNKS[0][1] - CHUNKS[0][0]) * per_head
@@ -308,9 +317,10 @@
             cache_keys[:, :, low:high],
             value_cache_rows[:, :, low:high],
         )
-        mine, other = gather_rows(attended, count)
+        bits = stage_bits(count, order)
+        mine, other = gather_rows(attended, count, bits)
         total = output_part(
-            me, mine, other, w_out, total, count, rows, low * per_head,
+            me, mine, other, w_out, total, count, rows, bits, low * per_head,
             order == len(CHUNKS) - 1,
         )
     return total

time: 89.3 us -> 72.5 us (0.81)
  local copies, waits for them, and re-layouts: 22.8 us -> 4.94 us
  Pallas kernels: 12.7 us -> 17.6 us
  waiting for transfers between devices: 26 us -> 21.9 us
    unnamed x20 -> x22, local copies, waits for them, and re-layouts: 19 us -> 1.14 us
    pallas_call x4, Pallas kernels: 12.7 us -> 17.6 us  [the longest x2 12.7 us: project(): pl.pallas_call(functools.partial(projection_kernel, count, rows, bits, ti...]
    ppermute x16, waiting for transfers between devices: 26 us -> 21.9 us  [swap(): return lax.ppermute(value, 'gx', [(i, i ^ bit) for i in range(count)])]
  transfers between devices with their start and end apart: 16 -> 16, of which waited for: 11 -> 10; matrix products, arithmetic and copies ran while one was open for 6% -> 7% of each run, Pallas kernels for 6% -> 12%
where the time goes in v2:
time: 72.5 us; the launch traced here: 72.3 us
  starting transfers between devices  23.7 us (33%)
  waiting for transfers between devices  21.9 us (30%)
  Pallas kernels  17.6 us (24%)
  local copies, waits for them, and re-layouts  4.94 us (7%)
  matrix products  2.09 us (3%)
  other arithmetic  1.56 us (2%)
    ppermute x16, starting transfers between devices, swap(): return lax.ppermute(value, 'gx', [(i, i ^ bit) for i in range(count)])  23.7 us
    ppermute x16, waiting for transfers between devices, swap(): return lax.ppermute(value, 'gx', [(i, i ^ bit) for i in range(count)])  21.9 us
    pallas_call x2, Pallas kernels, project(): pl.pallas_call(functools.partial(projection_kernel, count, rows, bits, ti...  12.7 us
    pallas_call x2, Pallas kernels, output_part(): pl.pallas_call(functools.partial(output_kernel, count, rows, bits, tiles,...  4.91 us
    slice x1, local copies, waits for them, and re-layouts, body(): cache_keys[:, :, low:high]  1.51 us
    slice x1, local copies, waits for them, and re-layouts, body(): value_cache_rows[:, :, low:high]  1.51 us
  transfers between devices with their start and end apart: 16, of which 10 were waited for; matrix products, arithmetic and copies ran while one was open for 7% of the time, Pallas kernels for 12%

profile of v2, /device:TPU:0, one launch (start us, length us, event | category | flops | bytes accessed | tf_op | source)
XLA Modules:
  0.0 72.3 jit_solution(930909906291994134)
XLA Ops:
  0.0 0.7 broadcast_in_dim.5.gain_ref
  0.7 0.9 %copy-done = bf16[128,1024]{1,0:T(8,128)(2,1)S(1)} copy-done((bf16[128,1024]{1,0:T(8,128)(2,1)S(1)}, bf16[128,1024]{1,0:T(8,128)(2,1)}, u32[]{:S(2)}) %copy-start) | copy-done | bytes 262168
  1.6 6.4 %shard_map.65 = (bf16[64,5248]{1,0:T(8,128)(2,1)S(1)}, f32[64,5248]{1,0:T(8,128)S(1)}) custom-call(s32[1]{0:T(128)} %bitcast.me_ref, bf16[128,1024]{1,0:T(8,128)(2,1)S(1)} %copy-done, bf16[1,1024]{1,0:T(2,128)(2,1)S(1)} %broadcast_in_dim.5.gain_ref, bf16[1024,9216]{1,0:T(8,128)(2,1)} %w_ref.3), custom_call_target="tpu_custom_call" | custom-call | flops 1342177280 | bytes 12500992 | tf_op jit(solution)/shard_map/pallas_call | solution.py:98
  8.1 0.0 copy-start.1
  8.1 0.5 collective-permute-start.4
  8.6 6.3 %shard_map.64 = (bf16[64,4096]{1,0:T(8,128)(2,1)S(1)}, f32[64,4096]{1,0:T(8,128)S(1)}) custom-call(s32[1]{0:T(128)} %bitcast.me_ref, bf16[128,1024]{1,0:T(8,128)(2,1)S(1)} %copy-done, bf16[1,1024]{1,0:T(2,128)(2,1)S(1)} %broadcast_in_dim.5.gain_ref, bf16[1024,9216]{1,0:T(8,128)(2,1)} %w_ref.3), custom_call_target="tpu_custom_call" | custom-call | flops 1073741824 | bytes 9961472 | tf_op jit(solution)/shard_map/pallas_call | solution.py:98
  14.9 0.0 copy-start.2
  14.9 0.1 collective-permute-start
  15.0 1.5 %fusion.31 = (bf16[8,256,2,128]{3,2,1,0:T(2,128)(2,1)S(1)}, bf16[8,256,2,128]{3,2,1,0:T(2,128)(2,1)S(1)}) fusion(bf16[8,256,4,128]{3,2,1,0:T(4,128)(2,1)S(1)} %copy-done.1), kind=kLoop, calls=%fused_computation.87 | loop fusion | bytes 4194304 | tf_op jit(solution)/shard_map/slice | solution.py:317
  16.6 0.0 slice-start.2
  16.6 1.5 %fusion.32 = (bf16[8,256,2,128]{3,2,1,0:T(2,128)(2,1)S(1)}, bf16[8,256,2,128]{3,2,1,0:T(2,128)(2,1)S(1)}) fusion(bf16[8,256,4,128]{3,2,1,0:T(4,128)(2,1)S(1)} %copy-done.2), kind=kLoop, calls=%fused_computation.88 | loop fusion | bytes 4194304 | tf_op jit(solution)/shard_map/slice | solution.py:318
  18.1 0.0 collective-permute-done.4
  18.1 0.1 add_convert_fusion
  18.2 3.0 %collective-permute-start.5 = (bf16[32,5248]{1,0:T(8,128)(2,1)S(1)}, bf16[32,5248]{1,0:T(8,128)(2,1)S(1)}, u32[]{:S(2)}, u32[]{:S(2)}) collective-permute-start(bf16[32,5248]{1,0:T(8,128)(2,1)S(1)} %add_convert_fusion), channel_id=1, source_target_pairs={{0,2},{1,3},{2,0},{3,1},{4,6},{5,7},{6,4},{7,5},{8,10},{9,11},{10,... | collective-permute-start | bytes 1007624 | tf_op jit(solution)/shard_map/ppermute | solution.py:251
  21.2 0.0 collective-permute-done
  21.3 1.6 %collective-permute-start.1 = (bf16[32,4096]{1,0:T(8,128)(2,1)S(1)}, bf16[32,4096]{1,0:T(8,128)(2,1)S(1)}, u32[]{:S(2)}, u32[]{:S(2)}) collective-permute-start(bf16[32,4096]{1,0:T(8,128)(2,1)S(1)} %add_convert_fusion.1), channel_id=1, source_target_pairs={{0,4},{1,5},{2,6},{3,7},{4,0},{5,1},{6,2},{7,3},{8,12},{9,13},{10,... | collective-permute-start | bytes 786440 | tf_op jit(solution)/shard_map/ppermute | solution.py:251
  22.9 6.4 %collective-permute-done.5 = bf16[32,5248]{1,0:T(8,128)(2,1)S(1)} collective-permute-done((bf16[32,5248]{1,0:T(8,128)(2,1)S(1)}, bf16[32,5248]{1,0:T(8,128)(2,1)S(1)}, u32[]{:S(2)}, u32[]{:S(2)}) %collective-permute-start.5) | collective-permute-done | bytes 335904 | tf_op jit(solution)/shard_map/ppermute | solution.py:251
  29.3 0.1 add_convert_fusion.2
  29.4 1.9 %collective-permute-start.6 = (bf16[16,5248]{1,0:T(8,128)(2,1)S(1)}, bf16[16,5248]{1,0:T(8,128)(2,1)S(1)}, u32[]{:S(2)}, u32[]{:S(2)}) collective-permute-start(bf16[16,5248]{1,0:T(8,128)(2,1)S(1)} %add_convert_fusion.2), channel_id=1, source_target_pairs={{0,4},{1,5},{2,6},{3,7},{4,0},{5,1},{6,2},{7,3},{8,12},{9,13},{10,... | collective-permute-start | bytes 503816 | tf_op jit(solution)/shard_map/ppermute | solution.py:251
  31.2 0.0 collective-permute-done.1
  31.3 2.7 %collective-permute-start.2 = (bf16[16,4096]{1,0:T(8,128)(2,1)S(1)}, bf16[16,4096]{1,0:T(8,128)(2,1)S(1)}, u32[]{:S(2)}, u32[]{:S(2)}) collective-permute-start(bf16[16,4096]{1,0:T(8,128)(2,1)S(1)} %add_convert_fusion.3), channel_id=1, source_target_pairs={{0,8},{1,9},{2,10},{3,11},{4,12},{5,13},{6,14},{7,15},{8,0},{9,1},... | collective-permute-start | bytes 393224 | tf_op jit(solution)/shard_map/ppermute | solution.py:251
  33.9 3.3 %collective-permute-done.6 = bf16[16,5248]{1,0:T(8,128)(2,1)S(1)} collective-permute-done((bf16[16,5248]{1,0:T(8,128)(2,1)S(1)}, bf16[16,5248]{1,0:T(8,128)(2,1)S(1)}, u32[]{:S(2)}, u32[]{:S(2)}) %collective-permute-start.6) | collective-permute-done | bytes 167968 | tf_op jit(solution)/shard_map/ppermute | solution.py:251
  37.3 1.8 %collective-permute-start.7 = (bf16[8,5248]{1,0:T(8,128)(2,1)S(1)}, bf16[8,5248]{1,0:T(8,128)(2,1)S(1)}, u32[]{:S(2)}, u32[]{:S(2)}) collective-permute-start(bf16[8,5248]{1,0:T(8,128)(2,1)S(1)} %add_convert_fusion.4), channel_id=1, source_target_pairs={{0,8},{1,9},{2,10},{3,11},{4,12},{5,13},{6,14},{7,15},{8,0},{9,1},... | collective-permute-start | bytes 251912 | tf_op jit(solution)/shard_map/ppermute | solution.py:251
  39.2 0.9 %collective-permute-done.2 = bf16[16,4096]{1,0:T(8,128)(2,1)S(1)} collective-permute-done((bf16[16,4096]{1,0:T(8,128)(2,1)S(1)}, bf16[16,4096]{1,0:T(8,128)(2,1)S(1)}, u32[]{:S(2)}, u32[]{:S(2)}) %collective-permute-start.2) | collective-permute-done | bytes 131104 | tf_op jit(solution)/shard_map/ppermute | solution.py:251
  40.1 1.6 %collective-permute-start.3 = (bf16[8,4096]{1,0:T(8,128)(2,1)S(1)}, bf16[8,4096]{1,0:T(8,128)(2,1)S(1)}, u32[]{:S(2)}, u32[]{:S(2)}) collective-permute-start(bf16[8,4096]{1,0:T(8,128)(2,1)S(1)} %add_convert_fusion.7), channel_id=1, source_target_pairs={{0,2},{1,3},{2,0},{3,1},{4,6},{5,7},{6,4},{7,5},{8,10},{9,11},{10,... | collective-permute-start | bytes 196616 | tf_op jit(solution)/shard_map/ppermute | solution.py:251
  41.7 1.9 %collective-permute-done.7 = bf16[8,5248]{1,0:T(8,128)(2,1)S(1)} collective-permute-done((bf16[8,5248]{1,0:T(8,128)(2,1)S(1)}, bf16[8,5248]{1,0:T(8,128)(2,1)S(1)}, u32[]{:S(2)}, u32[]{:S(2)}) %collective-permute-start.7) | collective-permute-done | bytes 84000 | tf_op jit(solution)/shard_map/ppermute | solution.py:251
  43.7 0.1 convert_add_fusion
  43.7 0.1 slice_reduce_fusion
  43.8 0.1 slice_multiply_fusion.1
  43.9 0.1 add_convert_fusion.8
  44.0 0.5 collective-permute-done.3
  44.5 0.1 fusion.8
  44.6 0.1 subtract_convert_fusion
  44.8 0.1 fusion.20
  44.8 0.2 fusion.13
  45.1 0.0 slice-start.3
  45.1 0.5 fusion.34
  45.6 0.2 fusion.7
  45.9 0.3 fusion.1
  46.3 0.5 collective-permute-start.12
  46.8 0.2 fusion.14
  47.0 0.5 fusion.33
  47.6 0.2 fusion.6
  47.8 0.3 fusion
  48.2 1.6 %collective-permute-start.8 = (bf16[8,4096]{1,0:T(8,128)(2,1)S(1)}, bf16[8,4096]{1,0:T(8,128)(2,1)S(1)}, u32[]{:S(2)}, u32[]{:S(2)}) collective-permute-start(bf16[8,4096]{1,0:T(8,128)(2,1)S(1)} %bitcast.40), channel_id=1, source_target_pairs={{0,2},{1,3},{2,0},{3,1},{4,6},{5,7},{6,4},{7,5},{8,10},{9,11},{10,... | collective-permute-start | bytes 196616 | tf_op jit(solution)/shard_map/ppermute | solution.py:251
  49.8 1.8 %collective-permute-done.12 = bf16[8,4096]{1,0:T(8,128)(2,1)S(1)} collective-permute-done((bf16[8,4096]{1,0:T(8,128)(2,1)S(1)}, bf16[8,4096]{1,0:T(8,128)(2,1)S(1)}, u32[]{:S(2)}, u32[]{:S(2)}) %collective-permute-start.12) | collective-permute-done | bytes 65568 | tf_op jit(solution)/shard_map/ppermute | solution.py:251
  51.6 1.9 %collective-permute-start.13 = (bf16[16,4096]{1,0:T(8,128)(2,1)S(1)}, bf16[16,4096]{1,0:T(8,128)(2,1)S(1)}, u32[]{:S(2)}, u32[]{:S(2)}) collective-permute-start(bf16[16,4096]{1,0:T(8,128)(2,1)S(1)} %pad_maximum_fusion.3), channel_id=1, source_target_pairs={{0,4},{1,5},{2,6},{3,7},{4,0},{5,1},{6,2},{7,3},{8,12},{9,13},{10,... | collective-permute-start | bytes 393224 | tf_op jit(solution)/shard_map/ppermute | solution.py:251
  53.5 0.0 collective-permute-done.8
  53.5 1.6 %collective-permute-start.9 = (bf16[16,4096]{1,0:T(8,128)(2,1)S(1)}, bf16[16,4096]{1,0:T(8,128)(2,1)S(1)}, u32[]{:S(2)}, u32[]{:S(2)}) collective-permute-start(bf16[16,4096]{1,0:T(8,128)(2,1)S(1)} %pad_maximum_fusion.2), channel_id=1, source_target_pairs={{0,8},{1,9},{2,10},{3,11},{4,12},{5,13},{6,14},{7,15},{8,0},{9,1},... | collective-permute-start | bytes 393224 | tf_op jit(solution)/shard_map/ppermute | solution.py:251
  55.2 1.7 %collective-permute-done.13 = bf16[16,4096]{1,0:T(8,128)(2,1)S(1)} collective-permute-done((bf16[16,4096]{1,0:T(8,128)(2,1)S(1)}, bf16[16,4096]{1,0:T(8,128)(2,1)S(1)}, u32[]{:S(2)}, u32[]{:S(2)}) %collective-permute-start.13) | collective-permute-done | bytes 131104 | tf_op jit(solution)/shard_map/ppermute | solution.py:251
  56.9 1.6 %collective-permute-start.14 = (bf16[32,4096]{1,0:T(8,128)(2,1)S(1)}, bf16[32,4096]{1,0:T(8,128)(2,1)S(1)}, u32[]{:S(2)}, u32[]{:S(2)}) collective-permute-start(bf16[32,4096]{1,0:T(8,128)(2,1)S(1)} %pad_maximum_fusion.1), channel_id=1, source_target_pairs={{0,2},{1,3},{2,0},{3,1},{4,6},{5,7},{6,4},{7,5},{8,10},{9,11},{10,... | collective-permute-start | bytes 786440 | tf_op jit(solution)/shard_map/ppermute | solution.py:251
  58.5 1.1 %collective-permute-done.9 = bf16[16,4096]{1,0:T(8,128)(2,1)S(1)} collective-permute-done((bf16[16,4096]{1,0:T(8,128)(2,1)S(1)}, bf16[16,4096]{1,0:T(8,128)(2,1)S(1)}, u32[]{:S(2)}, u32[]{:S(2)}) %collective-permute-start.9) | collective-permute-done | bytes 131104 | tf_op jit(solution)/shard_map/ppermute | solution.py:251
  59.6 3.2 %collective-permute-start.10 = (bf16[32,4096]{1,0:T(8,128)(2,1)S(1)}, bf16[32,4096]{1,0:T(8,128)(2,1)S(1)}, u32[]{:S(2)}, u32[]{:S(2)}) collective-permute-start(bf16[32,4096]{1,0:T(8,128)(2,1)S(1)} %pad_maximum_fusion), channel_id=1, source_target_pairs={{0,4},{1,5},{2,6},{3,7},{4,0},{5,1},{6,2},{7,3},{8,12},{9,13},{10,... | collective-permute-start | bytes 786440 | tf_op jit(solution)/shard_map/ppermute | solution.py:251
  62.9 0.4 collective-permute-done.14
  63.3 0.1 collective-permute-start.15
  63.4 3.8 %collective-permute-done.10 = bf16[32,4096]{1,0:T(8,128)(2,1)S(1)} collective-permute-done((bf16[32,4096]{1,0:T(8,128)(2,1)S(1)}, bf16[32,4096]{1,0:T(8,128)(2,1)S(1)}, u32[]{:S(2)}, u32[]{:S(2)}) %collective-permute-start.10) | collective-permute-done | bytes 262176 | tf_op jit(solution)/shard_map/ppermute | solution.py:251
  67.2 0.1 collective-permute-start.11
  67.3 0.0 collective-permute-done.15.refs_1_
  67.3 0.0 slice-done
  67.3 0.0 slice-done.1
  67.3 0.0 slice-done.2
  67.3 2.1 %shard_map.66.refs_3_ = f32[128,1024]{1,0:T(8,128)S(1)} custom-call(s32[1]{0:T(128)} %bitcast.me_ref, bf16[64,4096]{1,0:T(8,128)(2,1)S(1)} %constant_dynamic-update-slice_fusion.4.refs_0_, bf16[64,4096]{1,0:T(8,128)(2,1)S(1)} %collective-permute-done.15.refs_1_, bf16[8192,1024]{1,0:T(8,128)(2,1)S(1)} %bitcast.36), custom_call_target="tpu_custom_call" | custom-call | flops 1073741824 | bytes 9699328 | tf_op jit(solution)/shard_map/pallas_call | solution.py:177
  69.4 0.0 collective-permute-done.11.refs_1_
  69.5 2.8 %shard_map.67 = bf16[128,1024]{1,0:T(8,128)(2,1)} custom-call(s32[1]{0:T(128)} %bitcast.me_ref, bf16[64,4096]{1,0:T(8,128)(2,1)S(1)} %constant_dynamic-update-slice_fusion.refs_0_, bf16[64,4096]{1,0:T(8,128)(2,1)S(1)} %collective-permute-done.11.refs_1_, bf16[8192,1024]{1,0:T(8,128)(2,1)S(1)} %bitcast.36, f32[128,1024]{1,0:T(8,128)S(1)} %shard_map.66.refs_3_), custom_call_target="tpu_custom_call" | custom-call | flops 1073741824 | bytes 9699328 | tf_op jit(solution)/shard_map/pallas_call | solution.py:177
  (40 shorter events, 0.6 us)
Async XLA Ops:
  0.7 0.9 %copy-start = (bf16[128,1024]{1,0:T(8,128)(2,1)S(1)}, bf16[128,1024]{1,0:T(8,128)(2,1)}, u32[]{:S(2)}) copy-start(bf16[128,1024]{1,0:T(8,128)(2,1)} %acts_ref.3) | copy-start | bytes 786436
  8.1 6.9 %copy-start.1 = (bf16[8,256,4,128]{3,2,1,0:T(4,128)(2,1)S(1)}, bf16[8,256,4,128]{3,2,1,0:T(4,128)(2,1)}, u32[]{:S(2)}) copy-start(bf16[8,256,4,128]{3,2,1,0:T(4,128)(2,1)} %param.10) | copy-start | bytes 6291460
  8.1 10.0 %collective-permute-start.4 = (bf16[64,5248]{1,0:T(8,128)(2,1)S(1)}, bf16[64,5248]{1,0:T(8,128)(2,1)S(1)}, u32[]{:S(2)}, u32[]{:S(2)}) collective-permute-start(bf16[64,5248]{1,0:T(8,128)(2,1)S(1)} %get-tuple-element.15), channel_id=1, source_target_pairs={{0,1},{1,0},{2,3},{3,2},{4,5},{5,4},{6,7},{7,6},{8,9},{9,8},{10,11... | collective-permute-start | bytes 2015240 | tf_op jit(solution)/shard_map/ppermute | solution.py:251
  8.6 58.7 %slice-start = ((s8[16777216]{0:T(1024)(128)(4,1)}), s8[4194304]{0:T(1024)(128)(4,1)S(1)}, s32[]{:S(2)}) async-start(s8[16777216]{0:T(1024)(128)(4,1)} %bitcast.35), calls=%async_computation | async-start | bytes 8388608
  8.6 58.7 %slice-start.1 = ((s8[16777216]{0:T(1024)(128)(4,1)}), s8[4194304]{0:T(1024)(128)(4,1)S(1)}, s32[]{:S(2)}) async-start(s8[16777216]{0:T(1024)(128)(4,1)} %bitcast.35), calls=%async_computation.1 | async-start | bytes 8388608
  14.9 1.7 %copy-start.2 = (bf16[8,256,4,128]{3,2,1,0:T(4,128)(2,1)S(1)}, bf16[8,256,4,128]{3,2,1,0:T(4,128)(2,1)}, u32[]{:S(2)}) copy-start(bf16[8,256,4,128]{3,2,1,0:T(4,128)(2,1)} %param.11) | copy-start | bytes 6291460
  14.9 6.3 %collective-permute-start = (bf16[64,4096]{1,0:T(8,128)(2,1)S(1)}, bf16[64,4096]{1,0:T(8,128)(2,1)S(1)}, u32[]{:S(2)}, u32[]{:S(2)}) collective-permute-start(bf16[64,4096]{1,0:T(8,128)(2,1)S(1)} %get-tuple-element.13), channel_id=1, source_target_pairs={{0,1},{1,0},{2,3},{3,2},{4,5},{5,4},{6,7},{7,6},{8,9},{9,8},{10,11... | collective-permute-start | bytes 1572872 | tf_op jit(solution)/shard_map/ppermute | solution.py:251
  16.6 50.7 %slice-start.2 = ((s8[16777216]{0:T(1024)(128)(4,1)}), s8[4194304]{0:T(1024)(128)(4,1)S(1)}, s32[]{:S(2)}) async-start(s8[16777216]{0:T(1024)(128)(4,1)} %bitcast.35), calls=%async_computation.2 | async-start | bytes 8388608
  18.2 11.1 %collective-permute-start.5 = (bf16[32,5248]{1,0:T(8,128)(2,1)S(1)}, bf16[32,5248]{1,0:T(8,128)(2,1)S(1)}, u32[]{:S(2)}, u32[]{:S(2)}) collective-permute-start(bf16[32,5248]{1,0:T(8,128)(2,1)S(1)} %add_convert_fusion), channel_id=1, source_target_pairs={{0,2},{1,3},{2,0},{3,1},{4,6},{5,7},{6,4},{7,5},{8,10},{9,11},{10,... | collective-permute-start | bytes 1007624 | tf_op jit(solution)/shard_map/ppermute | solution.py:251
  21.3 10.0 %collective-permute-start.1 = (bf16[32,4096]{1,0:T(8,128)(2,1)S(1)}, bf16[32,4096]{1,0:T(8,128)(2,1)S(1)}, u32[]{:S(2)}, u32[]{:S(2)}) collective-permute-start(bf16[32,4096]{1,0:T(8,128)(2,1)S(1)} %add_convert_fusion.1), channel_id=1, source_target_pairs={{0,4},{1,5},{2,6},{3,7},{4,0},{5,1},{6,2},{7,3},{8,12},{9,13},{10,... | collective-permute-start | bytes 786440 | tf_op jit(solution)/shard_map/ppermute | solution.py:251
  29.4 7.9 %collective-permute-start.6 = (bf16[16,5248]{1,0:T(8,128)(2,1)S(1)}, bf16[16,5248]{1,0:T(8,128)(2,1)S(1)}, u32[]{:S(2)}, u32[]{:S(2)}) collective-permute-start(bf16[16,5248]{1,0:T(8,128)(2,1)S(1)} %add_convert_fusion.2), channel_id=1, source_target_pairs={{0,4},{1,5},{2,6},{3,7},{4,0},{5,1},{6,2},{7,3},{8,12},{9,13},{10,... | collective-permute-start | bytes 503816 | tf_op jit(solution)/shard_map/ppermute | solution.py:251
  31.3 8.8 %collective-permute-start.2 = (bf16[16,4096]{1,0:T(8,128)(2,1)S(1)}, bf16[16,4096]{1,0:T(8,128)(2,1)S(1)}, u32[]{:S(2)}, u32[]{:S(2)}) collective-permute-start(bf16[16,4096]{1,0:T(8,128)(2,1)S(1)} %add_convert_fusion.3), channel_id=1, source_target_pairs={{0,8},{1,9},{2,10},{3,11},{4,12},{5,13},{6,14},{7,15},{8,0},{9,1},... | collective-permute-start | bytes 393224 | tf_op jit(solution)/shard_map/ppermute | solution.py:251
  37.3 6.3 %collective-permute-start.7 = (bf16[8,5248]{1,0:T(8,128)(2,1)S(1)}, bf16[8,5248]{1,0:T(8,128)(2,1)S(1)}, u32[]{:S(2)}, u32[]{:S(2)}) collective-permute-start(bf16[8,5248]{1,0:T(8,128)(2,1)S(1)} %add_convert_fusion.4), channel_id=1, source_target_pairs={{0,8},{1,9},{2,10},{3,11},{4,12},{5,13},{6,14},{7,15},{8,0},{9,1},... | collective-permute-start | bytes 251912 | tf_op jit(solution)/shard_map/ppermute | solution.py:251
  40.1 4.3 %collective-permute-start.3 = (bf16[8,4096]{1,0:T(8,128)(2,1)S(1)}, bf16[8,4096]{1,0:T(8,128)(2,1)S(1)}, u32[]{:S(2)}, u32[]{:S(2)}) collective-permute-start(bf16[8,4096]{1,0:T(8,128)(2,1)S(1)} %add_convert_fusion.7), channel_id=1, source_target_pairs={{0,2},{1,3},{2,0},{3,1},{4,6},{5,7},{6,4},{7,5},{8,10},{9,11},{10,... | collective-permute-start | bytes 196616 | tf_op jit(solution)/shard_map/ppermute | solution.py:251
  45.1 22.3 %slice-start.3 = ((s8[16777216]{0:T(1024)(128)(4,1)}), s8[4194304]{0:T(1024)(128)(4,1)S(1)}, s32[]{:S(2)}) async-start(s8[16777216]{0:T(1024)(128)(4,1)} %bitcast.35), calls=%async_computation.3 | async-start | bytes 8388608
  46.3 5.3 %collective-permute-start.12 = (bf16[8,4096]{1,0:T(8,128)(2,1)S(1)}, bf16[8,4096]{1,0:T(8,128)(2,1)S(1)}, u32[]{:S(2)}, u32[]{:S(2)}) collective-permute-start(bf16[8,4096]{1,0:T(8,128)(2,1)S(1)} %bitcast.37), channel_id=1, source_target_pairs={{0,8},{1,9},{2,10},{3,11},{4,12},{5,13},{6,14},{7,15},{8,0},{9,1},... | collective-permute-start | bytes 196616 | tf_op jit(solution)/shard_map/ppermute | solution.py:251
  48.2 5.3 %collective-permute-start.8 = (bf16[8,4096]{1,0:T(8,128)(2,1)S(1)}, bf16[8,4096]{1,0:T(8,128)(2,1)S(1)}, u32[]{:S(2)}, u32[]{:S(2)}) collective-permute-start(bf16[8,4096]{1,0:T(8,128)(2,1)S(1)} %bitcast.40), channel_id=1, source_target_pairs={{0,2},{1,3},{2,0},{3,1},{4,6},{5,7},{6,4},{7,5},{8,10},{9,11},{10,... | collective-permute-start | bytes 196616 | tf_op jit(solution)/shard_map/ppermute | solution.py:251
  51.6 5.2 %collective-permute-start.13 = (bf16[16,4096]{1,0:T(8,128)(2,1)S(1)}, bf16[16,4096]{1,0:T(8,128)(2,1)S(1)}, u32[]{:S(2)}, u32[]{:S(2)}) collective-permute-start(bf16[16,4096]{1,0:T(8,128)(2,1)S(1)} %pad_maximum_fusion.3), channel_id=1, source_target_pairs={{0,4},{1,5},{2,6},{3,7},{4,0},{5,1},{6,2},{7,3},{8,12},{9,13},{10,... | collective-permute-start | bytes 393224 | tf_op jit(solution)/shard_map/ppermute | solution.py:251
  53.5 6.0 %collective-permute-start.9 = (bf16[16,4096]{1,0:T(8,128)(2,1)S(1)}, bf16[16,4096]{1,0:T(8,128)(2,1)S(1)}, u32[]{:S(2)}, u32[]{:S(2)}) collective-permute-start(bf16[16,4096]{1,0:T(8,128)(2,1)S(1)} %pad_maximum_fusion.2), channel_id=1, source_target_pairs={{0,8},{1,9},{2,10},{3,11},{4,12},{5,13},{6,14},{7,15},{8,0},{9,1},... | collective-permute-start | bytes 393224 | tf_op jit(solution)/shard_map/ppermute | solution.py:251
  56.9 6.4 %collective-permute-start.14 = (bf16[32,4096]{1,0:T(8,128)(2,1)S(1)}, bf16[32,4096]{1,0:T(8,128)(2,1)S(1)}, u32[]{:S(2)}, u32[]{:S(2)}) collective-permute-start(bf16[32,4096]{1,0:T(8,128)(2,1)S(1)} %pad_maximum_fusion.1), channel_id=1, source_target_pairs={{0,2},{1,3},{2,0},{3,1},{4,6},{5,7},{6,4},{7,5},{8,10},{9,11},{10,... | collective-permute-start | bytes 786440 | tf_op jit(solution)/shard_map/ppermute | solution.py:251
  59.6 7.6 %collective-permute-start.10 = (bf16[32,4096]{1,0:T(8,128)(2,1)S(1)}, bf16[32,4096]{1,0:T(8,128)(2,1)S(1)}, u32[]{:S(2)}, u32[]{:S(2)}) collective-permute-start(bf16[32,4096]{1,0:T(8,128)(2,1)S(1)} %pad_maximum_fusion), channel_id=1, source_target_pairs={{0,4},{1,5},{2,6},{3,7},{4,0},{5,1},{6,2},{7,3},{8,12},{9,13},{10,... | collective-permute-start | bytes 786440 | tf_op jit(solution)/shard_map/ppermute | solution.py:251
  63.3 4.0 %collective-permute-start.15 = (bf16[64,4096]{1,0:T(8,128)(2,1)S(1)}, bf16[64,4096]{1,0:T(8,128)(2,1)S(1)}, u32[]{:S(2)}, u32[]{:S(2)}) collective-permute-start(bf16[64,4096]{1,0:T(8,128)(2,1)S(1)} %constant_dynamic-update-slice_fusion.4.refs_0_), channel_id=1, source_target_pairs={{0,1},{1,0},{2,3},{3,2},{4,5},{5,4},{6,7},{7,6},{8,9},{9,8},{10,11... | collective-permute-start | bytes 1572872 | tf_op jit(solution)/shard_map/ppermute | solution.py:251
  67.2 2.2 %collective-permute-start.11 = (bf16[64,4096]{1,0:T(8,128)(2,1)S(1)}, bf16[64,4096]{1,0:T(8,128)(2,1)S(1)}, u32[]{:S(2)}, u32[]{:S(2)}) collective-permute-start(bf16[64,4096]{1,0:T(8,128)(2,1)S(1)} %constant_dynamic-update-slice_fusion.refs_0_), channel_id=1, source_target_pairs={{0,1},{1,0},{2,3},{3,2},{4,5},{5,4},{6,7},{7,6},{8,9},{9,8},{10,11... | collective-permute-start | bytes 1572872 | tf_op jit(solution)/shard_map/ppermute | solution.py:251

commit v3 on v1

v3 whole, which is shorter than its diff:
```python
import functools

import jax
import jax.numpy as jnp
from jax import lax
from jax.experimental import pallas as pl
from jax.experimental.pallas import tpu as pltpu
from jax.sharding import PartitionSpec as P

D = 16384
QUERY_HEADS = 64
KEY_VALUE_HEADS = 4
HEAD_SIZE = 128
CONTEXT_LENGTH = 256
GROUP = QUERY_HEADS // KEY_VALUE_HEADS
QUERY_WIDTH = QUERY_HEADS * HEAD_SIZE
QKVW = QUERY_WIDTH + 2 * KEY_VALUE_HEADS * HEAD_SIZE
TILE = 1024
LANES = 128
MIB = 1024 * 1024
CHUNKS = ((2, 4), (0, 2))


def stage_bits(count):
    bits = []
    bit = 2
    while bit < count:
        bits.append(bit)
        bit *= 2
    return bits, bits[1:] + bits[:1]


def place(index, count, order):
    result, size = 0, count // 2
    for bit in stage_bits(count)[order]:
        size //= 2
        result = result | ((index >> (bit.bit_length() - 1)) & 1) * size
    return result


def places(me, count):
    own = [place(me, count, order) for order in range(2)]
    core = me & 1
    result = []
    for block in range(count):
        order = block & 1
        half = jnp.bitwise_xor(core, order) * (count // 2)
        result.append(half + jnp.bitwise_xor(own[order], place(block, count, order)))
    return result


def fetch(w_ref, weights, sems, start, tiles):
    copies = [
        pltpu.make_async_copy(
            w_ref.at[:, pl.ds(start + tile * TILE, TILE)], weights.at[tile], sems.at[tile]
        )
        for tile in range(tiles)
    ]
    return copies


def multiply(copies, scaled, weights, send_ref, keep_ref):
    half = keep_ref.shape[0]
    for tile, copy in enumerate(copies):
        copy.wait()
        product = jnp.dot(scaled[...], weights[tile], preferred_element_type=jnp.float32)
        columns = slice(tile * TILE, (tile + 1) * TILE)
        keep_ref[:, columns] = product[:half]
        send_ref[:, columns] = product[half:].astype(jnp.bfloat16)


def first_kernel(
    count, rows, start, width,
    me_ref, acts_ref, gain_ref, w_ref, send_ref, keep_ref, scaled,
    narrow, gains, ordered, squares, weights, small_sems, sems,
):
    half = count * rows // 2
    me = me_ref[0]
    small = [
        pltpu.make_async_copy(acts_ref, narrow, small_sems.at[0]),
        pltpu.make_async_copy(gain_ref, gains, small_sems.at[1]),
    ]
    copies = fetch(w_ref, weights, sems, start, width // TILE)
    for copy in small + copies:
        copy.start()
    for copy in small:
        copy.wait()
    gain = gains[...].astype(jnp.float32)[None, :]
    lane = lax.broadcasted_iota(jnp.int32, (rows, LANES), 1)
    targets = places(me, count)
    for pair in range(count // 2):
        both = narrow[2 * pair * rows : 2 * (pair + 1) * rows, :].astype(jnp.float32)
        for side in range(2):
            wide = both[side * rows : (side + 1) * rows]
            target = targets[2 * pair + side]
            where = pl.ds(pl.multiple_of(target * rows, rows), rows)
            ordered[where, :] = wide * gain
            total = jnp.sum(wide * wide, axis=1, keepdims=True)
            high = total.astype(jnp.bfloat16).astype(jnp.float32)
            lanes = jnp.where(lane == 2 * me, high, 0.0)
            squares[where, :] = jnp.where(lane == 2 * me + 1, total - high, lanes)
    scaled[...] = ordered[...].astype(jnp.bfloat16)
    keep_ref[:, width:] = squares[:half]
    send_ref[:, width:] = squares[half:].astype(jnp.bfloat16)
    multiply(copies, scaled, weights, send_ref, keep_ref)


def later_kernel(start, width, scaled, w_ref, send_ref, keep_ref, weights, sems):
    copies = fetch(w_ref, weights, sems, start, width // TILE)
    for copy in copies:
        copy.start()
    multiply(copies, scaled, weights, send_ref, keep_ref)


def project(me, activations, gain, w_qkv, scaled, count, rows, start, width):
    tiles = width // TILE
    depth = w_qkv.shape[0]
    half = count * rows // 2
    first = scaled is None
    whole = width + (LANES if first else 0)
    in_hbm = pl.BlockSpec(memory_space=pltpu.HBM)
    in_vmem = pl.BlockSpec(memory_space=pltpu.VMEM)
    out_shape = [
        jax.ShapeDtypeStruct((half, whole), jnp.bfloat16),
        jax.ShapeDtypeStruct((half, whole), jnp.float32),
    ]
    scratch = [
        pltpu.VMEM((tiles, depth, TILE), jnp.bfloat16),
        pltpu.SemaphoreType.DMA((tiles,)),
    ]
    if first:
        kernel = functools.partial(first_kernel, count, rows, start, width)
        operands = (me, activations, gain, w_qkv)
        in_specs = [pl.BlockSpec(memory_space=pltpu.SMEM)] + [in_hbm] * 3
        out_shape.append(jax.ShapeDtypeStruct(activations.shape, jnp.bfloat16))
        scratch = [
            pltpu.VMEM(activations.shape, jnp.bfloat16),
            pltpu.VMEM(gain.shape, jnp.bfloat16),
            pltpu.VMEM(activations.shape, jnp.float32),
            pltpu.VMEM((2 * half, LANES), jnp.float32),
            scratch[0],
            pltpu.SemaphoreType.DMA((2,)),
            scratch[1],
        ]
    else:
        kernel = functools.partial(later_kernel, start, width)
        operands = (scaled, w_qkv)
        in_specs = [in_vmem, in_hbm]
    return pl.pallas_call(
        kernel,
        in_specs=in_specs,
        out_specs=[in_vmem] * len(out_shape),
        scratch_shapes=scratch,
        out_shape=out_shape,
        compiler_params=pltpu.CompilerParams(vmem_limit_bytes=24 * MIB),
        cost_estimate=pl.CostEstimate(
            flops=4 * half * depth * width,
            bytes_accessed=2 * depth * width + 6 * half * whole,
            transcendentals=0,
        ),
    )(*operands)


def output_kernel(count, rows, tiles, first, me_ref, *refs):
    mine_ref, other_ref, w_ref = refs[:3]
    out_ref, total = refs[-2:]
    step = pl.program_id(0)
    columns = pl.ds(pl.multiple_of(step * TILE, TILE), TILE)
    left = jnp.concatenate([mine_ref[:, columns], other_ref[:, columns]], axis=0)
    product = jnp.dot(left, w_ref[...], preferred_element_type=jnp.float32)

    @pl.when(step == 0)
    def _():
        total[...] = product if first else refs[3][...] + product

    @pl.when(step > 0)
    def _():
        total[...] += product

    @pl.when(step == tiles - 1)
    def _():
        if out_ref.dtype == jnp.float32:
            out_ref[...] = total[...]
            return
        sources = places(me_ref[0], count)
        for pair in range(count // 2):
            parts = []
            for source in sources[2 * pair : 2 * pair + 2]:
                parts.append(total[pl.ds(pl.multiple_of(source * rows, rows), rows), :])
            where = slice(2 * pair * rows, 2 * (pair + 1) * rows)
            out_ref[where, :] = jnp.concatenate(parts, axis=0).astype(out_ref.dtype)


def output_part(me, mine, other, w_out, before, count, rows, start, last):
    width = mine.shape[1]
    tiles = width // TILE
    columns = w_out.shape[1]
    whole = lambda j, me: (0, 0)
    in_specs = [
        pl.BlockSpec(mine.shape, whole),
        pl.BlockSpec(other.shape, whole),
        pl.BlockSpec((TILE, columns), lambda j, me: (start // TILE + j, 0)),
    ]
    operands = [mine, other, w_out]
    first = before is None
    if not first:
        in_specs.append(pl.BlockSpec(before.shape, whole))
        operands.append(before)
    shape = (count * rows, columns)
    return pl.pallas_call(
        functools.partial(output_kernel, count, rows, tiles, first),
        grid_spec=pltpu.PrefetchScalarGridSpec(
            num_scalar_prefetch=1,
            grid=(tiles,),
            in_specs=in_specs,
            out_specs=pl.BlockSpec(shape, whole),
            scratch_shapes=[pltpu.VMEM(shape, jnp.float32)],
        ),
        out_shape=jax.ShapeDtypeStruct(shape, jnp.bfloat16 if last else jnp.float32),
        compiler_params=pltpu.CompilerParams(vmem_limit_bytes=20 * MIB),
        cost_estimate=pl.CostEstimate(
            flops=2 * shape[0] * width * columns,
            bytes_accessed=2 * width * columns + 2 * shape[0] * (width + columns),
            transcendentals=0,
        ),
    )(me, *operands)


def rotation():
    half_dim = HEAD_SIZE // 2
    frequency = jnp.float32(500000.0) ** (
        -jnp.arange(half_dim, dtype=jnp.float32) * 2.0 / HEAD_SIZE
    )
    angles = jnp.float32(CONTEXT_LENGTH) * frequency
    return jnp.cos(angles), jnp.sin(angles)


def apply_rotary(tensor):
    half_dim = HEAD_SIZE // 2
    cosine, sine_part = rotation()
    first_half = tensor[..., :half_dim]
    second_half = tensor[..., half_dim:]
    return jnp.concatenate(
        [
            first_half * cosine - second_half * sine_part,
            second_half * cosine + first_half * sine_part,
        ],
        axis=-1,
    )


def attend(query_rows, fresh_keys, fresh_values, cache_keys, value_cache_rows):
    count_of_rows, heads = fresh_keys.shape[:2]
    grouped_queries = query_rows.reshape(count_of_rows, heads, GROUP, HEAD_SIZE)
    scaling = 1.0 / jnp.sqrt(jnp.float32(HEAD_SIZE))
    cached_scores = (
        jnp.einsum(
            "rkgd,rtkd->rkgt", grouped_queries, cache_keys, preferred_element_type=jnp.float32
        )
        * scaling
    )
    own_scores = (
        jnp.einsum("rkgd,rkd->rkg", grouped_queries, fresh_keys, preferred_element_type=jnp.float32)
        * scaling
    )
    highest = jnp.maximum(jnp.max(cached_scores, axis=-1), own_scores)
    cached_exp = jnp.exp(cached_scores - highest[..., None])
    own_exp = jnp.exp(own_scores - highest)
    denominator = jnp.sum(cached_exp, axis=-1) + own_exp
    cached_weights = (cached_exp / denominator[..., None]).astype(jnp.bfloat16)
    own_weights = (own_exp / denominator).astype(jnp.bfloat16)
    combined = jnp.einsum(
        "rkgt,rtkd->rkgd", cached_weights, value_cache_rows, preferred_element_type=jnp.float32
    )
    combined = (
        combined
        + own_weights.astype(jnp.float32)[..., None]
        * fresh_values.astype(jnp.float32)[:, :, None, :]
    )
    return combined.reshape(count_of_rows, heads * GROUP * HEAD_SIZE).astype(jnp.bfloat16)


def swap(value, count, stage=None):
    orders = stage_bits(count)
    partners = [
        (i, i ^ (1 if stage is None else orders[i & 1][stage])) for i in range(count)
    ]
    return lax.ppermute(value, "gx", partners)


def tie(value, token):
    return lax.optimization_barrier((value, token))[0]


class Reduction:
    def __init__(self, send, keep, count, rows):
        self.keep, self.count, self.rows = keep, count, rows
        self.size = count // 2
        self.received = [swap(send, count)]

    def combine(self, part):
        total = self.keep[part]
        for piece in self.received:
            total = total + piece[part].astype(jnp.float32)
        return total

    def stage(self):
        self.size //= 2
        part = slice(self.size * self.rows, 2 * self.size * self.rows)
        send = self.combine(part).astype(jnp.bfloat16)
        self.received.append(swap(send, self.count, len(self.received) - 1))
        return send

    def own(self):
        return self.combine(slice(0, self.rows))


def gather_rows(own, count):
    mine = own
    for stage in reversed(range(len(stage_bits(count)[0]))):
        mine = jnp.concatenate([mine, swap(mine, count, stage)], axis=0)
    return mine, swap(mine, count)


def body(count, activations, norm_gain, w_qkv, w_out, cache_keys, value_cache_rows):
    rows = cache_keys.shape[0]
    me = lax.axis_index("gx").astype(jnp.int32)[None]
    activations, norm_gain, w_qkv = [
        pltpu.with_memory_space_constraint(value, pltpu.HBM)
        for value in (activations, norm_gain, w_qkv)
    ]
    per_head = GROUP * HEAD_SIZE

    parts = []
    scaled = None
    for order, (low, high) in enumerate(CHUNKS):
        start = low * per_head
        width = (high * per_head if order else QKVW) - start
        send, keep, *rest = project(
            me, activations, norm_gain, w_qkv, scaled, count, rows, start, width
        )
        if order == 0:
            scaled = rest[0]
        parts.append(Reduction(send, keep, count, rows))
    w_out = tie(w_out, send)
    for stage in range(len(stage_bits(count)[0])):
        for part in parts:
            token = part.stage()
        if stage == 0:
            cache_keys = tie(cache_keys, token)
            value_cache_rows = tie(value_cache_rows, token)
    sums = [part.own() for part in parts]

    lead = sums[0]
    width = (CHUNKS[0][1] - CHUNKS[0][0]) * per_head
    own_squares = jnp.sum(lead[:, -LANES:], axis=1)
    inverse_rms = lax.rsqrt(own_squares / D + 1e-05)[:, None]
    fresh = lead[:, width:-LANES] * inverse_rms
    kv_width = KEY_VALUE_HEADS * HEAD_SIZE
    shape = (rows, KEY_VALUE_HEADS, HEAD_SIZE)
    fresh_keys = apply_rotary(fresh[:, :kv_width].reshape(shape)).astype(jnp.bfloat16)
    fresh_values = fresh[:, kv_width:].reshape(shape).astype(jnp.bfloat16)

    total = None
    for order, (low, high) in enumerate(CHUNKS):
        width = (high - low) * per_head
        queries = apply_rotary(
            (sums[order][:, :width] * inverse_rms).reshape(rows, width // HEAD_SIZE, HEAD_SIZE)
        ).astype(jnp.bfloat16)
        attended = attend(
            queries,
            fresh_keys[:, low:high],
            fresh_values[:, low:high],
            cache_keys[:, :, low:high],
            value_cache_rows[:, :, low:high],
        )
        mine, other = gather_rows(attended, count)
        total = output_part(
            me, mine, other, w_out, total, count, rows, low * per_head,
            order == len(CHUNKS) - 1,
        )
    return total


def solution(mesh):
    return jax.shard_map(
        functools.partial(body, mesh.shape["gx"]),
        mesh=mesh,
        in_specs=(
            P("groups", "gx"),
            P("gx"),
            P("gx", None),
            P(None, "gx"),
            P(("groups", "gx"), None, None, None),
            P(("groups", "gx"), None, None, None),
        ),
        out_specs=P("groups", "gx"),
        check_vma=False,
    )
```

time: 89.3 us -> 68.2 us (0.76)
  local copies, waits for them, and re-layouts: 22.8 us -> 1.28 us
  waiting for transfers between devices: 26 us -> 23.5 us
  Pallas kernels: 12.7 us -> 14.8 us
  starting transfers between devices: 23.4 us -> 24.4 us
    unnamed x20, local copies, waits for them, and re-layouts: 19 us -> 0.19 us
    pallas_call x2, Pallas kernels: 6.78 us -> 9.94 us  [project(): pl.pallas_call(kernel, in_specs=in_specs, out_specs=[in_vmem] * len(out_s...]
    slice x2 -> x0, local copies, waits for them, and re-layouts: 2.99 us -> none  [the longest x1 1.51 us: body(): value_cache_rows[:, :, low:high]]
    ppermute x16, waiting for transfers between devices: 26 us -> 23.5 us  [swap(): return lax.ppermute(value, 'gx', partners)]
    pallas_call x2, Pallas kernels: 5.96 us -> 4.89 us  [output_part(): pl.pallas_call(functools.partial(output_kernel, count, rows, tiles, first...]
    ppermute x16, starting transfers between devices: 23.4 us -> 24.4 us  [swap(): return lax.ppermute(value, 'gx', partners)]
    optimization_barrier x0 -> x2, local copies, waits for them, and re-layouts: none -> 0.99 us  [tie(): return lax.optimization_barrier((value, token))[0]]
  transfers between devices with their start and end apart: 16 -> 16, of which waited for: 11 -> 11; matrix products, arithmetic and copies ran while one was open for 6% -> 3% of each run, Pallas kernels for 6% -> 9%
where the time goes in v3:
time: 68.2 us; the launch traced here: 68.1 us
  starting transfers between devices  24.4 us (36%)
  waiting for transfers between devices  23.5 us (34%)
  Pallas kernels  14.8 us (22%)
  matrix products  2.07 us (3%)
  other arithmetic  1.57 us (2%)
  local copies, waits for them, and re-layouts  1.28 us (2%)
    ppermute x16, starting transfers between devices, swap(): return lax.ppermute(value, 'gx', partners)  24.4 us
    ppermute x16, waiting for transfers between devices, swap(): return lax.ppermute(value, 'gx', partners)  23.5 us
    pallas_call x2, Pallas kernels, project(): pl.pallas_call(kernel, in_specs=in_specs, out_specs=[in_vmem] * len(out_s...  9.94 us
    pallas_call x2, Pallas kernels, output_part(): pl.pallas_call(functools.partial(output_kernel, count, rows, tiles, first...  4.89 us
  transfers between devices with their start and end apart: 16, of which 11 were waited for; matrix products, arithmetic and copies ran while one was open for 3% of the time, Pallas kernels for 9%

profile of v3, /device:TPU:0, one launch (start us, length us, event | category | flops | bytes accessed | tf_op | source)
XLA Modules:
  0.0 68.1 jit_solution(11558941999905823217)
XLA Ops:
  0.0 5.8 %shard_map.64 = (bf16[64,5248]{1,0:T(8,128)(2,1)S(1)}, f32[64,5248]{1,0:T(8,128)S(1)}, bf16[128,1024]{1,0:T(8,128)(2,1)S(1)}) custom-call(s32[1]{0:T(128)} %bitcast.me_ref, bf16[128,1024]{1,0:T(8,128)(2,1)} %acts_ref.1, bf16[1024]{0:T(1024)(128)(2,1)} %gain_ref.1, bf16[1024,9216]{1,0:T(8,128)(2,1)} %w_ref.3), custom_call_target="tpu_custom_call" | custom-call | flops 1342177280 | bytes 12500992 | tf_op jit(solution)/shard_map/pallas_call | solution.py:149
  5.8 0.5 collective-permute-start.4
  6.3 4.1 %shard_map.65 = (bf16[64,4096]{1,0:T(8,128)(2,1)S(1)}, f32[64,4096]{1,0:T(8,128)S(1)}) custom-call(bf16[128,1024]{1,0:T(8,128)(2,1)S(1)} %get-tuple-element.13.scaled, bf16[1024,9216]{1,0:T(8,128)(2,1)} %w_ref.3), custom_call_target="tpu_custom_call" | custom-call | flops 1073741824 | bytes 9961472 | tf_op jit(solution)/shard_map/pallas_call | solution.py:149
  10.5 0.0 copy-start
  10.5 0.1 collective-permute-start
  10.7 0.0 collective-permute-done.4
  10.7 0.1 add_convert_fusion
  10.7 3.0 %collective-permute-start.5 = (bf16[32,5248]{1,0:T(8,128)(2,1)S(1)}, bf16[32,5248]{1,0:T(8,128)(2,1)S(1)}, u32[]{:S(2)}, u32[]{:S(2)}) collective-permute-start(bf16[32,5248]{1,0:T(8,128)(2,1)S(1)} %add_convert_fusion), channel_id=1, source_target_pairs={{0,2},{1,5},{2,0},{3,7},{4,6},{5,1},{6,4},{7,3},{8,10},{9,13},{10,... | collective-permute-start | bytes 1007624 | tf_op jit(solution)/shard_map/ppermute | solution.py:288
  13.8 0.0 collective-permute-done
  13.8 0.1 add_convert_fusion.1
  13.8 0.0 slice-start.2
  13.9 1.4 %collective-permute-start.1 = (bf16[32,4096]{1,0:T(8,128)(2,1)S(1)}, bf16[32,4096]{1,0:T(8,128)(2,1)S(1)}, u32[]{:S(2)}, u32[]{:S(2)}) collective-permute-start(bf16[32,4096]{1,0:T(8,128)(2,1)S(1)} %add_convert_fusion.1), channel_id=1, source_target_pairs={{0,2},{1,5},{2,0},{3,7},{4,6},{5,1},{6,4},{7,3},{8,10},{9,13},{10,... | collective-permute-start | bytes 786440 | tf_op jit(solution)/shard_map/ppermute | solution.py:288
  15.3 0.0 copy-done
  15.3 0.5 copy.9
  15.8 0.0 copy-done.1
  15.8 0.5 copy.10
  16.3 2.6 %collective-permute-done.5 = bf16[32,5248]{1,0:T(8,128)(2,1)S(1)} collective-permute-done((bf16[32,5248]{1,0:T(8,128)(2,1)S(1)}, bf16[32,5248]{1,0:T(8,128)(2,1)S(1)}, u32[]{:S(2)}, u32[]{:S(2)}) %collective-permute-start.5) | collective-permute-done | bytes 335904 | tf_op jit(solution)/shard_map/ppermute | solution.py:288
  18.9 0.1 add_convert_fusion.2
  19.0 2.1 %collective-permute-start.6 = (bf16[16,5248]{1,0:T(8,128)(2,1)S(1)}, bf16[16,5248]{1,0:T(8,128)(2,1)S(1)}, u32[]{:S(2)}, u32[]{:S(2)}) collective-permute-start(bf16[16,5248]{1,0:T(8,128)(2,1)S(1)} %add_convert_fusion.2), channel_id=1, source_target_pairs={{0,4},{1,9},{2,6},{3,11},{4,0},{5,13},{6,2},{7,15},{8,12},{9,1},{1... | collective-permute-start | bytes 503816 | tf_op jit(solution)/shard_map/ppermute | solution.py:288
  21.1 0.6 collective-permute-done.1
  21.7 0.1 add_convert_fusion.3
  21.8 2.1 %collective-permute-start.2 = (bf16[16,4096]{1,0:T(8,128)(2,1)S(1)}, bf16[16,4096]{1,0:T(8,128)(2,1)S(1)}, u32[]{:S(2)}, u32[]{:S(2)}) collective-permute-start(bf16[16,4096]{1,0:T(8,128)(2,1)S(1)} %add_convert_fusion.3), channel_id=1, source_target_pairs={{0,4},{1,9},{2,6},{3,11},{4,0},{5,13},{6,2},{7,15},{8,12},{9,1},{1... | collective-permute-start | bytes 393224 | tf_op jit(solution)/shard_map/ppermute | solution.py:288
  23.9 1.8 %collective-permute-done.6 = bf16[16,5248]{1,0:T(8,128)(2,1)S(1)} collective-permute-done((bf16[16,5248]{1,0:T(8,128)(2,1)S(1)}, bf16[16,5248]{1,0:T(8,128)(2,1)S(1)}, u32[]{:S(2)}, u32[]{:S(2)}) %collective-permute-start.6) | collective-permute-done | bytes 167968 | tf_op jit(solution)/shard_map/ppermute | solution.py:288
  25.8 2.8 %collective-permute-start.7 = (bf16[8,5248]{1,0:T(8,128)(2,1)S(1)}, bf16[8,5248]{1,0:T(8,128)(2,1)S(1)}, u32[]{:S(2)}, u32[]{:S(2)}) collective-permute-start(bf16[8,5248]{1,0:T(8,128)(2,1)S(1)} %add_convert_fusion.4), channel_id=1, source_target_pairs={{0,8},{1,3},{2,10},{3,1},{4,12},{5,7},{6,14},{7,5},{8,0},{9,11},{1... | collective-permute-start | bytes 251912 | tf_op jit(solution)/shard_map/ppermute | solution.py:288
  28.6 0.0 collective-permute-done.2
  28.6 2.6 %collective-permute-start.3 = (bf16[8,4096]{1,0:T(8,128)(2,1)S(1)}, bf16[8,4096]{1,0:T(8,128)(2,1)S(1)}, u32[]{:S(2)}, u32[]{:S(2)}) collective-permute-start(bf16[8,4096]{1,0:T(8,128)(2,1)S(1)} %add_convert_fusion.7), channel_id=1, source_target_pairs={{0,8},{1,3},{2,10},{3,1},{4,12},{5,7},{6,14},{7,5},{8,0},{9,11},{1... | collective-permute-start | bytes 196616 | tf_op jit(solution)/shard_map/ppermute | solution.py:288
  31.2 0.1 collective-permute-done.7
  31.2 0.1 convert_add_fusion
  31.3 0.1 slice_reduce_fusion
  31.4 0.1 slice_multiply_fusion.1
  31.5 0.1 add_convert_fusion.8
  31.6 2.2 %collective-permute-done.3 = bf16[8,4096]{1,0:T(8,128)(2,1)S(1)} collective-permute-done((bf16[8,4096]{1,0:T(8,128)(2,1)S(1)}, bf16[8,4096]{1,0:T(8,128)(2,1)S(1)}, u32[]{:S(2)}, u32[]{:S(2)}) %collective-permute-start.3) | collective-permute-done | bytes 65568 | tf_op jit(solution)/shard_map/ppermute | solution.py:288
  33.8 0.1 fusion.8
  33.9 0.1 subtract_convert_fusion
  34.1 0.1 fusion.20
  34.2 0.2 fusion.14
  34.4 0.0 slice-start.3
  34.4 0.5 fusion.31
  35.0 0.2 fusion.6
  35.2 0.3 fusion
  35.7 0.5 fusion.32
  36.2 0.2 fusion.13
  36.4 0.2 fusion.7
  36.7 2.6 %collective-permute-start.8 = (bf16[8,4096]{1,0:T(8,128)(2,1)S(1)}, bf16[8,4096]{1,0:T(8,128)(2,1)S(1)}, u32[]{:S(2)}, u32[]{:S(2)}) collective-permute-start(bf16[8,4096]{1,0:T(8,128)(2,1)S(1)} %bitcast.37), channel_id=1, source_target_pairs={{0,8},{1,3},{2,10},{3,1},{4,12},{5,7},{6,14},{7,5},{8,0},{9,11},{1... | collective-permute-start | bytes 196616 | tf_op jit(solution)/shard_map/ppermute | solution.py:288
  39.2 0.3 fusion.1
  39.6 0.5 collective-permute-start.12
  40.1 4.6 %collective-permute-done.8 = bf16[8,4096]{1,0:T(8,128)(2,1)S(1)} collective-permute-done((bf16[8,4096]{1,0:T(8,128)(2,1)S(1)}, bf16[8,4096]{1,0:T(8,128)(2,1)S(1)}, u32[]{:S(2)}, u32[]{:S(2)}) %collective-permute-start.8) | collective-permute-done | bytes 65568 | tf_op jit(solution)/shard_map/ppermute | solution.py:288
  44.7 2.5 %collective-permute-start.9 = (bf16[16,4096]{1,0:T(8,128)(2,1)S(1)}, bf16[16,4096]{1,0:T(8,128)(2,1)S(1)}, u32[]{:S(2)}, u32[]{:S(2)}) collective-permute-start(bf16[16,4096]{1,0:T(8,128)(2,1)S(1)} %pad_maximum_fusion.2), channel_id=1, source_target_pairs={{0,4},{1,9},{2,6},{3,11},{4,0},{5,13},{6,2},{7,15},{8,12},{9,1},{1... | collective-permute-start | bytes 393224 | tf_op jit(solution)/shard_map/ppermute | solution.py:288
  47.2 1.0 %collective-permute-done.12 = bf16[8,4096]{1,0:T(8,128)(2,1)S(1)} collective-permute-done((bf16[8,4096]{1,0:T(8,128)(2,1)S(1)}, bf16[8,4096]{1,0:T(8,128)(2,1)S(1)}, u32[]{:S(2)}, u32[]{:S(2)}) %collective-permute-start.12) | collective-permute-done | bytes 65568 | tf_op jit(solution)/shard_map/ppermute | solution.py:288
  48.2 0.4 collective-permute-start.13
  48.6 2.4 %collective-permute-done.9 = bf16[16,4096]{1,0:T(8,128)(2,1)S(1)} collective-permute-done((bf16[16,4096]{1,0:T(8,128)(2,1)S(1)}, bf16[16,4096]{1,0:T(8,128)(2,1)S(1)}, u32[]{:S(2)}, u32[]{:S(2)}) %collective-permute-start.9) | collective-permute-done | bytes 131104 | tf_op jit(solution)/shard_map/ppermute | solution.py:288
  51.0 1.6 %collective-permute-start.10 = (bf16[32,4096]{1,0:T(8,128)(2,1)S(1)}, bf16[32,4096]{1,0:T(8,128)(2,1)S(1)}, u32[]{:S(2)}, u32[]{:S(2)}) collective-permute-start(bf16[32,4096]{1,0:T(8,128)(2,1)S(1)} %pad_maximum_fusion), channel_id=1, source_target_pairs={{0,2},{1,5},{2,0},{3,7},{4,6},{5,1},{6,4},{7,3},{8,10},{9,13},{10,... | collective-permute-start | bytes 786440 | tf_op jit(solution)/shard_map/ppermute | solution.py:288
  52.6 2.1 %collective-permute-done.13 = bf16[16,4096]{1,0:T(8,128)(2,1)S(1)} collective-permute-done((bf16[16,4096]{1,0:T(8,128)(2,1)S(1)}, bf16[16,4096]{1,0:T(8,128)(2,1)S(1)}, u32[]{:S(2)}, u32[]{:S(2)}) %collective-permute-start.13) | collective-permute-done | bytes 131104 | tf_op jit(solution)/shard_map/ppermute | solution.py:288
  54.7 1.6 %collective-permute-start.14 = (bf16[32,4096]{1,0:T(8,128)(2,1)S(1)}, bf16[32,4096]{1,0:T(8,128)(2,1)S(1)}, u32[]{:S(2)}, u32[]{:S(2)}) collective-permute-start(bf16[32,4096]{1,0:T(8,128)(2,1)S(1)} %pad_maximum_fusion.1), channel_id=1, source_target_pairs={{0,2},{1,5},{2,0},{3,7},{4,6},{5,1},{6,4},{7,3},{8,10},{9,13},{10,... | collective-permute-start | bytes 786440 | tf_op jit(solution)/shard_map/ppermute | solution.py:288
  56.4 4.8 %collective-permute-done.14 = bf16[32,4096]{1,0:T(8,128)(2,1)S(1)} collective-permute-done((bf16[32,4096]{1,0:T(8,128)(2,1)S(1)}, bf16[32,4096]{1,0:T(8,128)(2,1)S(1)}, u32[]{:S(2)}, u32[]{:S(2)}) %collective-permute-start.14) | collective-permute-done | bytes 262176 | tf_op jit(solution)/shard_map/ppermute | solution.py:288
  61.2 0.1 collective-permute-start.15
  61.3 0.0 collective-permute-done.10
  61.3 0.5 collective-permute-start.11
  61.9 1.3 %collective-permute-done.15.refs_1_ = bf16[64,4096]{1,0:T(8,128)(2,1)S(1)} collective-permute-done((bf16[64,4096]{1,0:T(8,128)(2,1)S(1)}, bf16[64,4096]{1,0:T(8,128)(2,1)S(1)}, u32[]{:S(2)}, u32[]{:S(2)}) %collective-permute-start.15) | collective-permute-done | bytes 524320 | tf_op jit(solution)/shard_map/ppermute | solution.py:288
  63.2 0.0 slice-done.2
  63.2 0.0 slice-done.3
  63.2 2.1 %shard_map.66.refs_3_ = f32[128,1024]{1,0:T(8,128)S(1)} custom-call(s32[1]{0:T(128)} %bitcast.me_ref, bf16[64,4096]{1,0:T(8,128)(2,1)S(1)} %constant_dynamic-update-slice_fusion.4.refs_0_, bf16[64,4096]{1,0:T(8,128)(2,1)S(1)} %collective-permute-done.15.refs_1_, bf16[8192,1024]{1,0:T(8,128)(2,1)S(1)} %bitcast.36), custom_call_target="tpu_custom_call" | custom-call | flops 1073741824 | bytes 9699328 | tf_op jit(solution)/shard_map/pallas_call | solution.py:210
  65.3 0.0 collective-permute-done.11.refs_1_
  65.3 2.8 %shard_map.67 = bf16[128,1024]{1,0:T(8,128)(2,1)} custom-call(s32[1]{0:T(128)} %bitcast.me_ref, bf16[64,4096]{1,0:T(8,128)(2,1)S(1)} %constant_dynamic-update-slice_fusion.refs_0_, bf16[64,4096]{1,0:T(8,128)(2,1)S(1)} %collective-permute-done.11.refs_1_, bf16[8192,1024]{1,0:T(8,128)(2,1)S(1)} %bitcast.36, f32[128,1024]{1,0:T(8,128)S(1)} %shard_map.66.refs_3_), custom_call_target="tpu_custom_call" | custom-call | flops 1073741824 | bytes 9699328 | tf_op jit(solution)/shard_map/pallas_call | solution.py:210
  (37 shorter events, 0.5 us)
Async XLA Ops:
  5.8 4.8 %collective-permute-start.4 = (bf16[64,5248]{1,0:T(8,128)(2,1)S(1)}, bf16[64,5248]{1,0:T(8,128)(2,1)S(1)}, u32[]{:S(2)}, u32[]{:S(2)}) collective-permute-start(bf16[64,5248]{1,0:T(8,128)(2,1)S(1)} %get-tuple-element.17), channel_id=1, source_target_pairs={{0,1},{1,0},{2,3},{3,2},{4,5},{5,4},{6,7},{7,6},{8,9},{9,8},{10,11... | collective-permute-start | bytes 2015240 | tf_op jit(solution)/shard_map/ppermute | solution.py:288
  6.3 56.8 %slice-start = ((s8[16777216]{0:T(1024)(128)(4,1)}), s8[4194304]{0:T(1024)(128)(4,1)S(1)}, s32[]{:S(2)}) async-start(s8[16777216]{0:T(1024)(128)(4,1)} %bitcast.35), calls=%async_computation | async-start | bytes 8388608
  6.3 56.8 %slice-start.1 = ((s8[16777216]{0:T(1024)(128)(4,1)}), s8[4194304]{0:T(1024)(128)(4,1)S(1)}, s32[]{:S(2)}) async-start(s8[16777216]{0:T(1024)(128)(4,1)} %bitcast.35), calls=%async_computation.1 | async-start | bytes 8388608
  10.5 4.8 %copy-start = (bf16[8,256,4,128]{3,2,1,0:T(4,128)(2,1)S(1)}, bf16[8,256,4,128]{3,2,1,0:T(4,128)(2,1)}, u32[]{:S(2)}) copy-start(bf16[8,256,4,128]{3,2,1,0:T(4,128)(2,1)} %param.10) | copy-start | bytes 6291460
  10.5 3.3 %collective-permute-start = (bf16[64,4096]{1,0:T(8,128)(2,1)S(1)}, bf16[64,4096]{1,0:T(8,128)(2,1)S(1)}, u32[]{:S(2)}, u32[]{:S(2)}) collective-permute-start(bf16[64,4096]{1,0:T(8,128)(2,1)S(1)} %get-tuple-element.15), channel_id=1, source_target_pairs={{0,1},{1,0},{2,3},{3,2},{4,5},{5,4},{6,7},{7,6},{8,9},{9,8},{10,11... | collective-permute-start | bytes 1572872 | tf_op jit(solution)/shard_map/ppermute | solution.py:288
  10.7 8.2 %collective-permute-start.5 = (bf16[32,5248]{1,0:T(8,128)(2,1)S(1)}, bf16[32,5248]{1,0:T(8,128)(2,1)S(1)}, u32[]{:S(2)}, u32[]{:S(2)}) collective-permute-start(bf16[32,5248]{1,0:T(8,128)(2,1)S(1)} %add_convert_fusion), channel_id=1, source_target_pairs={{0,2},{1,5},{2,0},{3,7},{4,6},{5,1},{6,4},{7,3},{8,10},{9,13},{10,... | collective-permute-start | bytes 1007624 | tf_op jit(solution)/shard_map/ppermute | solution.py:288
  13.8 2.0 %copy-start.1 = (bf16[8,256,4,128]{3,2,1,0:T(4,128)(2,1)S(1)}, bf16[8,256,4,128]{3,2,1,0:T(4,128)(2,1)}, u32[]{:S(2)}) copy-start(bf16[8,256,4,128]{3,2,1,0:T(4,128)(2,1)} %param.11) | copy-start | bytes 6291460
  13.8 49.3 %slice-start.2 = ((s8[16777216]{0:T(1024)(128)(4,1)}), s8[4194304]{0:T(1024)(128)(4,1)S(1)}, s32[]{:S(2)}) async-start(s8[16777216]{0:T(1024)(128)(4,1)} %bitcast.35), calls=%async_computation.2 | async-start | bytes 8388608
  13.9 7.9 %collective-permute-start.1 = (bf16[32,4096]{1,0:T(8,128)(2,1)S(1)}, bf16[32,4096]{1,0:T(8,128)(2,1)S(1)}, u32[]{:S(2)}, u32[]{:S(2)}) collective-permute-start(bf16[32,4096]{1,0:T(8,128)(2,1)S(1)} %add_convert_fusion.1), channel_id=1, source_target_pairs={{0,2},{1,5},{2,0},{3,7},{4,6},{5,1},{6,4},{7,3},{8,10},{9,13},{10,... | collective-permute-start | bytes 786440 | tf_op jit(solution)/shard_map/ppermute | solution.py:288
  19.0 6.8 %collective-permute-start.6 = (bf16[16,5248]{1,0:T(8,128)(2,1)S(1)}, bf16[16,5248]{1,0:T(8,128)(2,1)S(1)}, u32[]{:S(2)}, u32[]{:S(2)}) collective-permute-start(bf16[16,5248]{1,0:T(8,128)(2,1)S(1)} %add_convert_fusion.2), channel_id=1, source_target_pairs={{0,4},{1,9},{2,6},{3,11},{4,0},{5,13},{6,2},{7,15},{8,12},{9,1},{1... | collective-permute-start | bytes 503816 | tf_op jit(solution)/shard_map/ppermute | solution.py:288
  21.8 6.8 %collective-permute-start.2 = (bf16[16,4096]{1,0:T(8,128)(2,1)S(1)}, bf16[16,4096]{1,0:T(8,128)(2,1)S(1)}, u32[]{:S(2)}, u32[]{:S(2)}) collective-permute-start(bf16[16,4096]{1,0:T(8,128)(2,1)S(1)} %add_convert_fusion.3), channel_id=1, source_target_pairs={{0,4},{1,9},{2,6},{3,11},{4,0},{5,13},{6,2},{7,15},{8,12},{9,1},{1... | collective-permute-start | bytes 393224 | tf_op jit(solution)/shard_map/ppermute | solution.py:288
  25.8 5.4 %collective-permute-start.7 = (bf16[8,5248]{1,0:T(8,128)(2,1)S(1)}, bf16[8,5248]{1,0:T(8,128)(2,1)S(1)}, u32[]{:S(2)}, u32[]{:S(2)}) collective-permute-start(bf16[8,5248]{1,0:T(8,128)(2,1)S(1)} %add_convert_fusion.4), channel_id=1, source_target_pairs={{0,8},{1,3},{2,10},{3,1},{4,12},{5,7},{6,14},{7,5},{8,0},{9,11},{1... | collective-permute-start | bytes 251912 | tf_op jit(solution)/shard_map/ppermute | solution.py:288
  28.6 5.2 %collective-permute-start.3 = (bf16[8,4096]{1,0:T(8,128)(2,1)S(1)}, bf16[8,4096]{1,0:T(8,128)(2,1)S(1)}, u32[]{:S(2)}, u32[]{:S(2)}) collective-permute-start(bf16[8,4096]{1,0:T(8,128)(2,1)S(1)} %add_convert_fusion.7), channel_id=1, source_target_pairs={{0,8},{1,3},{2,10},{3,1},{4,12},{5,7},{6,14},{7,5},{8,0},{9,11},{1... | collective-permute-start | bytes 196616 | tf_op jit(solution)/shard_map/ppermute | solution.py:288
  34.4 28.7 %slice-start.3 = ((s8[16777216]{0:T(1024)(128)(4,1)}), s8[4194304]{0:T(1024)(128)(4,1)S(1)}, s32[]{:S(2)}) async-start(s8[16777216]{0:T(1024)(128)(4,1)} %bitcast.35), calls=%async_computation.3 | async-start | bytes 8388608
  36.7 8.0 %collective-permute-start.8 = (bf16[8,4096]{1,0:T(8,128)(2,1)S(1)}, bf16[8,4096]{1,0:T(8,128)(2,1)S(1)}, u32[]{:S(2)}, u32[]{:S(2)}) collective-permute-start(bf16[8,4096]{1,0:T(8,128)(2,1)S(1)} %bitcast.37), channel_id=1, source_target_pairs={{0,8},{1,3},{2,10},{3,1},{4,12},{5,7},{6,14},{7,5},{8,0},{9,11},{1... | collective-permute-start | bytes 196616 | tf_op jit(solution)/shard_map/ppermute | solution.py:288
  39.6 8.6 %collective-permute-start.12 = (bf16[8,4096]{1,0:T(8,128)(2,1)S(1)}, bf16[8,4096]{1,0:T(8,128)(2,1)S(1)}, u32[]{:S(2)}, u32[]{:S(2)}) collective-permute-start(bf16[8,4096]{1,0:T(8,128)(2,1)S(1)} %bitcast.40), channel_id=1, source_target_pairs={{0,8},{1,3},{2,10},{3,1},{4,12},{5,7},{6,14},{7,5},{8,0},{9,11},{1... | collective-permute-start | bytes 196616 | tf_op jit(solution)/shard_map/ppermute | solution.py:288
  44.7 6.3 %collective-permute-start.9 = (bf16[16,4096]{1,0:T(8,128)(2,1)S(1)}, bf16[16,4096]{1,0:T(8,128)(2,1)S(1)}, u32[]{:S(2)}, u32[]{:S(2)}) collective-permute-start(bf16[16,4096]{1,0:T(8,128)(2,1)S(1)} %pad_maximum_fusion.2), channel_id=1, source_target_pairs={{0,4},{1,9},{2,6},{3,11},{4,0},{5,13},{6,2},{7,15},{8,12},{9,1},{1... | collective-permute-start | bytes 393224 | tf_op jit(solution)/shard_map/ppermute | solution.py:288
  48.2 6.5 %collective-permute-start.13 = (bf16[16,4096]{1,0:T(8,128)(2,1)S(1)}, bf16[16,4096]{1,0:T(8,128)(2,1)S(1)}, u32[]{:S(2)}, u32[]{:S(2)}) collective-permute-start(bf16[16,4096]{1,0:T(8,128)(2,1)S(1)} %pad_maximum_fusion.3), channel_id=1, source_target_pairs={{0,4},{1,9},{2,6},{3,11},{4,0},{5,13},{6,2},{7,15},{8,12},{9,1},{1... | collective-permute-start | bytes 393224 | tf_op jit(solution)/shard_map/ppermute | solution.py:288
  51.0 10.3 %collective-permute-start.10 = (bf16[32,4096]{1,0:T(8,128)(2,1)S(1)}, bf16[32,4096]{1,0:T(8,128)(2,1)S(1)}, u32[]{:S(2)}, u32[]{:S(2)}) collective-permute-start(bf16[32,4096]{1,0:T(8,128)(2,1)S(1)} %pad_maximum_fusion), channel_id=1, source_target_pairs={{0,2},{1,5},{2,0},{3,7},{4,6},{5,1},{6,4},{7,3},{8,10},{9,13},{10,... | collective-permute-start | bytes 786440 | tf_op jit(solution)/shard_map/ppermute | solution.py:288
  54.7 6.4 %collective-permute-start.14 = (bf16[32,4096]{1,0:T(8,128)(2,1)S(1)}, bf16[32,4096]{1,0:T(8,128)(2,1)S(1)}, u32[]{:S(2)}, u32[]{:S(2)}) collective-permute-start(bf16[32,4096]{1,0:T(8,128)(2,1)S(1)} %pad_maximum_fusion.1), channel_id=1, source_target_pairs={{0,2},{1,5},{2,0},{3,7},{4,6},{5,1},{6,4},{7,3},{8,10},{9,13},{10,... | collective-permute-start | bytes 786440 | tf_op jit(solution)/shard_map/ppermute | solution.py:288
  61.2 2.0 %collective-permute-start.15 = (bf16[64,4096]{1,0:T(8,128)(2,1)S(1)}, bf16[64,4096]{1,0:T(8,128)(2,1)S(1)}, u32[]{:S(2)}, u32[]{:S(2)}) collective-permute-start(bf16[64,4096]{1,0:T(8,128)(2,1)S(1)} %constant_dynamic-update-slice_fusion.4.refs_0_), channel_id=1, source_target_pairs={{0,1},{1,0},{2,3},{3,2},{4,5},{5,4},{6,7},{7,6},{8,9},{9,8},{10,11... | collective-permute-start | bytes 1572872 | tf_op jit(solution)/shard_map/ppermute | solution.py:288
  61.3 4.0 %collective-permute-start.11 = (bf16[64,4096]{1,0:T(8,128)(2,1)S(1)}, bf16[64,4096]{1,0:T(8,128)(2,1)S(1)}, u32[]{:S(2)}, u32[]{:S(2)}) collective-permute-start(bf16[64,4096]{1,0:T(8,128)(2,1)S(1)} %constant_dynamic-update-slice_fusion.refs_0_), channel_id=1, source_target_pairs={{0,1},{1,0},{2,3},{3,2},{4,5},{5,4},{6,7},{7,6},{8,9},{9,8},{10,11... | collective-permute-start | bytes 1572872 | tf_op jit(solution)/shard_map/ppermute | solution.py:288

commit v4 on v3

--- a/solution.py
+++ b/solution.py
@@ -16,36 +16,39 @@
 QUERY_WIDTH = QUERY_HEADS * HEAD_SIZE
 QKVW = QUERY_WIDTH + 2 * KEY_VALUE_HEADS * HEAD_SIZE
 TILE = 1024
+ORDERS = ("is", "is")
 LANES = 128
 MIB = 1024 * 1024
 CHUNKS = ((2, 4), (0, 2))
 
 
-def stage_bits(count):
+def stage_bits(count, phase):
     bits = []
     bit = 2
     while bit < count:
         bits.append(bit)
         bit *= 2
-    return bits, bits[1:] + bits[:1]
-
-
-def place(index, count, order):
+    swapped = bits[1:2] + bits[:1] + bits[2:]
+    rotated = bits[1:] + bits[:1]
+    return [{"i": bits, "s": swapped, "r": rotated}[name] for name in ORDERS[phase]]
+
+
+def place(index, count, phase, order):
     result, size = 0, count // 2
-    for bit in stage_bits(count)[order]:
+    for bit in stage_bits(count, phase)[order]:
         size //= 2
         result = result | ((index >> (bit.bit_length() - 1)) & 1) * size
     return result
 
 
-def places(me, count):
-    own = [place(me, count, order) for order in range(2)]
+def places(me, count, phase):
+    own = [place(me, count, phase, order) for order in range(2)]
     core = me & 1
     result = []
     for block in range(count):
         order = block & 1
         half = jnp.bitwise_xor(core, order) * (count // 2)
-        result.append(half + jnp.bitwise_xor(own[order], place(block, count, order)))
+        result.append(half + jnp.bitwise_xor(own[order], place(block, count, phase, order)))
     return result
 
 
@@ -87,7 +90,7 @@
         copy.wait()
     gain = gains[...].astype(jnp.float32)[None, :]
     lane = lax.broadcasted_iota(jnp.int32, (rows, LANES), 1)
-    targets = places(me, count)
+    targets = places(me, count, 0)
     for pair in range(count // 2):
         both = narrow[2 * pair * rows : 2 * (pair + 1) * rows, :].astype(jnp.float32)
         for side in range(2):
@@ -182,7 +185,7 @@
         if out_ref.dtype == jnp.float32:
             out_ref[...] = total[...]
             return
-        sources = places(me_ref[0], count)
+        sources = places(me_ref[0], count, 1)
         for pair in range(count // 2):
             parts = []
             for source in sources[2 * pair : 2 * pair + 2]:
@@ -280,10 +283,10 @@
     return combined.reshape(count_of_rows, heads * GROUP * HEAD_SIZE).astype(jnp.bfloat16)
 
 
-def swap(value, count, stage=None):
-    orders = stage_bits(count)
+def swap(value, count, phase=None, stage=None):
+    orders = None if phase is None else stage_bits(count, phase)
     partners = [
-        (i, i ^ (1 if stage is None else orders[i & 1][stage])) for i in range(count)
+        (i, i ^ (1 if phase is None else orders[i & 1][stage])) for i in range(count)
     ]
     return lax.ppermute(value, "gx", partners)
 
@@ -308,18 +311,11 @@
         self.size //= 2
         part = slice(self.size * self.rows, 2 * self.size * self.rows)
         send = self.combine(part).astype(jnp.bfloat16)
-        self.received.append(swap(send, self.count, len(self.received) - 1))
+        self.received.append(swap(send, self.count, 0, len(self.received) - 1))
         return send
 
     def own(self):
         return self.combine(slice(0, self.rows))
-
-
-def gather_rows(own, count):
-    mine = own
-    for stage in reversed(range(len(stage_bits(count)[0]))):
-        mine = jnp.concatenate([mine, swap(mine, count, stage)], axis=0)
-    return mine, swap(mine, count)
 
 
 def body(count, activations, norm_gain, w_qkv, w_out, cache_keys, value_cache_rows):
@@ -343,38 +339,52 @@
             scaled = rest[0]
         parts.append(Reduction(send, keep, count, rows))
     w_out = tie(w_out, send)
-    for stage in range(len(stage_bits(count)[0])):
+    stages = len(stage_bits(count, 0)[0])
+    for stage in range(stages):
         for part in parts:
             token = part.stage()
         if stage == 0:
             cache_keys = tie(cache_keys, token)
             value_cache_rows = tie(value_cache_rows, token)
-    sums = [part.own() for part in parts]
-
-    lead = sums[0]
-    width = (CHUNKS[0][1] - CHUNKS[0][0]) * per_head
-    own_squares = jnp.sum(lead[:, -LANES:], axis=1)
-    inverse_rms = lax.rsqrt(own_squares / D + 1e-05)[:, None]
-    fresh = lead[:, width:-LANES] * inverse_rms
-    kv_width = KEY_VALUE_HEADS * HEAD_SIZE
-    shape = (rows, KEY_VALUE_HEADS, HEAD_SIZE)
-    fresh_keys = apply_rotary(fresh[:, :kv_width].reshape(shape)).astype(jnp.bfloat16)
-    fresh_values = fresh[:, kv_width:].reshape(shape).astype(jnp.bfloat16)
-
+    gathered = []
+    for order, (low, high) in enumerate(CHUNKS):
+        width = (high - low) * per_head
+        if order > 0:
+            parts[order].keep = tie(parts[order].keep, gathered[-1])
+        sums = parts[order].own()
+        if order == 0:
+            own_squares = jnp.sum(sums[:, -LANES:], axis=1)
+            inverse_rms = lax.rsqrt(own_squares / D + 1e-05)[:, None]
+            fresh = sums[:, width:-LANES] * inverse_rms
+            kv_width = KEY_VALUE_HEADS * HEAD_SIZE
+            shape = (rows, KEY_VALUE_HEADS, HEAD_SIZE)
+            fresh_keys = apply_rotary(fresh[:, :kv_width].reshape(shape)).astype(jnp.bfloat16)
+            fresh_values = fresh[:, kv_width:].reshape(shape).astype(jnp.bfloat16)
+        queries = apply_rotary(
+            (sums[:, :width] * inverse_rms).reshape(rows, width // HEAD_SIZE, HEAD_SIZE)
+        ).astype(jnp.bfloat16)
+        gathered.append(
+            attend(
+                queries,
+                fresh_keys[:, low:high],
+                fresh_values[:, low:high],
+                cache_keys[:, :, low:high],
+                value_cache_rows[:, :, low:high],
+            )
+        )
+
+    for stage in reversed(range(stages)):
+        before = None
+        for order in range(len(CHUNKS)):
+            mine = gathered[order]
+            if before is not None:
+                mine = tie(mine, before)
+            before = mine
+            gathered[order] = jnp.concatenate([mine, swap(mine, count, 1, stage)], axis=0)
     total = None
     for order, (low, high) in enumerate(CHUNKS):
-        width = (high - low) * per_head
-        queries = apply_rotary(
-            (sums[order][:, :width] * inverse_rms).reshape(rows, width // HEAD_SIZE, HEAD_SIZE)
-        ).astype(jnp.bfloat16)
-        attended = attend(
-            queries,
-            fresh_keys[:, low:high],
-            fresh_values[:, low:high],
-            cache_keys[:, :, low:high],
-            value_cache_rows[:, :, low:high],
-        )
-        mine, other = gather_rows(attended, count)
+        mine = gathered[order]
+        other = swap(mine, count)
         total = output_part(
             me, mine, other, w_out, total, count, rows, low * per_head,
             order == len(CHUNKS) - 1,

time: 68.2 us -> 61.7 us (0.905)
  waiting for transfers between devices: 23.5 us -> 13.6 us
  starting transfers between devices: 24.4 us -> 27.6 us
    ppermute x16, waiting for transfers between devices: 23.5 us -> 13.6 us  [swap(): return lax.ppermute(value, 'gx', partners)]
    ppermute x16, starting transfers between devices: 24.4 us -> 27.6 us  [swap(): return lax.ppermute(value, 'gx', partners)]
  transfers between devices with their start and end apart: 16 -> 16, of which waited for: 11 -> 10; matrix products, arithmetic and copies ran while one was open for 3% -> 8% of each run, Pallas kernels for 9% -> 10%
where the time goes in v4:
time: 61.7 us; the launch traced here: 61.5 us
  starting transfers between devices  27.6 us (45%)
  Pallas kernels  14.8 us (24%)
  waiting for transfers between devices  13.6 us (22%)
  matrix products  2.09 us (3%)
  other arithmetic  1.69 us (3%)
  local copies, waits for them, and re-layouts  1.27 us (2%)
    ppermute x16, starting transfers between devices, swap(): return lax.ppermute(value, 'gx', partners)  27.6 us
    ppermute x16, waiting for transfers between devices, swap(): return lax.ppermute(value, 'gx', partners)  13.6 us
    pallas_call x2, Pallas kernels, project(): pl.pallas_call(kernel, in_specs=in_specs, out_specs=[in_vmem] * len(out_s...  9.94 us
    pallas_call x2, Pallas kernels, output_part(): pl.pallas_call(functools.partial(output_kernel, count, rows, tiles, first...  4.9 us
  transfers between devices with their start and end apart: 16, of which 10 were waited for; matrix products, arithmetic and copies ran while one was open for 8% of the time, Pallas kernels for 10%

profile of v4, /device:TPU:0, one launch (start us, length us, event | category | flops | bytes accessed | tf_op | source)
XLA Modules:
  0.0 61.5 jit_solution(5761566796261727599)
XLA Ops:
  0.0 5.8 %shard_map.64 = (bf16[64,5248]{1,0:T(8,128)(2,1)S(1)}, f32[64,5248]{1,0:T(8,128)S(1)}, bf16[128,1024]{1,0:T(8,128)(2,1)S(1)}) custom-call(s32[1]{0:T(128)} %bitcast.me_ref, bf16[128,1024]{1,0:T(8,128)(2,1)} %acts_ref.1, bf16[1024]{0:T(1024)(128)(2,1)} %gain_ref.1, bf16[1024,9216]{1,0:T(8,128)(2,1)} %w_ref.3), custom_call_target="tpu_custom_call" | custom-call | flops 1342177280 | bytes 12500992 | tf_op jit(solution)/shard_map/pallas_call | solution.py:152
  5.8 0.5 collective-permute-start
  6.3 4.1 %shard_map.65 = (bf16[64,4096]{1,0:T(8,128)(2,1)S(1)}, f32[64,4096]{1,0:T(8,128)S(1)}) custom-call(bf16[128,1024]{1,0:T(8,128)(2,1)S(1)} %get-tuple-element.17.scaled, bf16[1024,9216]{1,0:T(8,128)(2,1)} %w_ref.3), custom_call_target="tpu_custom_call" | custom-call | flops 1073741824 | bytes 9961472 | tf_op jit(solution)/shard_map/pallas_call | solution.py:152
  10.5 0.0 copy-start
  10.5 0.1 collective-permute-start.4
  10.7 0.0 collective-permute-done
  10.7 0.1 add_convert_fusion
  10.7 3.0 %collective-permute-start.1 = (bf16[32,5248]{1,0:T(8,128)(2,1)S(1)}, bf16[32,5248]{1,0:T(8,128)(2,1)S(1)}, u32[]{:S(2)}, u32[]{:S(2)}) collective-permute-start(bf16[32,5248]{1,0:T(8,128)(2,1)S(1)} %add_convert_fusion), channel_id=1, source_target_pairs={{0,2},{1,5},{2,0},{3,7},{4,6},{5,1},{6,4},{7,3},{8,10},{9,13},{10,... | collective-permute-start | bytes 1007624 | tf_op jit(solution)/shard_map/ppermute | solution.py:291
  13.8 0.0 collective-permute-done.4
  13.8 0.1 add_convert_fusion.1
  13.8 0.0 slice-start.2
  13.9 1.4 %collective-permute-start.5 = (bf16[32,4096]{1,0:T(8,128)(2,1)S(1)}, bf16[32,4096]{1,0:T(8,128)(2,1)S(1)}, u32[]{:S(2)}, u32[]{:S(2)}) collective-permute-start(bf16[32,4096]{1,0:T(8,128)(2,1)S(1)} %add_convert_fusion.1), channel_id=1, source_target_pairs={{0,2},{1,5},{2,0},{3,7},{4,6},{5,1},{6,4},{7,3},{8,10},{9,13},{10,... | collective-permute-start | bytes 786440 | tf_op jit(solution)/shard_map/ppermute | solution.py:291
  15.3 0.0 copy-done
  15.3 0.5 copy.9
  15.8 0.0 copy-done.1
  15.8 0.5 copy.10
  16.3 2.6 %collective-permute-done.1 = bf16[32,5248]{1,0:T(8,128)(2,1)S(1)} collective-permute-done((bf16[32,5248]{1,0:T(8,128)(2,1)S(1)}, bf16[32,5248]{1,0:T(8,128)(2,1)S(1)}, u32[]{:S(2)}, u32[]{:S(2)}) %collective-permute-start.1) | collective-permute-done | bytes 335904 | tf_op jit(solution)/shard_map/ppermute | solution.py:291
  18.9 0.1 add_convert_fusion.2
  19.0 2.1 %collective-permute-start.2 = (bf16[16,5248]{1,0:T(8,128)(2,1)S(1)}, bf16[16,5248]{1,0:T(8,128)(2,1)S(1)}, u32[]{:S(2)}, u32[]{:S(2)}) collective-permute-start(bf16[16,5248]{1,0:T(8,128)(2,1)S(1)} %add_convert_fusion.2), channel_id=1, source_target_pairs={{0,4},{1,3},{2,6},{3,1},{4,0},{5,7},{6,2},{7,5},{8,12},{9,11},{10,... | collective-permute-start | bytes 503816 | tf_op jit(solution)/shard_map/ppermute | solution.py:291
  21.1 1.1 %collective-permute-done.5 = bf16[32,4096]{1,0:T(8,128)(2,1)S(1)} collective-permute-done((bf16[32,4096]{1,0:T(8,128)(2,1)S(1)}, bf16[32,4096]{1,0:T(8,128)(2,1)S(1)}, u32[]{:S(2)}, u32[]{:S(2)}) %collective-permute-start.5) | collective-permute-done | bytes 262176 | tf_op jit(solution)/shard_map/ppermute | solution.py:291
  22.2 0.1 add_convert_fusion.3
  22.3 2.5 %collective-permute-start.6 = (bf16[16,4096]{1,0:T(8,128)(2,1)S(1)}, bf16[16,4096]{1,0:T(8,128)(2,1)S(1)}, u32[]{:S(2)}, u32[]{:S(2)}) collective-permute-start(bf16[16,4096]{1,0:T(8,128)(2,1)S(1)} %add_convert_fusion.3), channel_id=1, source_target_pairs={{0,4},{1,3},{2,6},{3,1},{4,0},{5,7},{6,2},{7,5},{8,12},{9,11},{10,... | collective-permute-start | bytes 393224 | tf_op jit(solution)/shard_map/ppermute | solution.py:291
  24.7 0.0 collective-permute-done.2
  24.8 2.8 %collective-permute-start.3 = (bf16[8,5248]{1,0:T(8,128)(2,1)S(1)}, bf16[8,5248]{1,0:T(8,128)(2,1)S(1)}, u32[]{:S(2)}, u32[]{:S(2)}) collective-permute-start(bf16[8,5248]{1,0:T(8,128)(2,1)S(1)} %add_convert_fusion.4), channel_id=1, source_target_pairs={{0,8},{1,9},{2,10},{3,11},{4,12},{5,13},{6,14},{7,15},{8,0},{9,1},... | collective-permute-start | bytes 251912 | tf_op jit(solution)/shard_map/ppermute | solution.py:291
  27.6 0.1 collective-permute-done.6
  27.7 4.0 %collective-permute-start.7 = (bf16[8,4096]{1,0:T(8,128)(2,1)S(1)}, bf16[8,4096]{1,0:T(8,128)(2,1)S(1)}, u32[]{:S(2)}, u32[]{:S(2)}) collective-permute-start(bf16[8,4096]{1,0:T(8,128)(2,1)S(1)} %add_convert_fusion.6), channel_id=1, source_target_pairs={{0,8},{1,9},{2,10},{3,11},{4,12},{5,13},{6,14},{7,15},{8,0},{9,1},... | collective-permute-start | bytes 196616 | tf_op jit(solution)/shard_map/ppermute | solution.py:291
  31.7 1.2 %collective-permute-done.3 = bf16[8,5248]{1,0:T(8,128)(2,1)S(1)} collective-permute-done((bf16[8,5248]{1,0:T(8,128)(2,1)S(1)}, bf16[8,5248]{1,0:T(8,128)(2,1)S(1)}, u32[]{:S(2)}, u32[]{:S(2)}) %collective-permute-start.3) | collective-permute-done | bytes 84000 | tf_op jit(solution)/shard_map/ppermute | solution.py:291
  33.0 0.1 convert_add_fusion
  33.0 0.1 slice_reduce_fusion
  33.1 0.1 slice_multiply_fusion.1
  33.2 0.1 fusion.8
  33.3 0.1 subtract_convert_fusion.1
  33.4 0.1 add_convert_fusion.8
  33.6 0.1 fusion.20
  33.6 0.2 fusion.14
  33.9 0.5 fusion.31
  34.4 0.0 slice-start.3
  34.4 0.2 fusion.6
  34.7 0.3 fusion
  35.1 0.3 collective-permute-start.9
  35.4 0.0 collective-permute-done.7
  35.4 0.1 multiply_bitcast_fusion
  35.5 0.1 subtract_convert_fusion
  35.7 0.5 fusion.32
  36.2 0.2 fusion.13
  36.4 0.2 fusion.7
  36.7 0.3 fusion.1
  37.0 2.7 %collective-permute-start.8 = (bf16[8,4096]{1,0:T(8,128)(2,1)S(1)}, bf16[8,4096]{1,0:T(8,128)(2,1)S(1)}, u32[]{:S(2)}, u32[]{:S(2)}) collective-permute-start(bf16[8,4096]{1,0:T(8,128)(2,1)S(1)} %bitcast.47), channel_id=1, source_target_pairs={{0,8},{1,9},{2,10},{3,11},{4,12},{5,13},{6,14},{7,15},{8,0},{9,1},... | collective-permute-start | bytes 196616 | tf_op jit(solution)/shard_map/ppermute | solution.py:291
  39.8 1.5 %collective-permute-done.9 = bf16[8,4096]{1,0:T(8,128)(2,1)S(1)} collective-permute-done((bf16[8,4096]{1,0:T(8,128)(2,1)S(1)}, bf16[8,4096]{1,0:T(8,128)(2,1)S(1)}, u32[]{:S(2)}, u32[]{:S(2)}) %collective-permute-start.9) | collective-permute-done | bytes 65568 | tf_op jit(solution)/shard_map/ppermute | solution.py:291
  41.2 0.1 collective-permute-start.11
  41.3 0.9 %collective-permute-done.8 = bf16[8,4096]{1,0:T(8,128)(2,1)S(1)} collective-permute-done((bf16[8,4096]{1,0:T(8,128)(2,1)S(1)}, bf16[8,4096]{1,0:T(8,128)(2,1)S(1)}, u32[]{:S(2)}, u32[]{:S(2)}) %collective-permute-start.8) | collective-permute-done | bytes 65568 | tf_op jit(solution)/shard_map/ppermute | solution.py:291
  42.3 3.3 %collective-permute-start.10 = (bf16[16,4096]{1,0:T(8,128)(2,1)S(1)}, bf16[16,4096]{1,0:T(8,128)(2,1)S(1)}, u32[]{:S(2)}, u32[]{:S(2)}) collective-permute-start(bf16[16,4096]{1,0:T(8,128)(2,1)S(1)} %pad_maximum_fusion.1), channel_id=1, source_target_pairs={{0,4},{1,3},{2,6},{3,1},{4,0},{5,7},{6,2},{7,5},{8,12},{9,11},{10,... | collective-permute-start | bytes 393224 | tf_op jit(solution)/shard_map/ppermute | solution.py:291
  45.6 1.2 %collective-permute-done.11 = bf16[16,4096]{1,0:T(8,128)(2,1)S(1)} collective-permute-done((bf16[16,4096]{1,0:T(8,128)(2,1)S(1)}, bf16[16,4096]{1,0:T(8,128)(2,1)S(1)}, u32[]{:S(2)}, u32[]{:S(2)}) %collective-permute-start.11) | collective-permute-done | bytes 131104 | tf_op jit(solution)/shard_map/ppermute | solution.py:291
  46.8 2.5 %collective-permute-start.14 = (bf16[32,4096]{1,0:T(8,128)(2,1)S(1)}, bf16[32,4096]{1,0:T(8,128)(2,1)S(1)}, u32[]{:S(2)}, u32[]{:S(2)}) collective-permute-start(bf16[32,4096]{1,0:T(8,128)(2,1)S(1)} %get-tuple-element.34), channel_id=1, source_target_pairs={{0,2},{1,5},{2,0},{3,7},{4,6},{5,1},{6,4},{7,3},{8,10},{9,13},{10,... | collective-permute-start | bytes 786440 | tf_op jit(solution)/shard_map/ppermute | solution.py:291
  49.3 0.7 %collective-permute-done.10 = bf16[16,4096]{1,0:T(8,128)(2,1)S(1)} collective-permute-done((bf16[16,4096]{1,0:T(8,128)(2,1)S(1)}, bf16[16,4096]{1,0:T(8,128)(2,1)S(1)}, u32[]{:S(2)}, u32[]{:S(2)}) %collective-permute-start.10) | collective-permute-done | bytes 131104 | tf_op jit(solution)/shard_map/ppermute | solution.py:291
  50.0 2.1 %collective-permute-start.12 = (bf16[32,4096]{1,0:T(8,128)(2,1)S(1)}, bf16[32,4096]{1,0:T(8,128)(2,1)S(1)}, u32[]{:S(2)}, u32[]{:S(2)}) collective-permute-start(bf16[32,4096]{1,0:T(8,128)(2,1)S(1)} %pad_maximum_fusion), channel_id=1, source_target_pairs={{0,2},{1,5},{2,0},{3,7},{4,6},{5,1},{6,4},{7,3},{8,10},{9,13},{10,... | collective-permute-start | bytes 786440 | tf_op jit(solution)/shard_map/ppermute | solution.py:291
  52.1 1.5 %collective-permute-done.14 = bf16[32,4096]{1,0:T(8,128)(2,1)S(1)} collective-permute-done((bf16[32,4096]{1,0:T(8,128)(2,1)S(1)}, bf16[32,4096]{1,0:T(8,128)(2,1)S(1)}, u32[]{:S(2)}, u32[]{:S(2)}) %collective-permute-start.14) | collective-permute-done | bytes 262176 | tf_op jit(solution)/shard_map/ppermute | solution.py:291
  53.6 0.1 collective-permute-start.15
  53.7 2.7 %collective-permute-done.12 = bf16[32,4096]{1,0:T(8,128)(2,1)S(1)} collective-permute-done((bf16[32,4096]{1,0:T(8,128)(2,1)S(1)}, bf16[32,4096]{1,0:T(8,128)(2,1)S(1)}, u32[]{:S(2)}, u32[]{:S(2)}) %collective-permute-start.12) | collective-permute-done | bytes 262176 | tf_op jit(solution)/shard_map/ppermute | solution.py:291
  56.5 0.1 collective-permute-start.13
  56.5 0.0 collective-permute-done.15.refs_1_
  56.6 2.1 %shard_map.66.refs_3_ = f32[128,1024]{1,0:T(8,128)S(1)} custom-call(s32[1]{0:T(128)} %bitcast.me_ref, bf16[64,4096]{1,0:T(8,128)(2,1)S(1)} %constant_dynamic-update-slice_fusion.7.refs_0_, bf16[64,4096]{1,0:T(8,128)(2,1)S(1)} %collective-permute-done.15.refs_1_, bf16[8192,1024]{1,0:T(8,128)(2,1)S(1)} %bitcast.38), custom_call_target="tpu_custom_call" | custom-call | flops 1073741824 | bytes 9699328 | tf_op jit(solution)/shard_map/pallas_call | solution.py:213
  58.7 0.0 collective-permute-done.13.refs_1_
  58.7 2.8 %shard_map.67 = bf16[128,1024]{1,0:T(8,128)(2,1)} custom-call(s32[1]{0:T(128)} %bitcast.me_ref, bf16[64,4096]{1,0:T(8,128)(2,1)S(1)} %constant_dynamic-update-slice_fusion.5.refs_0_, bf16[64,4096]{1,0:T(8,128)(2,1)S(1)} %collective-permute-done.13.refs_1_, bf16[8192,1024]{1,0:T(8,128)(2,1)S(1)} %bitcast.38, f32[128,1024]{1,0:T(8,128)S(1)} %shard_map.66.refs_3_), custom_call_target="tpu_custom_call" | custom-call | flops 1073741824 | bytes 9699328 | tf_op jit(solution)/shard_map/pallas_call | solution.py:213
  (35 shorter events, 0.5 us)
Async XLA Ops:
  5.8 4.8 %collective-permute-start = (bf16[64,5248]{1,0:T(8,128)(2,1)S(1)}, bf16[64,5248]{1,0:T(8,128)(2,1)S(1)}, u32[]{:S(2)}, u32[]{:S(2)}) collective-permute-start(bf16[64,5248]{1,0:T(8,128)(2,1)S(1)} %get-tuple-element.20), channel_id=1, source_target_pairs={{0,1},{1,0},{2,3},{3,2},{4,5},{5,4},{6,7},{7,6},{8,9},{9,8},{10,11... | collective-permute-start | bytes 2015240 | tf_op jit(solution)/shard_map/ppermute | solution.py:291
  6.3 50.2 %slice-start = ((s8[16777216]{0:T(1024)(128)(4,1)}), s8[4194304]{0:T(1024)(128)(4,1)S(1)}, s32[]{:S(2)}) async-start(s8[16777216]{0:T(1024)(128)(4,1)} %bitcast.37), calls=%async_computation | async-start | bytes 8388608
  6.3 50.2 %slice-start.1 = ((s8[16777216]{0:T(1024)(128)(4,1)}), s8[4194304]{0:T(1024)(128)(4,1)S(1)}, s32[]{:S(2)}) async-start(s8[16777216]{0:T(1024)(128)(4,1)} %bitcast.37), calls=%async_computation.1 | async-start | bytes 8388608
  10.5 4.8 %copy-start = (bf16[8,256,4,128]{3,2,1,0:T(4,128)(2,1)S(1)}, bf16[8,256,4,128]{3,2,1,0:T(4,128)(2,1)}, u32[]{:S(2)}) copy-start(bf16[8,256,4,128]{3,2,1,0:T(4,128)(2,1)} %param.10) | copy-start | bytes 6291460
  10.5 3.3 %collective-permute-start.4 = (bf16[64,4096]{1,0:T(8,128)(2,1)S(1)}, bf16[64,4096]{1,0:T(8,128)(2,1)S(1)}, u32[]{:S(2)}, u32[]{:S(2)}) collective-permute-start(bf16[64,4096]{1,0:T(8,128)(2,1)S(1)} %get-tuple-element.21), channel_id=1, source_target_pairs={{0,1},{1,0},{2,3},{3,2},{4,5},{5,4},{6,7},{7,6},{8,9},{9,8},{10,11... | collective-permute-start | bytes 1572872 | tf_op jit(solution)/shard_map/ppermute | solution.py:291
  10.7 8.2 %collective-permute-start.1 = (bf16[32,5248]{1,0:T(8,128)(2,1)S(1)}, bf16[32,5248]{1,0:T(8,128)(2,1)S(1)}, u32[]{:S(2)}, u32[]{:S(2)}) collective-permute-start(bf16[32,5248]{1,0:T(8,128)(2,1)S(1)} %add_convert_fusion), channel_id=1, source_target_pairs={{0,2},{1,5},{2,0},{3,7},{4,6},{5,1},{6,4},{7,3},{8,10},{9,13},{10,... | collective-permute-start | bytes 1007624 | tf_op jit(solution)/shard_map/ppermute | solution.py:291
  13.8 2.0 %copy-start.1 = (bf16[8,256,4,128]{3,2,1,0:T(4,128)(2,1)S(1)}, bf16[8,256,4,128]{3,2,1,0:T(4,128)(2,1)}, u32[]{:S(2)}) copy-start(bf16[8,256,4,128]{3,2,1,0:T(4,128)(2,1)} %param.11) | copy-start | bytes 6291460
  13.8 42.7 %slice-start.2 = ((s8[16777216]{0:T(1024)(128)(4,1)}), s8[4194304]{0:T(1024)(128)(4,1)S(1)}, s32[]{:S(2)}) async-start(s8[16777216]{0:T(1024)(128)(4,1)} %bitcast.37), calls=%async_computation.2 | async-start | bytes 8388608
  13.9 8.4 %collective-permute-start.5 = (bf16[32,4096]{1,0:T(8,128)(2,1)S(1)}, bf16[32,4096]{1,0:T(8,128)(2,1)S(1)}, u32[]{:S(2)}, u32[]{:S(2)}) collective-permute-start(bf16[32,4096]{1,0:T(8,128)(2,1)S(1)} %add_convert_fusion.1), channel_id=1, source_target_pairs={{0,2},{1,5},{2,0},{3,7},{4,6},{5,1},{6,4},{7,3},{8,10},{9,13},{10,... | collective-permute-start | bytes 786440 | tf_op jit(solution)/shard_map/ppermute | solution.py:291
  19.0 5.8 %collective-permute-start.2 = (bf16[16,5248]{1,0:T(8,128)(2,1)S(1)}, bf16[16,5248]{1,0:T(8,128)(2,1)S(1)}, u32[]{:S(2)}, u32[]{:S(2)}) collective-permute-start(bf16[16,5248]{1,0:T(8,128)(2,1)S(1)} %add_convert_fusion.2), channel_id=1, source_target_pairs={{0,4},{1,3},{2,6},{3,1},{4,0},{5,7},{6,2},{7,5},{8,12},{9,11},{10,... | collective-permute-start | bytes 503816 | tf_op jit(solution)/shard_map/ppermute | solution.py:291
  22.3 5.4 %collective-permute-start.6 = (bf16[16,4096]{1,0:T(8,128)(2,1)S(1)}, bf16[16,4096]{1,0:T(8,128)(2,1)S(1)}, u32[]{:S(2)}, u32[]{:S(2)}) collective-permute-start(bf16[16,4096]{1,0:T(8,128)(2,1)S(1)} %add_convert_fusion.3), channel_id=1, source_target_pairs={{0,4},{1,3},{2,6},{3,1},{4,0},{5,7},{6,2},{7,5},{8,12},{9,11},{10,... | collective-permute-start | bytes 393224 | tf_op jit(solution)/shard_map/ppermute | solution.py:291
  24.8 8.2 %collective-permute-start.3 = (bf16[8,5248]{1,0:T(8,128)(2,1)S(1)}, bf16[8,5248]{1,0:T(8,128)(2,1)S(1)}, u32[]{:S(2)}, u32[]{:S(2)}) collective-permute-start(bf16[8,5248]{1,0:T(8,128)(2,1)S(1)} %add_convert_fusion.4), channel_id=1, source_target_pairs={{0,8},{1,9},{2,10},{3,11},{4,12},{5,13},{6,14},{7,15},{8,0},{9,1},... | collective-permute-start | bytes 251912 | tf_op jit(solution)/shard_map/ppermute | solution.py:291
  27.7 7.7 %collective-permute-start.7 = (bf16[8,4096]{1,0:T(8,128)(2,1)S(1)}, bf16[8,4096]{1,0:T(8,128)(2,1)S(1)}, u32[]{:S(2)}, u32[]{:S(2)}) collective-permute-start(bf16[8,4096]{1,0:T(8,128)(2,1)S(1)} %add_convert_fusion.6), channel_id=1, source_target_pairs={{0,8},{1,9},{2,10},{3,11},{4,12},{5,13},{6,14},{7,15},{8,0},{9,1},... | collective-permute-start | bytes 196616 | tf_op jit(solution)/shard_map/ppermute | solution.py:291
  34.4 22.2 %slice-start.3 = ((s8[16777216]{0:T(1024)(128)(4,1)}), s8[4194304]{0:T(1024)(128)(4,1)S(1)}, s32[]{:S(2)}) async-start(s8[16777216]{0:T(1024)(128)(4,1)} %bitcast.37), calls=%async_computation.3 | async-start | bytes 8388608
  35.1 6.2 %collective-permute-start.9 = (bf16[8,4096]{1,0:T(8,128)(2,1)S(1)}, bf16[8,4096]{1,0:T(8,128)(2,1)S(1)}, u32[]{:S(2)}, u32[]{:S(2)}) collective-permute-start(bf16[8,4096]{1,0:T(8,128)(2,1)S(1)} %bitcast.51), channel_id=1, source_target_pairs={{0,8},{1,9},{2,10},{3,11},{4,12},{5,13},{6,14},{7,15},{8,0},{9,1},... | collective-permute-start | bytes 196616 | tf_op jit(solution)/shard_map/ppermute | solution.py:291
  37.0 5.2 %collective-permute-start.8 = (bf16[8,4096]{1,0:T(8,128)(2,1)S(1)}, bf16[8,4096]{1,0:T(8,128)(2,1)S(1)}, u32[]{:S(2)}, u32[]{:S(2)}) collective-permute-start(bf16[8,4096]{1,0:T(8,128)(2,1)S(1)} %bitcast.47), channel_id=1, source_target_pairs={{0,8},{1,9},{2,10},{3,11},{4,12},{5,13},{6,14},{7,15},{8,0},{9,1},... | collective-permute-start | bytes 196616 | tf_op jit(solution)/shard_map/ppermute | solution.py:291
  41.2 5.5 %collective-permute-start.11 = (bf16[16,4096]{1,0:T(8,128)(2,1)S(1)}, bf16[16,4096]{1,0:T(8,128)(2,1)S(1)}, u32[]{:S(2)}, u32[]{:S(2)}) collective-permute-start(bf16[16,4096]{1,0:T(8,128)(2,1)S(1)} %get-tuple-element.37), channel_id=1, source_target_pairs={{0,4},{1,3},{2,6},{3,1},{4,0},{5,7},{6,2},{7,5},{8,12},{9,11},{10,... | collective-permute-start | bytes 393224 | tf_op jit(solution)/shard_map/ppermute | solution.py:291
  42.3 7.7 %collective-permute-start.10 = (bf16[16,4096]{1,0:T(8,128)(2,1)S(1)}, bf16[16,4096]{1,0:T(8,128)(2,1)S(1)}, u32[]{:S(2)}, u32[]{:S(2)}) collective-permute-start(bf16[16,4096]{1,0:T(8,128)(2,1)S(1)} %pad_maximum_fusion.1), channel_id=1, source_target_pairs={{0,4},{1,3},{2,6},{3,1},{4,0},{5,7},{6,2},{7,5},{8,12},{9,11},{10,... | collective-permute-start | bytes 393224 | tf_op jit(solution)/shard_map/ppermute | solution.py:291
  46.8 6.8 %collective-permute-start.14 = (bf16[32,4096]{1,0:T(8,128)(2,1)S(1)}, bf16[32,4096]{1,0:T(8,128)(2,1)S(1)}, u32[]{:S(2)}, u32[]{:S(2)}) collective-permute-start(bf16[32,4096]{1,0:T(8,128)(2,1)S(1)} %get-tuple-element.34), channel_id=1, source_target_pairs={{0,2},{1,5},{2,0},{3,7},{4,6},{5,1},{6,4},{7,3},{8,10},{9,13},{10,... | collective-permute-start | bytes 786440 | tf_op jit(solution)/shard_map/ppermute | solution.py:291
  50.0 6.4 %collective-permute-start.12 = (bf16[32,4096]{1,0:T(8,128)(2,1)S(1)}, bf16[32,4096]{1,0:T(8,128)(2,1)S(1)}, u32[]{:S(2)}, u32[]{:S(2)}) collective-permute-start(bf16[32,4096]{1,0:T(8,128)(2,1)S(1)} %pad_maximum_fusion), channel_id=1, source_target_pairs={{0,2},{1,5},{2,0},{3,7},{4,6},{5,1},{6,4},{7,3},{8,10},{9,13},{10,... | collective-permute-start | bytes 786440 | tf_op jit(solution)/shard_map/ppermute | solution.py:291
  53.6 2.9 %collective-permute-start.15 = (bf16[64,4096]{1,0:T(8,128)(2,1)S(1)}, bf16[64,4096]{1,0:T(8,128)(2,1)S(1)}, u32[]{:S(2)}, u32[]{:S(2)}) collective-permute-start(bf16[64,4096]{1,0:T(8,128)(2,1)S(1)} %constant_dynamic-update-slice_fusion.7.refs_0_), channel_id=1, source_target_pairs={{0,1},{1,0},{2,3},{3,2},{4,5},{5,4},{6,7},{7,6},{8,9},{9,8},{10,11... | collective-permute-start | bytes 1572872 | tf_op jit(solution)/shard_map/ppermute | solution.py:291
  56.5 2.2 %collective-permute-start.13 = (bf16[64,4096]{1,0:T(8,128)(2,1)S(1)}, bf16[64,4096]{1,0:T(8,128)(2,1)S(1)}, u32[]{:S(2)}, u32[]{:S(2)}) collective-permute-start(bf16[64,4096]{1,0:T(8,128)(2,1)S(1)} %constant_dynamic-update-slice_fusion.5.refs_0_), channel_id=1, source_target_pairs={{0,1},{1,0},{2,3},{3,2},{4,5},{5,4},{6,7},{7,6},{8,9},{9,8},{10,11... | collective-permute-start | bytes 1572872 | tf_op jit(solution)/shard_map/ppermute | solution.py:291

commit v5 on v4

--- a/solution.py
+++ b/solution.py
@@ -16,6 +16,7 @@
 QUERY_WIDTH = QUERY_HEADS * HEAD_SIZE
 QKVW = QUERY_WIDTH + 2 * KEY_VALUE_HEADS * HEAD_SIZE
 TILE = 1024
+COLUMNS = 256
 ORDERS = ("is", "is")
 LANES = 128
 MIB = 1024 * 1024
@@ -64,8 +65,9 @@
 
 def multiply(copies, scaled, weights, send_ref, keep_ref):
     half = keep_ref.shape[0]
-    for tile, copy in enumerate(copies):
-        copy.wait()
+    for tile in range(weights.shape[0]):
+        if copies:
+            copies[tile].wait()
         product = jnp.dot(scaled[...], weights[tile], preferred_element_type=jnp.float32)
         columns = slice(tile * TILE, (tile + 1) * TILE)
         keep_ref[:, columns] = product[:half]
@@ -73,10 +75,11 @@
 
 
 def first_kernel(
-    count, rows, start, width,
-    me_ref, acts_ref, gain_ref, w_ref, send_ref, keep_ref, scaled,
-    narrow, gains, ordered, squares, weights, small_sems, sems,
+    count, rows, span, later_span,
+    me_ref, acts_ref, gain_ref, w_ref, send_ref, keep_ref, scaled, later_weights,
+    narrow, gains, ordered, squares, weights, small_sems, sems, later_sems,
 ):
+    start, width = span
     half = count * rows // 2
     me = me_ref[0]
     small = [
@@ -84,7 +87,8 @@
         pltpu.make_async_copy(gain_ref, gains, small_sems.at[1]),
     ]
     copies = fetch(w_ref, weights, sems, start, width // TILE)
-    for copy in small + copies:
+    later = fetch(w_ref, later_weights, later_sems, later_span[0], later_span[1] // TILE)
+    for copy in small + copies + later:
         copy.start()
     for copy in small:
         copy.wait()
@@ -106,124 +110,111 @@
     keep_ref[:, width:] = squares[:half]
     send_ref[:, width:] = squares[half:].astype(jnp.bfloat16)
     multiply(copies, scaled, weights, send_ref, keep_ref)
-
-
-def later_kernel(start, width, scaled, w_ref, send_ref, keep_ref, weights, sems):
-    copies = fetch(w_ref, weights, sems, start, width // TILE)
-    for copy in copies:
-        copy.start()
-    multiply(copies, scaled, weights, send_ref, keep_ref)
-
-
-def project(me, activations, gain, w_qkv, scaled, count, rows, start, width):
-    tiles = width // TILE
+    for copy in later:
+        copy.wait()
+
+
+def later_kernel(scaled, weights, send_ref, keep_ref):
+    multiply(None, scaled, weights, send_ref, keep_ref)
+
+
+def project(me, activations, gain, w_qkv, count, rows, spans):
     depth = w_qkv.shape[0]
     half = count * rows // 2
-    first = scaled is None
-    whole = width + (LANES if first else 0)
     in_hbm = pl.BlockSpec(memory_space=pltpu.HBM)
     in_vmem = pl.BlockSpec(memory_space=pltpu.VMEM)
-    out_shape = [
-        jax.ShapeDtypeStruct((half, whole), jnp.bfloat16),
-        jax.ShapeDtypeStruct((half, whole), jnp.float32),
-    ]
-    scratch = [
-        pltpu.VMEM((tiles, depth, TILE), jnp.bfloat16),
-        pltpu.SemaphoreType.DMA((tiles,)),
-    ]
-    if first:
-        kernel = functools.partial(first_kernel, count, rows, start, width)
-        operands = (me, activations, gain, w_qkv)
-        in_specs = [pl.BlockSpec(memory_space=pltpu.SMEM)] + [in_hbm] * 3
-        out_shape.append(jax.ShapeDtypeStruct(activations.shape, jnp.bfloat16))
-        scratch = [
+
+    def call(kernel, in_specs, operands, width, whole, more_out, scratch):
+        out_shape = [
+            jax.ShapeDtypeStruct((half, whole), jnp.bfloat16),
+            jax.ShapeDtypeStruct((half, whole), jnp.float32),
+        ] + more_out
+        return pl.pallas_call(
+            kernel,
+            in_specs=in_specs,
+            out_specs=[in_vmem] * len(out_shape),
+            scratch_shapes=scratch,
+            out_shape=out_shape,
+            compiler_params=pltpu.CompilerParams(vmem_limit_bytes=28 * MIB),
+            cost_estimate=pl.CostEstimate(
+                flops=4 * half * depth * width,
+                bytes_accessed=2 * depth * width + 6 * half * whole,
+                transcendentals=0,
+            ),
+        )(*operands)
+
+    tiles, later_tiles = [width // TILE for _, width in spans]
+    width, later_width = [width for _, width in spans]
+    send, keep, scaled, weights = call(
+        functools.partial(first_kernel, count, rows, *spans),
+        [pl.BlockSpec(memory_space=pltpu.SMEM)] + [in_hbm] * 3,
+        (me, activations, gain, w_qkv),
+        width,
+        width + LANES,
+        [
+            jax.ShapeDtypeStruct(activations.shape, jnp.bfloat16),
+            jax.ShapeDtypeStruct((later_tiles, depth, TILE), jnp.bfloat16),
+        ],
+        [
             pltpu.VMEM(activations.shape, jnp.bfloat16),
             pltpu.VMEM(gain.shape, jnp.bfloat16),
             pltpu.VMEM(activations.shape, jnp.float32),
             pltpu.VMEM((2 * half, LANES), jnp.float32),
-            scratch[0],
+            pltpu.VMEM((tiles, depth, TILE), jnp.bfloat16),
             pltpu.SemaphoreType.DMA((2,)),
-            scratch[1],
-        ]
-    else:
-        kernel = functools.partial(later_kernel, start, width)
-        operands = (scaled, w_qkv)
-        in_specs = [in_vmem, in_hbm]
+            pltpu.SemaphoreType.DMA((tiles,)),
+            pltpu.SemaphoreType.DMA((later_tiles,)),
+        ],
+    )
+    later = call(
+        later_kernel, [in_vmem] * 2, (scaled, weights), later_width, later_width, [], []
+    )
+    return (send, keep), later
+
+
+def output_kernel(count, rows, start, me_ref, mine_ref, other_ref, w_ref, *refs):
+    *before, out_ref, total = refs
+    depth = mine_ref.shape[1]
+    left = jnp.concatenate([mine_ref[...], other_ref[...]], axis=0)
+    last = out_ref.dtype != jnp.float32
+    width = min(COLUMNS, total.shape[1])
+    for column in range(0, total.shape[1], width):
+        columns = slice(column, column + width)
+        product = jnp.dot(
+            left, w_ref[start : start + depth, columns], preferred_element_type=jnp.float32
+        )
+        for part in before:
+            product += part[:, columns]
+        if last:
+            total[:, columns] = product
+        else:
+            out_ref[:, columns] = product
+    if not last:
+        return
+    sources = places(me_ref[0], count, 1)
+    for pair in range(count // 2):
+        parts = []
+        for source in sources[2 * pair : 2 * pair + 2]:
+            parts.append(total[pl.ds(pl.multiple_of(source * rows, rows), rows), :])
+        where = slice(2 * pair * rows, 2 * (pair + 1) * rows)
+        out_ref[where, :] = jnp.concatenate(parts, axis=0).astype(out_ref.dtype)
+
+
+def output_part(me, mine, other, w_out, before, count, rows, start, last):
+    depth, columns = mine.shape[1], w_out.shape[1]
+    shape = (count * rows, columns)
+    operands = (mine, other, w_out) + (() if before is None else (before,))
+    in_vmem = pl.BlockSpec(memory_space=pltpu.VMEM)
     return pl.pallas_call(
-        kernel,
-        in_specs=in_specs,
-        out_specs=[in_vmem] * len(out_shape),
-        scratch_shapes=scratch,
-        out_shape=out_shape,
-        compiler_params=pltpu.CompilerParams(vmem_limit_bytes=24 * MIB),
+        functools.partial(output_kernel, count, rows, start),
+        in_specs=[pl.BlockSpec(memory_space=pltpu.SMEM)] + [in_vmem] * len(operands),
+        out_specs=in_vmem,
+        scratch_shapes=[pltpu.VMEM(shape, jnp.float32)],
+        out_shape=jax.ShapeDtypeStruct(shape, jnp.bfloat16 if last else jnp.float32),
+        compiler_params=pltpu.CompilerParams(vmem_limit_bytes=28 * MIB),
         cost_estimate=pl.CostEstimate(
-            flops=4 * half * depth * width,
-            bytes_accessed=2 * depth * width + 6 * half * whole,
-            transcendentals=0,
-        ),
-    )(*operands)
-
-
-def output_kernel(count, rows, tiles, first, me_ref, *refs):
-    mine_ref, other_ref, w_ref = refs[:3]
-    out_ref, total = refs[-2:]
-    step = pl.program_id(0)
-    columns = pl.ds(pl.multiple_of(step * TILE, TILE), TILE)
-    left = jnp.concatenate([mine_ref[:, columns], other_ref[:, columns]], axis=0)
-    product = jnp.dot(left, w_ref[...], preferred_element_type=jnp.float32)
-
-    @pl.when(step == 0)
-    def _():
-        total[...] = product if first else refs[3][...] + product
-
-    @pl.when(step > 0)
-    def _():
-        total[...] += product
-
-    @pl.when(step == tiles - 1)
-    def _():
-        if out_ref.dtype == jnp.float32:
-            out_ref[...] = total[...]
-            return
-        sources = places(me_ref[0], count, 1)
-        for pair in range(count // 2):
-            parts = []
-            for source in sources[2 * pair : 2 * pair + 2]:
-                parts.append(total[pl.ds(pl.multiple_of(source * rows, rows), rows), :])
-            where = slice(2 * pair * rows, 2 * (pair + 1) * rows)
-            out_ref[where, :] = jnp.concatenate(parts, axis=0).astype(out_ref.dtype)
-
-
-def output_part(me, mine, other, w_out, before, count, rows, start, last):
-    width = mine.shape[1]
-    tiles = width // TILE
-    columns = w_out.shape[1]
-    whole = lambda j, me: (0, 0)
-    in_specs = [
-        pl.BlockSpec(mine.shape, whole),
-        pl.BlockSpec(other.shape, whole),
-        pl.BlockSpec((TILE, columns), lambda j, me: (start // TILE + j, 0)),
-    ]
-    operands = [mine, other, w_out]
-    first = before is None
-    if not first:
-        in_specs.append(pl.BlockSpec(before.shape, whole))
-        operands.append(before)
-    shape = (count * rows, columns)
-    return pl.pallas_call(
-        functools.partial(output_kernel, count, rows, tiles, first),
-        grid_spec=pltpu.PrefetchScalarGridSpec(
-            num_scalar_prefetch=1,
-            grid=(tiles,),
-            in_specs=in_specs,
-            out_specs=pl.BlockSpec(shape, whole),
-            scratch_shapes=[pltpu.VMEM(shape, jnp.float32)],
-        ),
-        out_shape=jax.ShapeDtypeStruct(shape, jnp.bfloat16 if last else jnp.float32),
-        compiler_params=pltpu.CompilerParams(vmem_limit_bytes=20 * MIB),
-        cost_estimate=pl.CostEstimate(
-            flops=2 * shape[0] * width * columns,
-            bytes_accessed=2 * width * columns + 2 * shape[0] * (width + columns),
+            flops=2 * shape[0] * depth * columns,
+            bytes_accessed=2 * depth * columns + 2 * shape[0] * (depth + columns),
             transcendentals=0,
         ),
     )(me, *operands)
@@ -327,16 +318,12 @@
     ]
     per_head = GROUP * HEAD_SIZE
 
-    parts = []
-    scaled = None
+    spans = []
     for order, (low, high) in enumerate(CHUNKS):
         start = low * per_head
-        width = (high * per_head if order else QKVW) - start
-        send, keep, *rest = project(
-            me, activations, norm_gain, w_qkv, scaled, count, rows, start, width
-        )
-        if order == 0:
-            scaled = rest[0]
+        spans.append((start, (high * per_head if order else QKVW) - start))
+    parts = []
+    for send, keep in project(me, activations, norm_gain, w_qkv, count, rows, spans):
         parts.append(Reduction(send, keep, count, rows))
     w_out = tie(w_out, send)
     stages = len(stage_bits(count, 0)[0])

time: 61.7 us -> 59.9 us (0.971)
  Pallas kernels: 14.8 us -> 12.3 us
  waiting for transfers between devices: 13.6 us -> 14.4 us
    pallas_call x4, Pallas kernels: 14.8 us -> 12.3 us  [the longest x2 8.95 us: call(): pl.pallas_call(kernel, in_specs=in_specs, out_specs=[in_vmem] * len(out_s...]
    ppermute x16, waiting for transfers between devices: 13.6 us -> 14.4 us  [swap(): return lax.ppermute(value, 'gx', partners)]
  transfers between devices with their start and end apart: 16 -> 16, of which waited for: 10 -> 11; matrix products, arithmetic and copies ran while one was open for 8% -> 8% of each run, Pallas kernels for 10% -> 4%
where the time goes in v5:
time: 59.9 us; the launch traced here: 59.7 us
  starting transfers between devices  27.5 us (46%)
  waiting for transfers between devices  14.4 us (24%)
  Pallas kernels  12.3 us (21%)
  matrix products  2.09 us (3%)
  other arithmetic  1.68 us (3%)
  local copies, waits for them, and re-layouts  1.27 us (2%)
    ppermute x16, starting transfers between devices, swap(): return lax.ppermute(value, 'gx', partners)  27.5 us
    ppermute x16, waiting for transfers between devices, swap(): return lax.ppermute(value, 'gx', partners)  14.4 us
    pallas_call x2, Pallas kernels, call(): pl.pallas_call(kernel, in_specs=in_specs, out_specs=[in_vmem] * len(out_s...  8.95 us
    pallas_call x2, Pallas kernels, output_part(): pl.pallas_call(functools.partial(output_kernel, count, rows, start), in_s...  3.34 us
  transfers between devices with their start and end apart: 16, of which 11 were waited for; matrix products, arithmetic and copies ran while one was open for 8% of the time, Pallas kernels for 4%

profile of v5, /device:TPU:0, one launch (start us, length us, event | category | flops | bytes accessed | tf_op | source)
XLA Modules:
  0.0 59.7 jit_solution(8757115025873163211)
XLA Ops:
  0.0 7.7 %shard_map.64 = (bf16[64,5248]{1,0:T(8,128)(2,1)S(1)}, f32[64,5248]{1,0:T(8,128)S(1)}, bf16[128,1024]{1,0:T(8,128)(2,1)S(1)}, bf16[4,1024,1024]{2,1,0:T(8,128)(2,1)S(1)}) custom-call(s32[1]{0:T(128)} %bitcast.me_ref, bf16[128,1024]{1,0:T(8,128)(2,1)} %acts_ref.1, bf16[1024]{0:T(1024)(128)(2,1)} %gain_ref.1, bf16[1024,9216]{1,0:T(8,128)(2,1)} %w_ref.1), custom_call_target="tpu_custom_call" | custom-call | flops 1342177280 | bytes 12500992 | tf_op jit(solution)/shard_map/pallas_call | solution.py:132
  7.7 0.5 collective-permute-start
  8.2 1.3 %shard_map.65 = (bf16[64,4096]{1,0:T(8,128)(2,1)S(1)}, f32[64,4096]{1,0:T(8,128)S(1)}) custom-call(bf16[128,1024]{1,0:T(8,128)(2,1)S(1)} %get-tuple-element.18.scaled, bf16[4,1024,1024]{2,1,0:T(8,128)(2,1)S(1)} %get-tuple-element.19.weights), custom_call_target="tpu_custom_call" | custom-call | flops 1073741824 | bytes 9961472 | tf_op jit(solution)/shard_map/pallas_call | solution.py:132
  9.5 0.0 copy-start
  9.5 0.1 collective-permute-start.4
  9.7 0.3 collective-permute-done
  10.0 0.1 add_convert_fusion
  10.0 3.0 %collective-permute-start.1 = (bf16[32,5248]{1,0:T(8,128)(2,1)S(1)}, bf16[32,5248]{1,0:T(8,128)(2,1)S(1)}, u32[]{:S(2)}, u32[]{:S(2)}) collective-permute-start(bf16[32,5248]{1,0:T(8,128)(2,1)S(1)} %add_convert_fusion), channel_id=1, source_target_pairs={{0,2},{1,5},{2,0},{3,7},{4,6},{5,1},{6,4},{7,3},{8,10},{9,13},{10,... | collective-permute-start | bytes 1007624 | tf_op jit(solution)/shard_map/ppermute | solution.py:282
  13.0 0.0 collective-permute-done.4
  13.0 0.1 add_convert_fusion.1
  13.0 1.2 %collective-permute-start.5 = (bf16[32,4096]{1,0:T(8,128)(2,1)S(1)}, bf16[32,4096]{1,0:T(8,128)(2,1)S(1)}, u32[]{:S(2)}, u32[]{:S(2)}) collective-permute-start(bf16[32,4096]{1,0:T(8,128)(2,1)S(1)} %add_convert_fusion.1), channel_id=1, source_target_pairs={{0,2},{1,5},{2,0},{3,7},{4,6},{5,1},{6,4},{7,3},{8,10},{9,13},{10,... | collective-permute-start | bytes 786440 | tf_op jit(solution)/shard_map/ppermute | solution.py:282
  14.3 0.0 copy-done
  14.3 0.5 copy.9
  14.8 0.0 copy-done.1
  14.8 0.0 slice-start.2
  14.8 0.5 copy.10
  15.3 2.8 %collective-permute-done.1 = bf16[32,5248]{1,0:T(8,128)(2,1)S(1)} collective-permute-done((bf16[32,5248]{1,0:T(8,128)(2,1)S(1)}, bf16[32,5248]{1,0:T(8,128)(2,1)S(1)}, u32[]{:S(2)}, u32[]{:S(2)}) %collective-permute-start.1) | collective-permute-done | bytes 335904 | tf_op jit(solution)/shard_map/ppermute | solution.py:282
  18.1 0.1 add_convert_fusion.2
  18.2 2.1 %collective-permute-start.2 = (bf16[16,5248]{1,0:T(8,128)(2,1)S(1)}, bf16[16,5248]{1,0:T(8,128)(2,1)S(1)}, u32[]{:S(2)}, u32[]{:S(2)}) collective-permute-start(bf16[16,5248]{1,0:T(8,128)(2,1)S(1)} %add_convert_fusion.2), channel_id=1, source_target_pairs={{0,4},{1,3},{2,6},{3,1},{4,0},{5,7},{6,2},{7,5},{8,12},{9,11},{10,... | collective-permute-start | bytes 503816 | tf_op jit(solution)/shard_map/ppermute | solution.py:282
  20.3 1.0 %collective-permute-done.5 = bf16[32,4096]{1,0:T(8,128)(2,1)S(1)} collective-permute-done((bf16[32,4096]{1,0:T(8,128)(2,1)S(1)}, bf16[32,4096]{1,0:T(8,128)(2,1)S(1)}, u32[]{:S(2)}, u32[]{:S(2)}) %collective-permute-start.5) | collective-permute-done | bytes 262176 | tf_op jit(solution)/shard_map/ppermute | solution.py:282
  21.4 2.5 %collective-permute-start.6 = (bf16[16,4096]{1,0:T(8,128)(2,1)S(1)}, bf16[16,4096]{1,0:T(8,128)(2,1)S(1)}, u32[]{:S(2)}, u32[]{:S(2)}) collective-permute-start(bf16[16,4096]{1,0:T(8,128)(2,1)S(1)} %add_convert_fusion.3), channel_id=1, source_target_pairs={{0,4},{1,3},{2,6},{3,1},{4,0},{5,7},{6,2},{7,5},{8,12},{9,11},{10,... | collective-permute-start | bytes 393224 | tf_op jit(solution)/shard_map/ppermute | solution.py:282
  23.9 0.0 collective-permute-done.2
  23.9 2.9 %collective-permute-start.3 = (bf16[8,5248]{1,0:T(8,128)(2,1)S(1)}, bf16[8,5248]{1,0:T(8,128)(2,1)S(1)}, u32[]{:S(2)}, u32[]{:S(2)}) collective-permute-start(bf16[8,5248]{1,0:T(8,128)(2,1)S(1)} %add_convert_fusion.4), channel_id=1, source_target_pairs={{0,8},{1,9},{2,10},{3,11},{4,12},{5,13},{6,14},{7,15},{8,0},{9,1},... | collective-permute-start | bytes 251912 | tf_op jit(solution)/shard_map/ppermute | solution.py:282
  26.8 0.0 collective-permute-done.6
  26.9 4.0 %collective-permute-start.7 = (bf16[8,4096]{1,0:T(8,128)(2,1)S(1)}, bf16[8,4096]{1,0:T(8,128)(2,1)S(1)}, u32[]{:S(2)}, u32[]{:S(2)}) collective-permute-start(bf16[8,4096]{1,0:T(8,128)(2,1)S(1)} %add_convert_fusion.6), channel_id=1, source_target_pairs={{0,8},{1,9},{2,10},{3,11},{4,12},{5,13},{6,14},{7,15},{8,0},{9,1},... | collective-permute-start | bytes 196616 | tf_op jit(solution)/shard_map/ppermute | solution.py:282
  30.8 1.2 %collective-permute-done.3 = bf16[8,5248]{1,0:T(8,128)(2,1)S(1)} collective-permute-done((bf16[8,5248]{1,0:T(8,128)(2,1)S(1)}, bf16[8,5248]{1,0:T(8,128)(2,1)S(1)}, u32[]{:S(2)}, u32[]{:S(2)}) %collective-permute-start.3) | collective-permute-done | bytes 84000 | tf_op jit(solution)/shard_map/ppermute | solution.py:282
  32.1 0.1 convert_add_fusion
  32.1 0.1 slice_reduce_fusion
  32.2 0.1 slice_multiply_fusion.1
  32.3 0.1 fusion.8
  32.4 0.1 add_convert_fusion.8
  32.5 0.1 subtract_convert_fusion.1
  32.7 0.1 fusion.20
  32.7 0.2 fusion.14
  33.0 0.5 fusion.31
  33.5 0.2 fusion.6
  33.8 0.0 slice-start.3
  33.8 0.3 fusion
  34.2 0.5 collective-permute-start.9
  34.6 0.0 collective-permute-done.7
  34.6 0.1 multiply_bitcast_fusion
  34.7 0.1 subtract_convert_fusion
  34.9 0.5 fusion.32
  35.4 0.2 fusion.13
  35.6 0.2 fusion.7
  35.9 0.3 fusion.1
  36.3 2.6 %collective-permute-start.8 = (bf16[8,4096]{1,0:T(8,128)(2,1)S(1)}, bf16[8,4096]{1,0:T(8,128)(2,1)S(1)}, u32[]{:S(2)}, u32[]{:S(2)}) collective-permute-start(bf16[8,4096]{1,0:T(8,128)(2,1)S(1)} %bitcast.47), channel_id=1, source_target_pairs={{0,8},{1,9},{2,10},{3,11},{4,12},{5,13},{6,14},{7,15},{8,0},{9,1},... | collective-permute-start | bytes 196616 | tf_op jit(solution)/shard_map/ppermute | solution.py:282
  38.9 1.6 %collective-permute-done.9 = bf16[8,4096]{1,0:T(8,128)(2,1)S(1)} collective-permute-done((bf16[8,4096]{1,0:T(8,128)(2,1)S(1)}, bf16[8,4096]{1,0:T(8,128)(2,1)S(1)}, u32[]{:S(2)}, u32[]{:S(2)}) %collective-permute-start.9) | collective-permute-done | bytes 65568 | tf_op jit(solution)/shard_map/ppermute | solution.py:282
  40.5 0.1 collective-permute-start.11
  40.6 0.9 %collective-permute-done.8 = bf16[8,4096]{1,0:T(8,128)(2,1)S(1)} collective-permute-done((bf16[8,4096]{1,0:T(8,128)(2,1)S(1)}, bf16[8,4096]{1,0:T(8,128)(2,1)S(1)}, u32[]{:S(2)}, u32[]{:S(2)}) %collective-permute-start.8) | collective-permute-done | bytes 65568 | tf_op jit(solution)/shard_map/ppermute | solution.py:282
  41.5 3.3 %collective-permute-start.10 = (bf16[16,4096]{1,0:T(8,128)(2,1)S(1)}, bf16[16,4096]{1,0:T(8,128)(2,1)S(1)}, u32[]{:S(2)}, u32[]{:S(2)}) collective-permute-start(bf16[16,4096]{1,0:T(8,128)(2,1)S(1)} %pad_maximum_fusion.1), channel_id=1, source_target_pairs={{0,4},{1,3},{2,6},{3,1},{4,0},{5,7},{6,2},{7,5},{8,12},{9,11},{10,... | collective-permute-start | bytes 393224 | tf_op jit(solution)/shard_map/ppermute | solution.py:282
  44.8 1.1 %collective-permute-done.11 = bf16[16,4096]{1,0:T(8,128)(2,1)S(1)} collective-permute-done((bf16[16,4096]{1,0:T(8,128)(2,1)S(1)}, bf16[16,4096]{1,0:T(8,128)(2,1)S(1)}, u32[]{:S(2)}, u32[]{:S(2)}) %collective-permute-start.11) | collective-permute-done | bytes 131104 | tf_op jit(solution)/shard_map/ppermute | solution.py:282
  46.0 2.5 %collective-permute-start.14 = (bf16[32,4096]{1,0:T(8,128)(2,1)S(1)}, bf16[32,4096]{1,0:T(8,128)(2,1)S(1)}, u32[]{:S(2)}, u32[]{:S(2)}) collective-permute-start(bf16[32,4096]{1,0:T(8,128)(2,1)S(1)} %get-tuple-element.36), channel_id=1, source_target_pairs={{0,2},{1,5},{2,0},{3,7},{4,6},{5,1},{6,4},{7,3},{8,10},{9,13},{10,... | collective-permute-start | bytes 786440 | tf_op jit(solution)/shard_map/ppermute | solution.py:282
  48.5 0.7 %collective-permute-done.10 = bf16[16,4096]{1,0:T(8,128)(2,1)S(1)} collective-permute-done((bf16[16,4096]{1,0:T(8,128)(2,1)S(1)}, bf16[16,4096]{1,0:T(8,128)(2,1)S(1)}, u32[]{:S(2)}, u32[]{:S(2)}) %collective-permute-start.10) | collective-permute-done | bytes 131104 | tf_op jit(solution)/shard_map/ppermute | solution.py:282
  49.2 2.1 %collective-permute-start.12 = (bf16[32,4096]{1,0:T(8,128)(2,1)S(1)}, bf16[32,4096]{1,0:T(8,128)(2,1)S(1)}, u32[]{:S(2)}, u32[]{:S(2)}) collective-permute-start(bf16[32,4096]{1,0:T(8,128)(2,1)S(1)} %pad_maximum_fusion), channel_id=1, source_target_pairs={{0,2},{1,5},{2,0},{3,7},{4,6},{5,1},{6,4},{7,3},{8,10},{9,13},{10,... | collective-permute-start | bytes 786440 | tf_op jit(solution)/shard_map/ppermute | solution.py:282
  51.3 1.5 %collective-permute-done.14 = bf16[32,4096]{1,0:T(8,128)(2,1)S(1)} collective-permute-done((bf16[32,4096]{1,0:T(8,128)(2,1)S(1)}, bf16[32,4096]{1,0:T(8,128)(2,1)S(1)}, u32[]{:S(2)}, u32[]{:S(2)}) %collective-permute-start.14) | collective-permute-done | bytes 262176 | tf_op jit(solution)/shard_map/ppermute | solution.py:282
  52.9 0.1 collective-permute-start.15
  53.0 2.7 %collective-permute-done.12 = bf16[32,4096]{1,0:T(8,128)(2,1)S(1)} collective-permute-done((bf16[32,4096]{1,0:T(8,128)(2,1)S(1)}, bf16[32,4096]{1,0:T(8,128)(2,1)S(1)}, u32[]{:S(2)}, u32[]{:S(2)}) %collective-permute-start.12) | collective-permute-done | bytes 262176 | tf_op jit(solution)/shard_map/ppermute | solution.py:282
  55.7 0.1 collective-permute-start.13
  55.8 0.0 collective-permute-done.15.other_ref
  55.8 0.0 slice-done
  55.8 1.3 %shard_map.66.refs_0_ = f32[128,1024]{1,0:T(8,128)S(1)} custom-call(s32[1]{0:T(128)} %bitcast.me_ref, bf16[64,4096]{1,0:T(8,128)(2,1)S(1)} %constant_dynamic-update-slice_fusion.7.mine_ref, bf16[64,4096]{1,0:T(8,128)(2,1)S(1)} %collective-permute-done.15.other_ref, bf16[8192,1024]{1,0:T(8,128)(2,1)S(1)} %bitcast.38), custom_call_target="tpu_custom_call" | custom-call | flops 1073741824 | bytes 9699328 | tf_op jit(solution)/shard_map/pallas_call | solution.py:208
  57.1 0.5 collective-permute-done.13.other_ref
  57.7 2.0 %shard_map.67 = bf16[128,1024]{1,0:T(8,128)(2,1)} custom-call(s32[1]{0:T(128)} %bitcast.me_ref, bf16[64,4096]{1,0:T(8,128)(2,1)S(1)} %constant_dynamic-update-slice_fusion.5.mine_ref, bf16[64,4096]{1,0:T(8,128)(2,1)S(1)} %collective-permute-done.13.other_ref, bf16[8192,1024]{1,0:T(8,128)(2,1)S(1)} %bitcast.38, f32[128,1024]{1,0:T(8,128)S(1)} %shard_map.66.refs_0_), custom_call_target="tpu_custom_call" | custom-call | flops 1073741824 | bytes 9699328 | tf_op jit(solution)/shard_map/pallas_call | solution.py:208
  (35 shorter events, 0.6 us)
Async XLA Ops:
  7.7 2.3 %collective-permute-start = (bf16[64,5248]{1,0:T(8,128)(2,1)S(1)}, bf16[64,5248]{1,0:T(8,128)(2,1)S(1)}, u32[]{:S(2)}, u32[]{:S(2)}) collective-permute-start(bf16[64,5248]{1,0:T(8,128)(2,1)S(1)} %get-tuple-element.22), channel_id=1, source_target_pairs={{0,1},{1,0},{2,3},{3,2},{4,5},{5,4},{6,7},{7,6},{8,9},{9,8},{10,11... | collective-permute-start | bytes 2015240 | tf_op jit(solution)/shard_map/ppermute | solution.py:282
  8.2 6.6 %copy-start.1 = (bf16[8,256,4,128]{3,2,1,0:T(4,128)(2,1)S(1)}, bf16[8,256,4,128]{3,2,1,0:T(4,128)(2,1)}, u32[]{:S(2)}) copy-start(bf16[8,256,4,128]{3,2,1,0:T(4,128)(2,1)} %param.11) | copy-start | bytes 6291460
  8.2 47.6 %slice-start = ((s8[16777216]{0:T(1024)(128)(4,1)}), s8[4194304]{0:T(1024)(128)(4,1)S(1)}, s32[]{:S(2)}) async-start(s8[16777216]{0:T(1024)(128)(4,1)} %bitcast.37), calls=%async_computation | async-start | bytes 8388608
  9.5 4.8 %copy-start = (bf16[8,256,4,128]{3,2,1,0:T(4,128)(2,1)S(1)}, bf16[8,256,4,128]{3,2,1,0:T(4,128)(2,1)}, u32[]{:S(2)}) copy-start(bf16[8,256,4,128]{3,2,1,0:T(4,128)(2,1)} %param.10) | copy-start | bytes 6291460
  9.5 3.5 %collective-permute-start.4 = (bf16[64,4096]{1,0:T(8,128)(2,1)S(1)}, bf16[64,4096]{1,0:T(8,128)(2,1)S(1)}, u32[]{:S(2)}, u32[]{:S(2)}) collective-permute-start(bf16[64,4096]{1,0:T(8,128)(2,1)S(1)} %get-tuple-element.23), channel_id=1, source_target_pairs={{0,1},{1,0},{2,3},{3,2},{4,5},{5,4},{6,7},{7,6},{8,9},{9,8},{10,11... | collective-permute-start | bytes 1572872 | tf_op jit(solution)/shard_map/ppermute | solution.py:282
  10.0 45.8 %slice-start.1 = ((s8[16777216]{0:T(1024)(128)(4,1)}), s8[4194304]{0:T(1024)(128)(4,1)S(1)}, s32[]{:S(2)}) async-start(s8[16777216]{0:T(1024)(128)(4,1)} %bitcast.37), calls=%async_computation.1 | async-start | bytes 8388608
  10.0 8.1 %collective-permute-start.1 = (bf16[32,5248]{1,0:T(8,128)(2,1)S(1)}, bf16[32,5248]{1,0:T(8,128)(2,1)S(1)}, u32[]{:S(2)}, u32[]{:S(2)}) collective-permute-start(bf16[32,5248]{1,0:T(8,128)(2,1)S(1)} %add_convert_fusion), channel_id=1, source_target_pairs={{0,2},{1,5},{2,0},{3,7},{4,6},{5,1},{6,4},{7,3},{8,10},{9,13},{10,... | collective-permute-start | bytes 1007624 | tf_op jit(solution)/shard_map/ppermute | solution.py:282
  13.0 8.3 %collective-permute-start.5 = (bf16[32,4096]{1,0:T(8,128)(2,1)S(1)}, bf16[32,4096]{1,0:T(8,128)(2,1)S(1)}, u32[]{:S(2)}, u32[]{:S(2)}) collective-permute-start(bf16[32,4096]{1,0:T(8,128)(2,1)S(1)} %add_convert_fusion.1), channel_id=1, source_target_pairs={{0,2},{1,5},{2,0},{3,7},{4,6},{5,1},{6,4},{7,3},{8,10},{9,13},{10,... | collective-permute-start | bytes 786440 | tf_op jit(solution)/shard_map/ppermute | solution.py:282
  14.8 41.0 %slice-start.2 = ((s8[16777216]{0:T(1024)(128)(4,1)}), s8[4194304]{0:T(1024)(128)(4,1)S(1)}, s32[]{:S(2)}) async-start(s8[16777216]{0:T(1024)(128)(4,1)} %bitcast.37), calls=%async_computation.2 | async-start | bytes 8388608
  18.2 5.7 %collective-permute-start.2 = (bf16[16,5248]{1,0:T(8,128)(2,1)S(1)}, bf16[16,5248]{1,0:T(8,128)(2,1)S(1)}, u32[]{:S(2)}, u32[]{:S(2)}) collective-permute-start(bf16[16,5248]{1,0:T(8,128)(2,1)S(1)} %add_convert_fusion.2), channel_id=1, source_target_pairs={{0,4},{1,3},{2,6},{3,1},{4,0},{5,7},{6,2},{7,5},{8,12},{9,11},{10,... | collective-permute-start | bytes 503816 | tf_op jit(solution)/shard_map/ppermute | solution.py:282
  21.4 5.4 %collective-permute-start.6 = (bf16[16,4096]{1,0:T(8,128)(2,1)S(1)}, bf16[16,4096]{1,0:T(8,128)(2,1)S(1)}, u32[]{:S(2)}, u32[]{:S(2)}) collective-permute-start(bf16[16,4096]{1,0:T(8,128)(2,1)S(1)} %add_convert_fusion.3), channel_id=1, source_target_pairs={{0,4},{1,3},{2,6},{3,1},{4,0},{5,7},{6,2},{7,5},{8,12},{9,11},{10,... | collective-permute-start | bytes 393224 | tf_op jit(solution)/shard_map/ppermute | solution.py:282
  23.9 8.1 %collective-permute-start.3 = (bf16[8,5248]{1,0:T(8,128)(2,1)S(1)}, bf16[8,5248]{1,0:T(8,128)(2,1)S(1)}, u32[]{:S(2)}, u32[]{:S(2)}) collective-permute-start(bf16[8,5248]{1,0:T(8,128)(2,1)S(1)} %add_convert_fusion.4), channel_id=1, source_target_pairs={{0,8},{1,9},{2,10},{3,11},{4,12},{5,13},{6,14},{7,15},{8,0},{9,1},... | collective-permute-start | bytes 251912 | tf_op jit(solution)/shard_map/ppermute | solution.py:282
  26.9 7.8 %collective-permute-start.7 = (bf16[8,4096]{1,0:T(8,128)(2,1)S(1)}, bf16[8,4096]{1,0:T(8,128)(2,1)S(1)}, u32[]{:S(2)}, u32[]{:S(2)}) collective-permute-start(bf16[8,4096]{1,0:T(8,128)(2,1)S(1)} %add_convert_fusion.6), channel_id=1, source_target_pairs={{0,8},{1,9},{2,10},{3,11},{4,12},{5,13},{6,14},{7,15},{8,0},{9,1},... | collective-permute-start | bytes 196616 | tf_op jit(solution)/shard_map/ppermute | solution.py:282
  33.8 22.0 %slice-start.3 = ((s8[16777216]{0:T(1024)(128)(4,1)}), s8[4194304]{0:T(1024)(128)(4,1)S(1)}, s32[]{:S(2)}) async-start(s8[16777216]{0:T(1024)(128)(4,1)} %bitcast.37), calls=%async_computation.3 | async-start | bytes 8388608
  34.2 6.3 %collective-permute-start.9 = (bf16[8,4096]{1,0:T(8,128)(2,1)S(1)}, bf16[8,4096]{1,0:T(8,128)(2,1)S(1)}, u32[]{:S(2)}, u32[]{:S(2)}) collective-permute-start(bf16[8,4096]{1,0:T(8,128)(2,1)S(1)} %bitcast.51), channel_id=1, source_target_pairs={{0,8},{1,9},{2,10},{3,11},{4,12},{5,13},{6,14},{7,15},{8,0},{9,1},... | collective-permute-start | bytes 196616 | tf_op jit(solution)/shard_map/ppermute | solution.py:282
  36.3 5.2 %collective-permute-start.8 = (bf16[8,4096]{1,0:T(8,128)(2,1)S(1)}, bf16[8,4096]{1,0:T(8,128)(2,1)S(1)}, u32[]{:S(2)}, u32[]{:S(2)}) collective-permute-start(bf16[8,4096]{1,0:T(8,128)(2,1)S(1)} %bitcast.47), channel_id=1, source_target_pairs={{0,8},{1,9},{2,10},{3,11},{4,12},{5,13},{6,14},{7,15},{8,0},{9,1},... | collective-permute-start | bytes 196616 | tf_op jit(solution)/shard_map/ppermute | solution.py:282
  40.5 5.5 %collective-permute-start.11 = (bf16[16,4096]{1,0:T(8,128)(2,1)S(1)}, bf16[16,4096]{1,0:T(8,128)(2,1)S(1)}, u32[]{:S(2)}, u32[]{:S(2)}) collective-permute-start(bf16[16,4096]{1,0:T(8,128)(2,1)S(1)} %get-tuple-element.39), channel_id=1, source_target_pairs={{0,4},{1,3},{2,6},{3,1},{4,0},{5,7},{6,2},{7,5},{8,12},{9,11},{10,... | collective-permute-start | bytes 393224 | tf_op jit(solution)/shard_map/ppermute | solution.py:282
  41.5 7.7 %collective-permute-start.10 = (bf16[16,4096]{1,0:T(8,128)(2,1)S(1)}, bf16[16,4096]{1,0:T(8,128)(2,1)S(1)}, u32[]{:S(2)}, u32[]{:S(2)}) collective-permute-start(bf16[16,4096]{1,0:T(8,128)(2,1)S(1)} %pad_maximum_fusion.1), channel_id=1, source_target_pairs={{0,4},{1,3},{2,6},{3,1},{4,0},{5,7},{6,2},{7,5},{8,12},{9,11},{10,... | collective-permute-start | bytes 393224 | tf_op jit(solution)/shard_map/ppermute | solution.py:282
  46.0 6.9 %collective-permute-start.14 = (bf16[32,4096]{1,0:T(8,128)(2,1)S(1)}, bf16[32,4096]{1,0:T(8,128)(2,1)S(1)}, u32[]{:S(2)}, u32[]{:S(2)}) collective-permute-start(bf16[32,4096]{1,0:T(8,128)(2,1)S(1)} %get-tuple-element.36), channel_id=1, source_target_pairs={{0,2},{1,5},{2,0},{3,7},{4,6},{5,1},{6,4},{7,3},{8,10},{9,13},{10,... | collective-permute-start | bytes 786440 | tf_op jit(solution)/shard_map/ppermute | solution.py:282
  49.2 6.4 %collective-permute-start.12 = (bf16[32,4096]{1,0:T(8,128)(2,1)S(1)}, bf16[32,4096]{1,0:T(8,128)(2,1)S(1)}, u32[]{:S(2)}, u32[]{:S(2)}) collective-permute-start(bf16[32,4096]{1,0:T(8,128)(2,1)S(1)} %pad_maximum_fusion), channel_id=1, source_target_pairs={{0,2},{1,5},{2,0},{3,7},{4,6},{5,1},{6,4},{7,3},{8,10},{9,13},{10,... | collective-permute-start | bytes 786440 | tf_op jit(solution)/shard_map/ppermute | solution.py:282
  52.9 2.9 %collective-permute-start.15 = (bf16[64,4096]{1,0:T(8,128)(2,1)S(1)}, bf16[64,4096]{1,0:T(8,128)(2,1)S(1)}, u32[]{:S(2)}, u32[]{:S(2)}) collective-permute-start(bf16[64,4096]{1,0:T(8,128)(2,1)S(1)} %constant_dynamic-update-slice_fusion.7.mine_ref), channel_id=1, source_target_pairs={{0,1},{1,0},{2,3},{3,2},{4,5},{5,4},{6,7},{7,6},{8,9},{9,8},{10,11... | collective-permute-start | bytes 1572872 | tf_op jit(solution)/shard_map/ppermute | solution.py:282
  55.7 2.0 %collective-permute-start.13 = (bf16[64,4096]{1,0:T(8,128)(2,1)S(1)}, bf16[64,4096]{1,0:T(8,128)(2,1)S(1)}, u32[]{:S(2)}, u32[]{:S(2)}) collective-permute-start(bf16[64,4096]{1,0:T(8,128)(2,1)S(1)} %constant_dynamic-update-slice_fusion.5.mine_ref), channel_id=1, source_target_pairs={{0,1},{1,0},{2,3},{3,2},{4,5},{5,4},{6,7},{7,6},{8,9},{9,8},{10,11... | collective-permute-start | bytes 1572872 | tf_op jit(solution)/shard_map/ppermute | solution.py:282

commit v6 on v5

--- a/solution.py
+++ b/solution.py
@@ -31,7 +31,15 @@
         bit *= 2
     swapped = bits[1:2] + bits[:1] + bits[2:]
     rotated = bits[1:] + bits[:1]
-    return [{"i": bits, "s": swapped, "r": rotated}[name] for name in ORDERS[phase]]
+    return [{"i": bits, "s": swapped, "r": rotated, "z": bits[:1] + bits[2:] + bits[1:2]}[name] for name in ORDERS[phase]]
+
+
+def parity(index, count):
+    result, shift = index, 1
+    while 1 << shift < count:
+        result = result ^ (index >> shift)
+        shift += 1
+    return result & 1
 
 
 def place(index, count, phase, order):
@@ -44,11 +52,10 @@
 
 def places(me, count, phase):
     own = [place(me, count, phase, order) for order in range(2)]
-    core = me & 1
     result = []
     for block in range(count):
-        order = block & 1
-        half = jnp.bitwise_xor(core, order) * (count // 2)
+        order = parity(block, count)
+        half = jnp.bitwise_xor(parity(me, count), order) * (count // 2)
         result.append(half + jnp.bitwise_xor(own[order], place(block, count, phase, order)))
     return result
 
@@ -276,9 +283,10 @@
 
 def swap(value, count, phase=None, stage=None):
     orders = None if phase is None else stage_bits(count, phase)
-    partners = [
-        (i, i ^ (1 if phase is None else orders[i & 1][stage])) for i in range(count)
-    ]
+    partners = []
+    for i in range(count):
+        mask = 1 if phase is None else orders[parity(i, count)][stage] ^ 1
+        partners.append((i, i ^ mask))
     return lax.ppermute(value, "gx", partners)
 
 

time: 59.9 us -> 58.8 us (0.982)
  waiting for transfers between devices: 14.4 us -> 11.9 us
  starting transfers between devices: 27.5 us -> 29.1 us
    ppermute x16, waiting for transfers between devices: 14.4 us -> 11.9 us  [swap(): return lax.ppermute(value, 'gx', partners)]
    ppermute x16, starting transfers between devices: 27.5 us -> 29.1 us  [swap(): return lax.ppermute(value, 'gx', partners)]
  transfers between devices with their start and end apart: 16 -> 16, of which waited for: 11 -> 10; matrix products, arithmetic and copies ran while one was open for 8% -> 9% of each run, Pallas kernels for 4% -> 4%
where the time goes in v6:
time: 58.8 us; the launch traced here: 58.7 us
  starting transfers between devices  29.1 us (49%)
  Pallas kernels  12.3 us (21%)
  waiting for transfers between devices  11.9 us (20%)
  matrix products  2.09 us (4%)
  other arithmetic  1.68 us (3%)
  local copies, waits for them, and re-layouts  1.27 us (2%)
    ppermute x16, starting transfers between devices, swap(): return lax.ppermute(value, 'gx', partners)  29.1 us
    ppermute x16, waiting for transfers between devices, swap(): return lax.ppermute(value, 'gx', partners)  11.9 us
    pallas_call x2, Pallas kernels, call(): pl.pallas_call(kernel, in_specs=in_specs, out_specs=[in_vmem] * len(out_s...  8.96 us
    pallas_call x2, Pallas kernels, output_part(): pl.pallas_call(functools.partial(output_kernel, count, rows, start), in_s...  3.34 us
  transfers between devices with their start and end apart: 16, of which 10 were waited for; matrix products, arithmetic and copies ran while one was open for 9% of the time, Pallas kernels for 4%

profile of v6, /device:TPU:0, one launch (start us, length us, event | category | flops | bytes accessed | tf_op | source)
XLA Modules:
  0.0 58.7 jit_solution(5854592720943129017)
XLA Ops:
  0.0 7.7 %shard_map.64 = (bf16[64,5248]{1,0:T(8,128)(2,1)S(1)}, f32[64,5248]{1,0:T(8,128)S(1)}, bf16[128,1024]{1,0:T(8,128)(2,1)S(1)}, bf16[4,1024,1024]{2,1,0:T(8,128)(2,1)S(1)}) custom-call(s32[1]{0:T(128)} %bitcast.me_ref, bf16[128,1024]{1,0:T(8,128)(2,1)} %acts_ref.1, bf16[1024]{0:T(1024)(128)(2,1)} %gain_ref.1, bf16[1024,9216]{1,0:T(8,128)(2,1)} %w_ref.1), custom_call_target="tpu_custom_call" | custom-call | flops 1342177280 | bytes 12500992 | tf_op jit(solution)/shard_map/pallas_call | solution.py:139
  7.7 0.5 collective-permute-start
  8.2 1.3 %shard_map.65 = (bf16[64,4096]{1,0:T(8,128)(2,1)S(1)}, f32[64,4096]{1,0:T(8,128)S(1)}) custom-call(bf16[128,1024]{1,0:T(8,128)(2,1)S(1)} %get-tuple-element.18.scaled, bf16[4,1024,1024]{2,1,0:T(8,128)(2,1)S(1)} %get-tuple-element.19.weights), custom_call_target="tpu_custom_call" | custom-call | flops 1073741824 | bytes 9961472 | tf_op jit(solution)/shard_map/pallas_call | solution.py:139
  9.5 0.0 copy-start
  9.5 0.1 collective-permute-start.4
  9.7 0.3 collective-permute-done
  10.0 0.1 add_convert_fusion
  10.0 2.7 %collective-permute-start.1 = (bf16[32,5248]{1,0:T(8,128)(2,1)S(1)}, bf16[32,5248]{1,0:T(8,128)(2,1)S(1)}, u32[]{:S(2)}, u32[]{:S(2)}) collective-permute-start(bf16[32,5248]{1,0:T(8,128)(2,1)S(1)} %add_convert_fusion), channel_id=1, source_target_pairs={{0,3},{1,4},{2,7},{3,0},{4,1},{5,6},{6,5},{7,2},{8,13},{9,10},{10,... | collective-permute-start | bytes 1007624 | tf_op jit(solution)/shard_map/ppermute | solution.py:290
  12.7 0.0 collective-permute-done.4
  12.7 0.1 add_convert_fusion.1
  12.8 1.5 %collective-permute-start.5 = (bf16[32,4096]{1,0:T(8,128)(2,1)S(1)}, bf16[32,4096]{1,0:T(8,128)(2,1)S(1)}, u32[]{:S(2)}, u32[]{:S(2)}) collective-permute-start(bf16[32,4096]{1,0:T(8,128)(2,1)S(1)} %add_convert_fusion.1), channel_id=1, source_target_pairs={{0,3},{1,4},{2,7},{3,0},{4,1},{5,6},{6,5},{7,2},{8,13},{9,10},{10,... | collective-permute-start | bytes 786440 | tf_op jit(solution)/shard_map/ppermute | solution.py:290
  14.2 0.5 copy.9
  14.8 0.0 slice-start.2
  14.8 0.5 copy.10
  15.3 2.3 %collective-permute-done.1 = bf16[32,5248]{1,0:T(8,128)(2,1)S(1)} collective-permute-done((bf16[32,5248]{1,0:T(8,128)(2,1)S(1)}, bf16[32,5248]{1,0:T(8,128)(2,1)S(1)}, u32[]{:S(2)}, u32[]{:S(2)}) %collective-permute-start.1) | collective-permute-done | bytes 335904 | tf_op jit(solution)/shard_map/ppermute | solution.py:290
  17.6 0.1 add_convert_fusion.2
  17.6 2.2 %collective-permute-start.2 = (bf16[16,5248]{1,0:T(8,128)(2,1)S(1)}, bf16[16,5248]{1,0:T(8,128)(2,1)S(1)}, u32[]{:S(2)}, u32[]{:S(2)}) collective-permute-start(bf16[16,5248]{1,0:T(8,128)(2,1)S(1)} %add_convert_fusion.2), channel_id=1, source_target_pairs={{0,5},{1,2},{2,1},{3,6},{4,7},{5,0},{6,3},{7,4},{8,11},{9,12},{10,... | collective-permute-start | bytes 503816 | tf_op jit(solution)/shard_map/ppermute | solution.py:290
  19.8 0.6 collective-permute-done.5
  20.4 1.9 %collective-permute-start.6 = (bf16[16,4096]{1,0:T(8,128)(2,1)S(1)}, bf16[16,4096]{1,0:T(8,128)(2,1)S(1)}, u32[]{:S(2)}, u32[]{:S(2)}) collective-permute-start(bf16[16,4096]{1,0:T(8,128)(2,1)S(1)} %add_convert_fusion.3), channel_id=1, source_target_pairs={{0,5},{1,2},{2,1},{3,6},{4,7},{5,0},{6,3},{7,4},{8,11},{9,12},{10,... | collective-permute-start | bytes 393224 | tf_op jit(solution)/shard_map/ppermute | solution.py:290
  22.3 0.5 collective-permute-done.2
  22.9 2.8 %collective-permute-start.3 = (bf16[8,5248]{1,0:T(8,128)(2,1)S(1)}, bf16[8,5248]{1,0:T(8,128)(2,1)S(1)}, u32[]{:S(2)}, u32[]{:S(2)}) collective-permute-start(bf16[8,5248]{1,0:T(8,128)(2,1)S(1)} %add_convert_fusion.4), channel_id=1, source_target_pairs={{0,9},{1,8},{2,11},{3,10},{4,13},{5,12},{6,15},{7,14},{8,1},{9,0},... | collective-permute-start | bytes 251912 | tf_op jit(solution)/shard_map/ppermute | solution.py:290
  25.7 0.0 collective-permute-done.6
  25.8 2.0 %collective-permute-start.7 = (bf16[8,4096]{1,0:T(8,128)(2,1)S(1)}, bf16[8,4096]{1,0:T(8,128)(2,1)S(1)}, u32[]{:S(2)}, u32[]{:S(2)}) collective-permute-start(bf16[8,4096]{1,0:T(8,128)(2,1)S(1)} %add_convert_fusion.6), channel_id=1, source_target_pairs={{0,9},{1,8},{2,11},{3,10},{4,13},{5,12},{6,15},{7,14},{8,1},{9,0},... | collective-permute-start | bytes 196616 | tf_op jit(solution)/shard_map/ppermute | solution.py:290
  27.8 2.4 %collective-permute-done.3 = bf16[8,5248]{1,0:T(8,128)(2,1)S(1)} collective-permute-done((bf16[8,5248]{1,0:T(8,128)(2,1)S(1)}, bf16[8,5248]{1,0:T(8,128)(2,1)S(1)}, u32[]{:S(2)}, u32[]{:S(2)}) %collective-permute-start.3) | collective-permute-done | bytes 84000 | tf_op jit(solution)/shard_map/ppermute | solution.py:290
  30.2 0.1 convert_add_fusion
  30.2 0.1 slice_reduce_fusion
  30.4 0.1 slice_multiply_fusion.1
  30.4 0.1 fusion.8
  30.6 0.1 add_convert_fusion.8
  30.6 0.1 subtract_convert_fusion.1
  30.8 0.1 fusion.20
  30.9 0.2 fusion.14
  31.1 0.5 fusion.31
  31.6 0.2 fusion.6
  31.9 0.0 slice-start.3
  31.9 0.3 fusion
  32.3 0.8 %collective-permute-start.9 = (bf16[8,4096]{1,0:T(8,128)(2,1)S(1)}, bf16[8,4096]{1,0:T(8,128)(2,1)S(1)}, u32[]{:S(2)}, u32[]{:S(2)}) collective-permute-start(bf16[8,4096]{1,0:T(8,128)(2,1)S(1)} %bitcast.51), channel_id=1, source_target_pairs={{0,9},{1,8},{2,11},{3,10},{4,13},{5,12},{6,15},{7,14},{8,1},{9,0},... | collective-permute-start | bytes 196616 | tf_op jit(solution)/shard_map/ppermute | solution.py:290
  33.1 0.0 collective-permute-done.7
  33.1 0.1 multiply_bitcast_fusion
  33.2 0.1 subtract_convert_fusion
  33.3 0.5 fusion.32
  33.8 0.2 fusion.13
  34.1 0.2 fusion.7
  34.3 0.3 fusion.1
  34.7 2.0 %collective-permute-start.8 = (bf16[8,4096]{1,0:T(8,128)(2,1)S(1)}, bf16[8,4096]{1,0:T(8,128)(2,1)S(1)}, u32[]{:S(2)}, u32[]{:S(2)}) collective-permute-start(bf16[8,4096]{1,0:T(8,128)(2,1)S(1)} %bitcast.47), channel_id=1, source_target_pairs={{0,9},{1,8},{2,11},{3,10},{4,13},{5,12},{6,15},{7,14},{8,1},{9,0},... | collective-permute-start | bytes 196616 | tf_op jit(solution)/shard_map/ppermute | solution.py:290
  36.7 0.3 collective-permute-done.9
  37.0 3.3 %collective-permute-start.11 = (bf16[16,4096]{1,0:T(8,128)(2,1)S(1)}, bf16[16,4096]{1,0:T(8,128)(2,1)S(1)}, u32[]{:S(2)}, u32[]{:S(2)}) collective-permute-start(bf16[16,4096]{1,0:T(8,128)(2,1)S(1)} %get-tuple-element.39), channel_id=1, source_target_pairs={{0,5},{1,2},{2,1},{3,6},{4,7},{5,0},{6,3},{7,4},{8,11},{9,12},{10,... | collective-permute-start | bytes 393224 | tf_op jit(solution)/shard_map/ppermute | solution.py:290
  40.3 1.2 %collective-permute-done.8 = bf16[8,4096]{1,0:T(8,128)(2,1)S(1)} collective-permute-done((bf16[8,4096]{1,0:T(8,128)(2,1)S(1)}, bf16[8,4096]{1,0:T(8,128)(2,1)S(1)}, u32[]{:S(2)}, u32[]{:S(2)}) %collective-permute-start.8) | collective-permute-done | bytes 65568 | tf_op jit(solution)/shard_map/ppermute | solution.py:290
  41.5 3.0 %collective-permute-start.10 = (bf16[16,4096]{1,0:T(8,128)(2,1)S(1)}, bf16[16,4096]{1,0:T(8,128)(2,1)S(1)}, u32[]{:S(2)}, u32[]{:S(2)}) collective-permute-start(bf16[16,4096]{1,0:T(8,128)(2,1)S(1)} %pad_maximum_fusion.1), channel_id=1, source_target_pairs={{0,5},{1,2},{2,1},{3,6},{4,7},{5,0},{6,3},{7,4},{8,11},{9,12},{10,... | collective-permute-start | bytes 393224 | tf_op jit(solution)/shard_map/ppermute | solution.py:290
  44.5 0.0 collective-permute-done.11
  44.5 2.9 %collective-permute-start.14 = (bf16[32,4096]{1,0:T(8,128)(2,1)S(1)}, bf16[32,4096]{1,0:T(8,128)(2,1)S(1)}, u32[]{:S(2)}, u32[]{:S(2)}) collective-permute-start(bf16[32,4096]{1,0:T(8,128)(2,1)S(1)} %get-tuple-element.36), channel_id=1, source_target_pairs={{0,3},{1,4},{2,7},{3,0},{4,1},{5,6},{6,5},{7,2},{8,13},{9,10},{10,... | collective-permute-start | bytes 786440 | tf_op jit(solution)/shard_map/ppermute | solution.py:290
  47.4 0.0 collective-permute-done.10
  47.5 1.6 %collective-permute-start.12 = (bf16[32,4096]{1,0:T(8,128)(2,1)S(1)}, bf16[32,4096]{1,0:T(8,128)(2,1)S(1)}, u32[]{:S(2)}, u32[]{:S(2)}) collective-permute-start(bf16[32,4096]{1,0:T(8,128)(2,1)S(1)} %pad_maximum_fusion), channel_id=1, source_target_pairs={{0,3},{1,4},{2,7},{3,0},{4,1},{5,6},{6,5},{7,2},{8,13},{9,10},{10,... | collective-permute-start | bytes 786440 | tf_op jit(solution)/shard_map/ppermute | solution.py:290
  49.1 2.4 %collective-permute-done.14 = bf16[32,4096]{1,0:T(8,128)(2,1)S(1)} collective-permute-done((bf16[32,4096]{1,0:T(8,128)(2,1)S(1)}, bf16[32,4096]{1,0:T(8,128)(2,1)S(1)}, u32[]{:S(2)}, u32[]{:S(2)}) %collective-permute-start.14) | collective-permute-done | bytes 262176 | tf_op jit(solution)/shard_map/ppermute | solution.py:290
  51.5 1.1 %collective-permute-start.15 = (bf16[64,4096]{1,0:T(8,128)(2,1)S(1)}, bf16[64,4096]{1,0:T(8,128)(2,1)S(1)}, u32[]{:S(2)}, u32[]{:S(2)}) collective-permute-start(bf16[64,4096]{1,0:T(8,128)(2,1)S(1)} %constant_dynamic-update-slice_fusion.7.mine_ref), channel_id=1, source_target_pairs={{0,1},{1,0},{2,3},{3,2},{4,5},{5,4},{6,7},{7,6},{8,9},{9,8},{10,11... | collective-permute-start | bytes 1572872 | tf_op jit(solution)/shard_map/ppermute | solution.py:290
  52.6 1.7 %collective-permute-done.12 = bf16[32,4096]{1,0:T(8,128)(2,1)S(1)} collective-permute-done((bf16[32,4096]{1,0:T(8,128)(2,1)S(1)}, bf16[32,4096]{1,0:T(8,128)(2,1)S(1)}, u32[]{:S(2)}, u32[]{:S(2)}) %collective-permute-start.12) | collective-permute-done | bytes 262176 | tf_op jit(solution)/shard_map/ppermute | solution.py:290
  54.3 0.8 %collective-permute-start.13 = (bf16[64,4096]{1,0:T(8,128)(2,1)S(1)}, bf16[64,4096]{1,0:T(8,128)(2,1)S(1)}, u32[]{:S(2)}, u32[]{:S(2)}) collective-permute-start(bf16[64,4096]{1,0:T(8,128)(2,1)S(1)} %constant_dynamic-update-slice_fusion.5.mine_ref), channel_id=1, source_target_pairs={{0,1},{1,0},{2,3},{3,2},{4,5},{5,4},{6,7},{7,6},{8,9},{9,8},{10,11... | collective-permute-start | bytes 1572872 | tf_op jit(solution)/shard_map/ppermute | solution.py:290
  55.1 0.0 collective-permute-done.15.other_ref
  55.1 0.0 slice-done.1
  55.1 0.0 slice-done.2
  55.1 0.0 slice-done.3
  55.1 1.3 %shard_map.66.refs_0_ = f32[128,1024]{1,0:T(8,128)S(1)} custom-call(s32[1]{0:T(128)} %bitcast.me_ref, bf16[64,4096]{1,0:T(8,128)(2,1)S(1)} %constant_dynamic-update-slice_fusion.7.mine_ref, bf16[64,4096]{1,0:T(8,128)(2,1)S(1)} %collective-permute-done.15.other_ref, bf16[8192,1024]{1,0:T(8,128)(2,1)S(1)} %bitcast.38), custom_call_target="tpu_custom_call" | custom-call | flops 1073741824 | bytes 9699328 | tf_op jit(solution)/shard_map/pallas_call | solution.py:215
  56.5 0.2 collective-permute-done.13.other_ref
  56.6 2.0 %shard_map.67 = bf16[128,1024]{1,0:T(8,128)(2,1)} custom-call(s32[1]{0:T(128)} %bitcast.me_ref, bf16[64,4096]{1,0:T(8,128)(2,1)S(1)} %constant_dynamic-update-slice_fusion.5.mine_ref, bf16[64,4096]{1,0:T(8,128)(2,1)S(1)} %collective-permute-done.13.other_ref, bf16[8192,1024]{1,0:T(8,128)(2,1)S(1)} %bitcast.38, f32[128,1024]{1,0:T(8,128)S(1)} %shard_map.66.refs_0_), custom_call_target="tpu_custom_call" | custom-call | flops 1073741824 | bytes 9699328 | tf_op jit(solution)/shard_map/pallas_call | solution.py:215
  (35 shorter events, 0.6 us)
Async XLA Ops:
  7.7 2.3 %collective-permute-start = (bf16[64,5248]{1,0:T(8,128)(2,1)S(1)}, bf16[64,5248]{1,0:T(8,128)(2,1)S(1)}, u32[]{:S(2)}, u32[]{:S(2)}) collective-permute-start(bf16[64,5248]{1,0:T(8,128)(2,1)S(1)} %get-tuple-element.22), channel_id=1, source_target_pairs={{0,1},{1,0},{2,3},{3,2},{4,5},{5,4},{6,7},{7,6},{8,9},{9,8},{10,11... | collective-permute-start | bytes 2015240 | tf_op jit(solution)/shard_map/ppermute | solution.py:290
  8.2 6.5 %copy-start.1 = (bf16[8,256,4,128]{3,2,1,0:T(4,128)(2,1)S(1)}, bf16[8,256,4,128]{3,2,1,0:T(4,128)(2,1)}, u32[]{:S(2)}) copy-start(bf16[8,256,4,128]{3,2,1,0:T(4,128)(2,1)} %param.11) | copy-start | bytes 6291460
  8.2 46.9 %slice-start = ((s8[16777216]{0:T(1024)(128)(4,1)}), s8[4194304]{0:T(1024)(128)(4,1)S(1)}, s32[]{:S(2)}) async-start(s8[16777216]{0:T(1024)(128)(4,1)} %bitcast.37), calls=%async_computation | async-start | bytes 8388608
  9.5 4.7 %copy-start = (bf16[8,256,4,128]{3,2,1,0:T(4,128)(2,1)S(1)}, bf16[8,256,4,128]{3,2,1,0:T(4,128)(2,1)}, u32[]{:S(2)}) copy-start(bf16[8,256,4,128]{3,2,1,0:T(4,128)(2,1)} %param.10) | copy-start | bytes 6291460
  9.5 3.2 %collective-permute-start.4 = (bf16[64,4096]{1,0:T(8,128)(2,1)S(1)}, bf16[64,4096]{1,0:T(8,128)(2,1)S(1)}, u32[]{:S(2)}, u32[]{:S(2)}) collective-permute-start(bf16[64,4096]{1,0:T(8,128)(2,1)S(1)} %get-tuple-element.23), channel_id=1, source_target_pairs={{0,1},{1,0},{2,3},{3,2},{4,5},{5,4},{6,7},{7,6},{8,9},{9,8},{10,11... | collective-permute-start | bytes 1572872 | tf_op jit(solution)/shard_map/ppermute | solution.py:290
  10.0 45.2 %slice-start.1 = ((s8[16777216]{0:T(1024)(128)(4,1)}), s8[4194304]{0:T(1024)(128)(4,1)S(1)}, s32[]{:S(2)}) async-start(s8[16777216]{0:T(1024)(128)(4,1)} %bitcast.37), calls=%async_computation.1 | async-start | bytes 8388608
  10.0 7.5 %collective-permute-start.1 = (bf16[32,5248]{1,0:T(8,128)(2,1)S(1)}, bf16[32,5248]{1,0:T(8,128)(2,1)S(1)}, u32[]{:S(2)}, u32[]{:S(2)}) collective-permute-start(bf16[32,5248]{1,0:T(8,128)(2,1)S(1)} %add_convert_fusion), channel_id=1, source_target_pairs={{0,3},{1,4},{2,7},{3,0},{4,1},{5,6},{6,5},{7,2},{8,13},{9,10},{10,... | collective-permute-start | bytes 1007624 | tf_op jit(solution)/shard_map/ppermute | solution.py:290
  12.8 7.6 %collective-permute-start.5 = (bf16[32,4096]{1,0:T(8,128)(2,1)S(1)}, bf16[32,4096]{1,0:T(8,128)(2,1)S(1)}, u32[]{:S(2)}, u32[]{:S(2)}) collective-permute-start(bf16[32,4096]{1,0:T(8,128)(2,1)S(1)} %add_convert_fusion.1), channel_id=1, source_target_pairs={{0,3},{1,4},{2,7},{3,0},{4,1},{5,6},{6,5},{7,2},{8,13},{9,10},{10,... | collective-permute-start | bytes 786440 | tf_op jit(solution)/shard_map/ppermute | solution.py:290
  14.8 40.4 %slice-start.2 = ((s8[16777216]{0:T(1024)(128)(4,1)}), s8[4194304]{0:T(1024)(128)(4,1)S(1)}, s32[]{:S(2)}) async-start(s8[16777216]{0:T(1024)(128)(4,1)} %bitcast.37), calls=%async_computation.2 | async-start | bytes 8388608
  17.6 5.2 %collective-permute-start.2 = (bf16[16,5248]{1,0:T(8,128)(2,1)S(1)}, bf16[16,5248]{1,0:T(8,128)(2,1)S(1)}, u32[]{:S(2)}, u32[]{:S(2)}) collective-permute-start(bf16[16,5248]{1,0:T(8,128)(2,1)S(1)} %add_convert_fusion.2), channel_id=1, source_target_pairs={{0,5},{1,2},{2,1},{3,6},{4,7},{5,0},{6,3},{7,4},{8,11},{9,12},{10,... | collective-permute-start | bytes 503816 | tf_op jit(solution)/shard_map/ppermute | solution.py:290
  20.4 5.3 %collective-permute-start.6 = (bf16[16,4096]{1,0:T(8,128)(2,1)S(1)}, bf16[16,4096]{1,0:T(8,128)(2,1)S(1)}, u32[]{:S(2)}, u32[]{:S(2)}) collective-permute-start(bf16[16,4096]{1,0:T(8,128)(2,1)S(1)} %add_convert_fusion.3), channel_id=1, source_target_pairs={{0,5},{1,2},{2,1},{3,6},{4,7},{5,0},{6,3},{7,4},{8,11},{9,12},{10,... | collective-permute-start | bytes 393224 | tf_op jit(solution)/shard_map/ppermute | solution.py:290
  22.9 7.3 %collective-permute-start.3 = (bf16[8,5248]{1,0:T(8,128)(2,1)S(1)}, bf16[8,5248]{1,0:T(8,128)(2,1)S(1)}, u32[]{:S(2)}, u32[]{:S(2)}) collective-permute-start(bf16[8,5248]{1,0:T(8,128)(2,1)S(1)} %add_convert_fusion.4), channel_id=1, source_target_pairs={{0,9},{1,8},{2,11},{3,10},{4,13},{5,12},{6,15},{7,14},{8,1},{9,0},... | collective-permute-start | bytes 251912 | tf_op jit(solution)/shard_map/ppermute | solution.py:290
  25.8 7.3 %collective-permute-start.7 = (bf16[8,4096]{1,0:T(8,128)(2,1)S(1)}, bf16[8,4096]{1,0:T(8,128)(2,1)S(1)}, u32[]{:S(2)}, u32[]{:S(2)}) collective-permute-start(bf16[8,4096]{1,0:T(8,128)(2,1)S(1)} %add_convert_fusion.6), channel_id=1, source_target_pairs={{0,9},{1,8},{2,11},{3,10},{4,13},{5,12},{6,15},{7,14},{8,1},{9,0},... | collective-permute-start | bytes 196616 | tf_op jit(solution)/shard_map/ppermute | solution.py:290
  31.9 23.2 %slice-start.3 = ((s8[16777216]{0:T(1024)(128)(4,1)}), s8[4194304]{0:T(1024)(128)(4,1)S(1)}, s32[]{:S(2)}) async-start(s8[16777216]{0:T(1024)(128)(4,1)} %bitcast.37), calls=%async_computation.3 | async-start | bytes 8388608
  32.3 4.7 %collective-permute-start.9 = (bf16[8,4096]{1,0:T(8,128)(2,1)S(1)}, bf16[8,4096]{1,0:T(8,128)(2,1)S(1)}, u32[]{:S(2)}, u32[]{:S(2)}) collective-permute-start(bf16[8,4096]{1,0:T(8,128)(2,1)S(1)} %bitcast.51), channel_id=1, source_target_pairs={{0,9},{1,8},{2,11},{3,10},{4,13},{5,12},{6,15},{7,14},{8,1},{9,0},... | collective-permute-start | bytes 196616 | tf_op jit(solution)/shard_map/ppermute | solution.py:290
  34.7 6.7 %collective-permute-start.8 = (bf16[8,4096]{1,0:T(8,128)(2,1)S(1)}, bf16[8,4096]{1,0:T(8,128)(2,1)S(1)}, u32[]{:S(2)}, u32[]{:S(2)}) collective-permute-start(bf16[8,4096]{1,0:T(8,128)(2,1)S(1)} %bitcast.47), channel_id=1, source_target_pairs={{0,9},{1,8},{2,11},{3,10},{4,13},{5,12},{6,15},{7,14},{8,1},{9,0},... | collective-permute-start | bytes 196616 | tf_op jit(solution)/shard_map/ppermute | solution.py:290
  37.0 7.5 %collective-permute-start.11 = (bf16[16,4096]{1,0:T(8,128)(2,1)S(1)}, bf16[16,4096]{1,0:T(8,128)(2,1)S(1)}, u32[]{:S(2)}, u32[]{:S(2)}) collective-permute-start(bf16[16,4096]{1,0:T(8,128)(2,1)S(1)} %get-tuple-element.39), channel_id=1, source_target_pairs={{0,5},{1,2},{2,1},{3,6},{4,7},{5,0},{6,3},{7,4},{8,11},{9,12},{10,... | collective-permute-start | bytes 393224 | tf_op jit(solution)/shard_map/ppermute | solution.py:290
  41.5 6.0 %collective-permute-start.10 = (bf16[16,4096]{1,0:T(8,128)(2,1)S(1)}, bf16[16,4096]{1,0:T(8,128)(2,1)S(1)}, u32[]{:S(2)}, u32[]{:S(2)}) collective-permute-start(bf16[16,4096]{1,0:T(8,128)(2,1)S(1)} %pad_maximum_fusion.1), channel_id=1, source_target_pairs={{0,5},{1,2},{2,1},{3,6},{4,7},{5,0},{6,3},{7,4},{8,11},{9,12},{10,... | collective-permute-start | bytes 393224 | tf_op jit(solution)/shard_map/ppermute | solution.py:290
  44.5 7.0 %collective-permute-start.14 = (bf16[32,4096]{1,0:T(8,128)(2,1)S(1)}, bf16[32,4096]{1,0:T(8,128)(2,1)S(1)}, u32[]{:S(2)}, u32[]{:S(2)}) collective-permute-start(bf16[32,4096]{1,0:T(8,128)(2,1)S(1)} %get-tuple-element.36), channel_id=1, source_target_pairs={{0,3},{1,4},{2,7},{3,0},{4,1},{5,6},{6,5},{7,2},{8,13},{9,10},{10,... | collective-permute-start | bytes 786440 | tf_op jit(solution)/shard_map/ppermute | solution.py:290
  47.5 6.8 %collective-permute-start.12 = (bf16[32,4096]{1,0:T(8,128)(2,1)S(1)}, bf16[32,4096]{1,0:T(8,128)(2,1)S(1)}, u32[]{:S(2)}, u32[]{:S(2)}) collective-permute-start(bf16[32,4096]{1,0:T(8,128)(2,1)S(1)} %pad_maximum_fusion), channel_id=1, source_target_pairs={{0,3},{1,4},{2,7},{3,0},{4,1},{5,6},{6,5},{7,2},{8,13},{9,10},{10,... | collective-permute-start | bytes 786440 | tf_op jit(solution)/shard_map/ppermute | solution.py:290
  51.5 3.6 %collective-permute-start.15 = (bf16[64,4096]{1,0:T(8,128)(2,1)S(1)}, bf16[64,4096]{1,0:T(8,128)(2,1)S(1)}, u32[]{:S(2)}, u32[]{:S(2)}) collective-permute-start(bf16[64,4096]{1,0:T(8,128)(2,1)S(1)} %constant_dynamic-update-slice_fusion.7.mine_ref), channel_id=1, source_target_pairs={{0,1},{1,0},{2,3},{3,2},{4,5},{5,4},{6,7},{7,6},{8,9},{9,8},{10,11... | collective-permute-start | bytes 1572872 | tf_op jit(solution)/shard_map/ppermute | solution.py:290
  54.3 2.3 %collective-permute-start.13 = (bf16[64,4096]{1,0:T(8,128)(2,1)S(1)}, bf16[64,4096]{1,0:T(8,128)(2,1)S(1)}, u32[]{:S(2)}, u32[]{:S(2)}) collective-permute-start(bf16[64,4096]{1,0:T(8,128)(2,1)S(1)} %constant_dynamic-update-slice_fusion.5.mine_ref), channel_id=1, source_target_pairs={{0,1},{1,0},{2,3},{3,2},{4,5},{5,4},{6,7},{7,6},{8,9},{9,8},{10,11... | collective-permute-start | bytes 1572872 | tf_op jit(solution)/shard_map/ppermute | solution.py:290

commit v7 on v6

--- a/solution.py
+++ b/solution.py
@@ -17,10 +17,11 @@
 QKVW = QUERY_WIDTH + 2 * KEY_VALUE_HEADS * HEAD_SIZE
 TILE = 1024
 COLUMNS = 256
-ORDERS = ("is", "is")
 LANES = 128
 MIB = 1024 * 1024
 CHUNKS = ((2, 4), (0, 2))
+ORDERS = ("ir", "is", "si")
+GATHER = len(CHUNKS)
 
 
 def stage_bits(count, phase):
@@ -53,9 +54,10 @@
 def places(me, count, phase):
     own = [place(me, count, phase, order) for order in range(2)]
     result = []
+    my_order = parity(me, count)
     for block in range(count):
         order = parity(block, count)
-        half = jnp.bitwise_xor(parity(me, count), order) * (count // 2)
+        half = jnp.bitwise_xor(my_order, order) * (count // 2)
         result.append(half + jnp.bitwise_xor(own[order], place(block, count, phase, order)))
     return result
 
@@ -83,8 +85,8 @@
 
 def first_kernel(
     count, rows, span, later_span,
-    me_ref, acts_ref, gain_ref, w_ref, send_ref, keep_ref, scaled, later_weights,
-    narrow, gains, ordered, squares, weights, small_sems, sems, later_sems,
+    me_ref, acts_ref, gain_ref, w_ref, send_ref, keep_ref, later_scaled, later_weights,
+    narrow, gains, ordered, scaled, squares, weights, small_sems, sems, later_sems,
 ):
     start, width = span
     half = count * rows // 2
@@ -101,19 +103,22 @@
         copy.wait()
     gain = gains[...].astype(jnp.float32)[None, :]
     lane = lax.broadcasted_iota(jnp.int32, (rows, LANES), 1)
-    targets = places(me, count, 0)
-    for pair in range(count // 2):
-        both = narrow[2 * pair * rows : 2 * (pair + 1) * rows, :].astype(jnp.float32)
-        for side in range(2):
-            wide = both[side * rows : (side + 1) * rows]
-            target = targets[2 * pair + side]
-            where = pl.ds(pl.multiple_of(target * rows, rows), rows)
-            ordered[where, :] = wide * gain
-            total = jnp.sum(wide * wide, axis=1, keepdims=True)
-            high = total.astype(jnp.bfloat16).astype(jnp.float32)
-            lanes = jnp.where(lane == 2 * me, high, 0.0)
-            squares[where, :] = jnp.where(lane == 2 * me + 1, total - high, lanes)
-    scaled[...] = ordered[...].astype(jnp.bfloat16)
+    for chunk, target_ref in ((1, later_scaled), (0, scaled)):
+        targets = places(me, count, chunk)
+        for pair in range(count // 2):
+            both = narrow[2 * pair * rows : 2 * (pair + 1) * rows, :].astype(jnp.float32)
+            for side in range(2):
+                wide = both[side * rows : (side + 1) * rows]
+                target = targets[2 * pair + side]
+                where = pl.ds(pl.multiple_of(target * rows, rows), rows)
+                ordered[where, :] = wide * gain
+                if chunk > 0:
+                    continue
+                total = jnp.sum(wide * wide, axis=1, keepdims=True)
+                high = total.astype(jnp.bfloat16).astype(jnp.float32)
+                lanes = jnp.where(lane == 2 * me, high, 0.0)
+                squares[where, :] = jnp.where(lane == 2 * me + 1, total - high, lanes)
+        target_ref[...] = ordered[...].astype(jnp.bfloat16)
     keep_ref[:, width:] = squares[:half]
     send_ref[:, width:] = squares[half:].astype(jnp.bfloat16)
     multiply(copies, scaled, weights, send_ref, keep_ref)
@@ -166,6 +171,7 @@
             pltpu.VMEM(activations.shape, jnp.bfloat16),
             pltpu.VMEM(gain.shape, jnp.bfloat16),
             pltpu.VMEM(activations.shape, jnp.float32),
+            pltpu.VMEM(activations.shape, jnp.bfloat16),
             pltpu.VMEM((2 * half, LANES), jnp.float32),
             pltpu.VMEM((tiles, depth, TILE), jnp.bfloat16),
             pltpu.SemaphoreType.DMA((2,)),
@@ -198,7 +204,7 @@
             out_ref[:, columns] = product
     if not last:
         return
-    sources = places(me_ref[0], count, 1)
+    sources = places(me_ref[0], count, GATHER)
     for pair in range(count // 2):
         parts = []
         for source in sources[2 * pair : 2 * pair + 2]:
@@ -295,7 +301,8 @@
 
 
 class Reduction:
-    def __init__(self, send, keep, count, rows):
+    def __init__(self, send, keep, count, rows, chunk):
+        self.chunk = chunk
         self.keep, self.count, self.rows = keep, count, rows
         self.size = count // 2
         self.received = [swap(send, count)]
@@ -310,7 +317,7 @@
         self.size //= 2
         part = slice(self.size * self.rows, 2 * self.size * self.rows)
         send = self.combine(part).astype(jnp.bfloat16)
-        self.received.append(swap(send, self.count, 0, len(self.received) - 1))
+        self.received.append(swap(send, self.count, self.chunk, len(self.received) - 1))
         return send
 
     def own(self):
@@ -332,7 +339,7 @@
         spans.append((start, (high * per_head if order else QKVW) - start))
     parts = []
     for send, keep in project(me, activations, norm_gain, w_qkv, count, rows, spans):
-        parts.append(Reduction(send, keep, count, rows))
+        parts.append(Reduction(send, keep, count, rows, len(parts)))
     w_out = tie(w_out, send)
     stages = len(stage_bits(count, 0)[0])
     for stage in range(stages):
@@ -375,7 +382,7 @@
             if before is not None:
                 mine = tie(mine, before)
             before = mine
-            gathered[order] = jnp.concatenate([mine, swap(mine, count, 1, stage)], axis=0)
+            gathered[order] = jnp.concatenate([mine, swap(mine, count, GATHER, stage)], axis=0)
     total = None
     for order, (low, high) in enumerate(CHUNKS):
         mine = gathered[order]

time: 58.8 us -> 57.9 us (0.985)
  starting transfers between devices: 29.1 us -> 23 us
  waiting for transfers between devices: 11.9 us -> 17 us
    ppermute x16, starting transfers between devices: 29.1 us -> 23 us  [swap(): return lax.ppermute(value, 'gx', partners)]
    ppermute x16, waiting for transfers between devices: 11.9 us -> 17 us  [swap(): return lax.ppermute(value, 'gx', partners)]
  transfers between devices with their start and end apart: 16 -> 16, of which waited for: 10 -> 12; matrix products, arithmetic and copies ran while one was open for 9% -> 9% of each run, Pallas kernels for 4% -> 4%
where the time goes in v7:
time: 57.9 us; the launch traced here: 57.7 us
  starting transfers between devices  23 us (40%)
  waiting for transfers between devices  17 us (29%)
  Pallas kernels  12.2 us (21%)
  matrix products  2.09 us (4%)
  other arithmetic  1.68 us (3%)
  local copies, waits for them, and re-layouts  1.27 us (2%)
    ppermute x16, starting transfers between devices, swap(): return lax.ppermute(value, 'gx', partners)  23 us
    ppermute x16, waiting for transfers between devices, swap(): return lax.ppermute(value, 'gx', partners)  17 us
    pallas_call x2, Pallas kernels, call(): pl.pallas_call(kernel, in_specs=in_specs, out_specs=[in_vmem] * len(out_s...  8.9 us
    pallas_call x2, Pallas kernels, output_part(): pl.pallas_call(functools.partial(output_kernel, count, rows, start), in_s...  3.34 us
  transfers between devices with their start and end apart: 16, of which 12 were waited for; matrix products, arithmetic and copies ran while one was open for 9% of the time, Pallas kernels for 4%

profile of v7, /device:TPU:0, one launch (start us, length us, event | category | flops | bytes accessed | tf_op | source)
XLA Modules:
  0.0 57.7 jit_solution(9165908386567615765)
XLA Ops:
  0.0 7.6 %shard_map.64 = (bf16[64,5248]{1,0:T(8,128)(2,1)S(1)}, f32[64,5248]{1,0:T(8,128)S(1)}, bf16[128,1024]{1,0:T(8,128)(2,1)S(1)}, bf16[4,1024,1024]{2,1,0:T(8,128)(2,1)S(1)}) custom-call(s32[1]{0:T(128)} %bitcast.me_ref, bf16[128,1024]{1,0:T(8,128)(2,1)} %acts_ref.1, bf16[1024]{0:T(1024)(128)(2,1)} %gain_ref.1, bf16[1024,9216]{1,0:T(8,128)(2,1)} %w_ref.1), custom_call_target="tpu_custom_call" | custom-call | flops 1342177280 | bytes 12500992 | tf_op jit(solution)/shard_map/pallas_call | solution.py:144
  7.6 0.5 collective-permute-start
  8.2 1.3 %shard_map.65 = (bf16[64,4096]{1,0:T(8,128)(2,1)S(1)}, f32[64,4096]{1,0:T(8,128)S(1)}) custom-call(bf16[128,1024]{1,0:T(8,128)(2,1)S(1)} %get-tuple-element.18.scaled, bf16[4,1024,1024]{2,1,0:T(8,128)(2,1)S(1)} %get-tuple-element.19.weights), custom_call_target="tpu_custom_call" | custom-call | flops 1073741824 | bytes 9961472 | tf_op jit(solution)/shard_map/pallas_call | solution.py:144
  9.4 0.0 copy-start
  9.4 0.1 collective-permute-start.4
  9.6 0.3 collective-permute-done
  9.9 0.1 add_convert_fusion
  10.0 2.7 %collective-permute-start.1 = (bf16[32,5248]{1,0:T(8,128)(2,1)S(1)}, bf16[32,5248]{1,0:T(8,128)(2,1)S(1)}, u32[]{:S(2)}, u32[]{:S(2)}) collective-permute-start(bf16[32,5248]{1,0:T(8,128)(2,1)S(1)} %add_convert_fusion), channel_id=1, source_target_pairs={{0,3},{1,4},{2,7},{3,0},{4,1},{5,6},{6,5},{7,2},{8,13},{9,10},{10,... | collective-permute-start | bytes 1007624 | tf_op jit(solution)/shard_map/ppermute | solution.py:296
  12.7 0.0 collective-permute-done.4
  12.7 0.1 add_convert_fusion.1
  12.7 1.5 %collective-permute-start.5 = (bf16[32,4096]{1,0:T(8,128)(2,1)S(1)}, bf16[32,4096]{1,0:T(8,128)(2,1)S(1)}, u32[]{:S(2)}, u32[]{:S(2)}) collective-permute-start(bf16[32,4096]{1,0:T(8,128)(2,1)S(1)} %add_convert_fusion.1), channel_id=1, source_target_pairs={{0,3},{1,4},{2,7},{3,0},{4,1},{5,6},{6,5},{7,2},{8,13},{9,10},{10,... | collective-permute-start | bytes 786440 | tf_op jit(solution)/shard_map/ppermute | solution.py:296
  14.2 0.0 copy-done
  14.2 0.5 copy.9
  14.7 0.0 copy-done.1
  14.7 0.0 slice-start.2
  14.7 0.5 copy.10
  15.2 2.3 %collective-permute-done.1 = bf16[32,5248]{1,0:T(8,128)(2,1)S(1)} collective-permute-done((bf16[32,5248]{1,0:T(8,128)(2,1)S(1)}, bf16[32,5248]{1,0:T(8,128)(2,1)S(1)}, u32[]{:S(2)}, u32[]{:S(2)}) %collective-permute-start.1) | collective-permute-done | bytes 335904 | tf_op jit(solution)/shard_map/ppermute | solution.py:296
  17.5 0.1 add_convert_fusion.2
  17.6 2.2 %collective-permute-start.2 = (bf16[16,5248]{1,0:T(8,128)(2,1)S(1)}, bf16[16,5248]{1,0:T(8,128)(2,1)S(1)}, u32[]{:S(2)}, u32[]{:S(2)}) collective-permute-start(bf16[16,5248]{1,0:T(8,128)(2,1)S(1)} %add_convert_fusion.2), channel_id=1, source_target_pairs={{0,5},{1,8},{2,11},{3,6},{4,13},{5,0},{6,3},{7,14},{8,1},{9,12},{1... | collective-permute-start | bytes 503816 | tf_op jit(solution)/shard_map/ppermute | solution.py:296
  19.7 0.6 %collective-permute-done.5 = bf16[32,4096]{1,0:T(8,128)(2,1)S(1)} collective-permute-done((bf16[32,4096]{1,0:T(8,128)(2,1)S(1)}, bf16[32,4096]{1,0:T(8,128)(2,1)S(1)}, u32[]{:S(2)}, u32[]{:S(2)}) %collective-permute-start.5) | collective-permute-done | bytes 262176 | tf_op jit(solution)/shard_map/ppermute | solution.py:296
  20.4 1.9 %collective-permute-start.6 = (bf16[16,4096]{1,0:T(8,128)(2,1)S(1)}, bf16[16,4096]{1,0:T(8,128)(2,1)S(1)}, u32[]{:S(2)}, u32[]{:S(2)}) collective-permute-start(bf16[16,4096]{1,0:T(8,128)(2,1)S(1)} %add_convert_fusion.3), channel_id=1, source_target_pairs={{0,5},{1,2},{2,1},{3,6},{4,7},{5,0},{6,3},{7,4},{8,11},{9,12},{10,... | collective-permute-start | bytes 393224 | tf_op jit(solution)/shard_map/ppermute | solution.py:296
  22.2 1.9 %collective-permute-done.2 = bf16[16,5248]{1,0:T(8,128)(2,1)S(1)} collective-permute-done((bf16[16,5248]{1,0:T(8,128)(2,1)S(1)}, bf16[16,5248]{1,0:T(8,128)(2,1)S(1)}, u32[]{:S(2)}, u32[]{:S(2)}) %collective-permute-start.2) | collective-permute-done | bytes 167968 | tf_op jit(solution)/shard_map/ppermute | solution.py:296
  24.1 2.9 %collective-permute-start.3 = (bf16[8,5248]{1,0:T(8,128)(2,1)S(1)}, bf16[8,5248]{1,0:T(8,128)(2,1)S(1)}, u32[]{:S(2)}, u32[]{:S(2)}) collective-permute-start(bf16[8,5248]{1,0:T(8,128)(2,1)S(1)} %add_convert_fusion.4), channel_id=1, source_target_pairs={{0,9},{1,2},{2,1},{3,10},{4,7},{5,12},{6,15},{7,4},{8,11},{9,0},{1... | collective-permute-start | bytes 251912 | tf_op jit(solution)/shard_map/ppermute | solution.py:296
  27.1 0.0 collective-permute-done.6
  27.1 1.1 %collective-permute-start.7 = (bf16[8,4096]{1,0:T(8,128)(2,1)S(1)}, bf16[8,4096]{1,0:T(8,128)(2,1)S(1)}, u32[]{:S(2)}, u32[]{:S(2)}) collective-permute-start(bf16[8,4096]{1,0:T(8,128)(2,1)S(1)} %add_convert_fusion.6), channel_id=1, source_target_pairs={{0,9},{1,8},{2,11},{3,10},{4,13},{5,12},{6,15},{7,14},{8,1},{9,0},... | collective-permute-start | bytes 196616 | tf_op jit(solution)/shard_map/ppermute | solution.py:296
  28.2 1.0 %collective-permute-done.3 = bf16[8,5248]{1,0:T(8,128)(2,1)S(1)} collective-permute-done((bf16[8,5248]{1,0:T(8,128)(2,1)S(1)}, bf16[8,5248]{1,0:T(8,128)(2,1)S(1)}, u32[]{:S(2)}, u32[]{:S(2)}) %collective-permute-start.3) | collective-permute-done | bytes 84000 | tf_op jit(solution)/shard_map/ppermute | solution.py:296
  29.2 0.1 convert_add_fusion
  29.3 0.1 slice_reduce_fusion
  29.4 0.1 slice_multiply_fusion.1
  29.5 0.1 fusion.8
  29.6 0.1 add_convert_fusion.8
  29.7 0.1 subtract_convert_fusion.1
  29.8 0.1 fusion.20
  29.9 0.2 fusion.14
  30.1 0.5 fusion.31
  30.6 0.2 fusion.6
  30.9 0.0 slice-start.3
  30.9 0.3 fusion
  31.3 2.7 %collective-permute-start.9 = (bf16[8,4096]{1,0:T(8,128)(2,1)S(1)}, bf16[8,4096]{1,0:T(8,128)(2,1)S(1)}, u32[]{:S(2)}, u32[]{:S(2)}) collective-permute-start(bf16[8,4096]{1,0:T(8,128)(2,1)S(1)} %bitcast.51), channel_id=1, source_target_pairs={{0,9},{1,8},{2,11},{3,10},{4,13},{5,12},{6,15},{7,14},{8,1},{9,0},... | collective-permute-start | bytes 196616 | tf_op jit(solution)/shard_map/ppermute | solution.py:296
  34.0 0.0 collective-permute-done.7
  34.0 0.1 multiply_bitcast_fusion
  34.1 0.1 subtract_convert_fusion
  34.3 0.5 fusion.32
  34.8 0.2 fusion.13
  35.0 0.2 fusion.7
  35.3 0.3 fusion.1
  35.7 0.1 collective-permute-start.8
  35.8 0.5 collective-permute-done.9
  36.2 5.5 %collective-permute-start.11 = (bf16[16,4096]{1,0:T(8,128)(2,1)S(1)}, bf16[16,4096]{1,0:T(8,128)(2,1)S(1)}, u32[]{:S(2)}, u32[]{:S(2)}) collective-permute-start(bf16[16,4096]{1,0:T(8,128)(2,1)S(1)} %get-tuple-element.39), channel_id=1, source_target_pairs={{0,3},{1,4},{2,7},{3,0},{4,1},{5,6},{6,5},{7,2},{8,13},{9,10},{10,... | collective-permute-start | bytes 393224 | tf_op jit(solution)/shard_map/ppermute | solution.py:296
  41.8 0.5 collective-permute-done.8
  42.3 1.6 %collective-permute-start.10 = (bf16[16,4096]{1,0:T(8,128)(2,1)S(1)}, bf16[16,4096]{1,0:T(8,128)(2,1)S(1)}, u32[]{:S(2)}, u32[]{:S(2)}) collective-permute-start(bf16[16,4096]{1,0:T(8,128)(2,1)S(1)} %pad_maximum_fusion.1), channel_id=1, source_target_pairs={{0,3},{1,4},{2,7},{3,0},{4,1},{5,6},{6,5},{7,2},{8,13},{9,10},{10,... | collective-permute-start | bytes 393224 | tf_op jit(solution)/shard_map/ppermute | solution.py:296
  43.9 0.5 collective-permute-done.11
  44.4 0.1 collective-permute-start.14
  44.5 3.3 %collective-permute-done.10 = bf16[16,4096]{1,0:T(8,128)(2,1)S(1)} collective-permute-done((bf16[16,4096]{1,0:T(8,128)(2,1)S(1)}, bf16[16,4096]{1,0:T(8,128)(2,1)S(1)}, u32[]{:S(2)}, u32[]{:S(2)}) %collective-permute-start.10) | collective-permute-done | bytes 131104 | tf_op jit(solution)/shard_map/ppermute | solution.py:296
  47.8 0.1 collective-permute-start.12
  47.9 2.4 %collective-permute-done.14 = bf16[32,4096]{1,0:T(8,128)(2,1)S(1)} collective-permute-done((bf16[32,4096]{1,0:T(8,128)(2,1)S(1)}, bf16[32,4096]{1,0:T(8,128)(2,1)S(1)}, u32[]{:S(2)}, u32[]{:S(2)}) %collective-permute-start.14) | collective-permute-done | bytes 262176 | tf_op jit(solution)/shard_map/ppermute | solution.py:296
  50.3 0.1 collective-permute-start.15
  50.4 3.3 %collective-permute-done.12 = bf16[32,4096]{1,0:T(8,128)(2,1)S(1)} collective-permute-done((bf16[32,4096]{1,0:T(8,128)(2,1)S(1)}, bf16[32,4096]{1,0:T(8,128)(2,1)S(1)}, u32[]{:S(2)}, u32[]{:S(2)}) %collective-permute-start.12) | collective-permute-done | bytes 262176 | tf_op jit(solution)/shard_map/ppermute | solution.py:296
  53.7 0.1 collective-permute-start.13
  53.8 0.0 collective-permute-done.15.other_ref
  53.8 0.0 slice-done
  53.8 1.3 %shard_map.66.refs_0_ = f32[128,1024]{1,0:T(8,128)S(1)} custom-call(s32[1]{0:T(128)} %bitcast.me_ref, bf16[64,4096]{1,0:T(8,128)(2,1)S(1)} %constant_dynamic-update-slice_fusion.7.mine_ref, bf16[64,4096]{1,0:T(8,128)(2,1)S(1)} %collective-permute-done.15.other_ref, bf16[8192,1024]{1,0:T(8,128)(2,1)S(1)} %bitcast.38), custom_call_target="tpu_custom_call" | custom-call | flops 1073741824 | bytes 9699328 | tf_op jit(solution)/shard_map/pallas_call | solution.py:221
  55.2 0.5 collective-permute-done.13.other_ref
  55.7 2.0 %shard_map.67 = bf16[128,1024]{1,0:T(8,128)(2,1)} custom-call(s32[1]{0:T(128)} %bitcast.me_ref, bf16[64,4096]{1,0:T(8,128)(2,1)S(1)} %constant_dynamic-update-slice_fusion.5.mine_ref, bf16[64,4096]{1,0:T(8,128)(2,1)S(1)} %collective-permute-done.13.other_ref, bf16[8192,1024]{1,0:T(8,128)(2,1)S(1)} %bitcast.38, f32[128,1024]{1,0:T(8,128)S(1)} %shard_map.66.refs_0_), custom_call_target="tpu_custom_call" | custom-call | flops 1073741824 | bytes 9699328 | tf_op jit(solution)/shard_map/pallas_call | solution.py:221
  (35 shorter events, 0.6 us)
Async XLA Ops:
  7.6 2.3 %collective-permute-start = (bf16[64,5248]{1,0:T(8,128)(2,1)S(1)}, bf16[64,5248]{1,0:T(8,128)(2,1)S(1)}, u32[]{:S(2)}, u32[]{:S(2)}) collective-permute-start(bf16[64,5248]{1,0:T(8,128)(2,1)S(1)} %get-tuple-element.22), channel_id=1, source_target_pairs={{0,1},{1,0},{2,3},{3,2},{4,5},{5,4},{6,7},{7,6},{8,9},{9,8},{10,11... | collective-permute-start | bytes 2015240 | tf_op jit(solution)/shard_map/ppermute | solution.py:296
  8.2 6.5 %copy-start.1 = (bf16[8,256,4,128]{3,2,1,0:T(4,128)(2,1)S(1)}, bf16[8,256,4,128]{3,2,1,0:T(4,128)(2,1)}, u32[]{:S(2)}) copy-start(bf16[8,256,4,128]{3,2,1,0:T(4,128)(2,1)} %param.11) | copy-start | bytes 6291460
  8.2 45.6 %slice-start = ((s8[16777216]{0:T(1024)(128)(4,1)}), s8[4194304]{0:T(1024)(128)(4,1)S(1)}, s32[]{:S(2)}) async-start(s8[16777216]{0:T(1024)(128)(4,1)} %bitcast.37), calls=%async_computation | async-start | bytes 8388608
  9.4 4.8 %copy-start = (bf16[8,256,4,128]{3,2,1,0:T(4,128)(2,1)S(1)}, bf16[8,256,4,128]{3,2,1,0:T(4,128)(2,1)}, u32[]{:S(2)}) copy-start(bf16[8,256,4,128]{3,2,1,0:T(4,128)(2,1)} %param.10) | copy-start | bytes 6291460
  9.4 3.2 %collective-permute-start.4 = (bf16[64,4096]{1,0:T(8,128)(2,1)S(1)}, bf16[64,4096]{1,0:T(8,128)(2,1)S(1)}, u32[]{:S(2)}, u32[]{:S(2)}) collective-permute-start(bf16[64,4096]{1,0:T(8,128)(2,1)S(1)} %get-tuple-element.23), channel_id=1, source_target_pairs={{0,1},{1,0},{2,3},{3,2},{4,5},{5,4},{6,7},{7,6},{8,9},{9,8},{10,11... | collective-permute-start | bytes 1572872 | tf_op jit(solution)/shard_map/ppermute | solution.py:296
  9.9 43.9 %slice-start.1 = ((s8[16777216]{0:T(1024)(128)(4,1)}), s8[4194304]{0:T(1024)(128)(4,1)S(1)}, s32[]{:S(2)}) async-start(s8[16777216]{0:T(1024)(128)(4,1)} %bitcast.37), calls=%async_computation.1 | async-start | bytes 8388608
  10.0 7.5 %collective-permute-start.1 = (bf16[32,5248]{1,0:T(8,128)(2,1)S(1)}, bf16[32,5248]{1,0:T(8,128)(2,1)S(1)}, u32[]{:S(2)}, u32[]{:S(2)}) collective-permute-start(bf16[32,5248]{1,0:T(8,128)(2,1)S(1)} %add_convert_fusion), channel_id=1, source_target_pairs={{0,3},{1,4},{2,7},{3,0},{4,1},{5,6},{6,5},{7,2},{8,13},{9,10},{10,... | collective-permute-start | bytes 1007624 | tf_op jit(solution)/shard_map/ppermute | solution.py:296
  12.7 7.6 %collective-permute-start.5 = (bf16[32,4096]{1,0:T(8,128)(2,1)S(1)}, bf16[32,4096]{1,0:T(8,128)(2,1)S(1)}, u32[]{:S(2)}, u32[]{:S(2)}) collective-permute-start(bf16[32,4096]{1,0:T(8,128)(2,1)S(1)} %add_convert_fusion.1), channel_id=1, source_target_pairs={{0,3},{1,4},{2,7},{3,0},{4,1},{5,6},{6,5},{7,2},{8,13},{9,10},{10,... | collective-permute-start | bytes 786440 | tf_op jit(solution)/shard_map/ppermute | solution.py:296
  14.7 39.1 %slice-start.2 = ((s8[16777216]{0:T(1024)(128)(4,1)}), s8[4194304]{0:T(1024)(128)(4,1)S(1)}, s32[]{:S(2)}) async-start(s8[16777216]{0:T(1024)(128)(4,1)} %bitcast.37), calls=%async_computation.2 | async-start | bytes 8388608
  17.6 6.5 %collective-permute-start.2 = (bf16[16,5248]{1,0:T(8,128)(2,1)S(1)}, bf16[16,5248]{1,0:T(8,128)(2,1)S(1)}, u32[]{:S(2)}, u32[]{:S(2)}) collective-permute-start(bf16[16,5248]{1,0:T(8,128)(2,1)S(1)} %add_convert_fusion.2), channel_id=1, source_target_pairs={{0,5},{1,8},{2,11},{3,6},{4,13},{5,0},{6,3},{7,14},{8,1},{9,12},{1... | collective-permute-start | bytes 503816 | tf_op jit(solution)/shard_map/ppermute | solution.py:296
  20.4 6.7 %collective-permute-start.6 = (bf16[16,4096]{1,0:T(8,128)(2,1)S(1)}, bf16[16,4096]{1,0:T(8,128)(2,1)S(1)}, u32[]{:S(2)}, u32[]{:S(2)}) collective-permute-start(bf16[16,4096]{1,0:T(8,128)(2,1)S(1)} %add_convert_fusion.3), channel_id=1, source_target_pairs={{0,5},{1,2},{2,1},{3,6},{4,7},{5,0},{6,3},{7,4},{8,11},{9,12},{10,... | collective-permute-start | bytes 393224 | tf_op jit(solution)/shard_map/ppermute | solution.py:296
  24.1 5.1 %collective-permute-start.3 = (bf16[8,5248]{1,0:T(8,128)(2,1)S(1)}, bf16[8,5248]{1,0:T(8,128)(2,1)S(1)}, u32[]{:S(2)}, u32[]{:S(2)}) collective-permute-start(bf16[8,5248]{1,0:T(8,128)(2,1)S(1)} %add_convert_fusion.4), channel_id=1, source_target_pairs={{0,9},{1,2},{2,1},{3,10},{4,7},{5,12},{6,15},{7,4},{8,11},{9,0},{1... | collective-permute-start | bytes 251912 | tf_op jit(solution)/shard_map/ppermute | solution.py:296
  27.1 6.9 %collective-permute-start.7 = (bf16[8,4096]{1,0:T(8,128)(2,1)S(1)}, bf16[8,4096]{1,0:T(8,128)(2,1)S(1)}, u32[]{:S(2)}, u32[]{:S(2)}) collective-permute-start(bf16[8,4096]{1,0:T(8,128)(2,1)S(1)} %add_convert_fusion.6), channel_id=1, source_target_pairs={{0,9},{1,8},{2,11},{3,10},{4,13},{5,12},{6,15},{7,14},{8,1},{9,0},... | collective-permute-start | bytes 196616 | tf_op jit(solution)/shard_map/ppermute | solution.py:296
  30.9 22.9 %slice-start.3 = ((s8[16777216]{0:T(1024)(128)(4,1)}), s8[4194304]{0:T(1024)(128)(4,1)S(1)}, s32[]{:S(2)}) async-start(s8[16777216]{0:T(1024)(128)(4,1)} %bitcast.37), calls=%async_computation.3 | async-start | bytes 8388608
  31.3 4.9 %collective-permute-start.9 = (bf16[8,4096]{1,0:T(8,128)(2,1)S(1)}, bf16[8,4096]{1,0:T(8,128)(2,1)S(1)}, u32[]{:S(2)}, u32[]{:S(2)}) collective-permute-start(bf16[8,4096]{1,0:T(8,128)(2,1)S(1)} %bitcast.51), channel_id=1, source_target_pairs={{0,9},{1,8},{2,11},{3,10},{4,13},{5,12},{6,15},{7,14},{8,1},{9,0},... | collective-permute-start | bytes 196616 | tf_op jit(solution)/shard_map/ppermute | solution.py:296
  35.7 6.6 %collective-permute-start.8 = (bf16[8,4096]{1,0:T(8,128)(2,1)S(1)}, bf16[8,4096]{1,0:T(8,128)(2,1)S(1)}, u32[]{:S(2)}, u32[]{:S(2)}) collective-permute-start(bf16[8,4096]{1,0:T(8,128)(2,1)S(1)} %bitcast.47), channel_id=1, source_target_pairs={{0,9},{1,8},{2,11},{3,10},{4,13},{5,12},{6,15},{7,14},{8,1},{9,0},... | collective-permute-start | bytes 196616 | tf_op jit(solution)/shard_map/ppermute | solution.py:296
  36.2 8.2 %collective-permute-start.11 = (bf16[16,4096]{1,0:T(8,128)(2,1)S(1)}, bf16[16,4096]{1,0:T(8,128)(2,1)S(1)}, u32[]{:S(2)}, u32[]{:S(2)}) collective-permute-start(bf16[16,4096]{1,0:T(8,128)(2,1)S(1)} %get-tuple-element.39), channel_id=1, source_target_pairs={{0,3},{1,4},{2,7},{3,0},{4,1},{5,6},{6,5},{7,2},{8,13},{9,10},{10,... | collective-permute-start | bytes 393224 | tf_op jit(solution)/shard_map/ppermute | solution.py:296
  42.3 5.5 %collective-permute-start.10 = (bf16[16,4096]{1,0:T(8,128)(2,1)S(1)}, bf16[16,4096]{1,0:T(8,128)(2,1)S(1)}, u32[]{:S(2)}, u32[]{:S(2)}) collective-permute-start(bf16[16,4096]{1,0:T(8,128)(2,1)S(1)} %pad_maximum_fusion.1), channel_id=1, source_target_pairs={{0,3},{1,4},{2,7},{3,0},{4,1},{5,6},{6,5},{7,2},{8,13},{9,10},{10,... | collective-permute-start | bytes 393224 | tf_op jit(solution)/shard_map/ppermute | solution.py:296
  44.4 5.9 %collective-permute-start.14 = (bf16[32,4096]{1,0:T(8,128)(2,1)S(1)}, bf16[32,4096]{1,0:T(8,128)(2,1)S(1)}, u32[]{:S(2)}, u32[]{:S(2)}) collective-permute-start(bf16[32,4096]{1,0:T(8,128)(2,1)S(1)} %get-tuple-element.36), channel_id=1, source_target_pairs={{0,5},{1,2},{2,1},{3,6},{4,7},{5,0},{6,3},{7,4},{8,11},{9,12},{10,... | collective-permute-start | bytes 786440 | tf_op jit(solution)/shard_map/ppermute | solution.py:296
  47.8 5.9 %collective-permute-start.12 = (bf16[32,4096]{1,0:T(8,128)(2,1)S(1)}, bf16[32,4096]{1,0:T(8,128)(2,1)S(1)}, u32[]{:S(2)}, u32[]{:S(2)}) collective-permute-start(bf16[32,4096]{1,0:T(8,128)(2,1)S(1)} %pad_maximum_fusion), channel_id=1, source_target_pairs={{0,5},{1,2},{2,1},{3,6},{4,7},{5,0},{6,3},{7,4},{8,11},{9,12},{10,... | collective-permute-start | bytes 786440 | tf_op jit(solution)/shard_map/ppermute | solution.py:296
  50.3 3.5 %collective-permute-start.15 = (bf16[64,4096]{1,0:T(8,128)(2,1)S(1)}, bf16[64,4096]{1,0:T(8,128)(2,1)S(1)}, u32[]{:S(2)}, u32[]{:S(2)}) collective-permute-start(bf16[64,4096]{1,0:T(8,128)(2,1)S(1)} %constant_dynamic-update-slice_fusion.7.mine_ref), channel_id=1, source_target_pairs={{0,1},{1,0},{2,3},{3,2},{4,5},{5,4},{6,7},{7,6},{8,9},{9,8},{10,11... | collective-permute-start | bytes 1572872 | tf_op jit(solution)/shard_map/ppermute | solution.py:296
  53.7 2.0 %collective-permute-start.13 = (bf16[64,4096]{1,0:T(8,128)(2,1)S(1)}, bf16[64,4096]{1,0:T(8,128)(2,1)S(1)}, u32[]{:S(2)}, u32[]{:S(2)}) collective-permute-start(bf16[64,4096]{1,0:T(8,128)(2,1)S(1)} %constant_dynamic-update-slice_fusion.5.mine_ref), channel_id=1, source_target_pairs={{0,1},{1,0},{2,3},{3,2},{4,5},{5,4},{6,7},{7,6},{8,9},{9,8},{10,11... | collective-permute-start | bytes 1572872 | tf_op jit(solution)/shard_map/ppermute | solution.py:296

commit v8 on v7

--- a/solution.py
+++ b/solution.py
@@ -267,7 +267,10 @@
         * scaling
     )
     own_scores = (
-        jnp.einsum("rkgd,rkd->rkg", grouped_queries, fresh_keys, preferred_element_type=jnp.float32)
+        jnp.sum(
+            grouped_queries.astype(jnp.float32) * fresh_keys.astype(jnp.float32)[:, :, None, :],
+            axis=-1,
+        )
         * scaling
     )
     highest = jnp.maximum(jnp.max(cached_scores, axis=-1), own_scores)

time: 57.9 us -> 57.8 us (level)
  no operation moved by 1% of the time
where the time goes in v8:
time: 57.8 us; the launch traced here: 57.7 us
  starting transfers between devices  23 us (40%)
  waiting for transfers between devices  17 us (29%)
  Pallas kernels  12.2 us (21%)
  other arithmetic  2.09 us (4%)
  matrix products  1.65 us (3%)
  local copies, waits for them, and re-layouts  1.28 us (2%)
    ppermute x16, starting transfers between devices, swap(): return lax.ppermute(value, 'gx', partners)  23 us
    ppermute x16, waiting for transfers between devices, swap(): return lax.ppermute(value, 'gx', partners)  17 us
    pallas_call x2, Pallas kernels, call(): pl.pallas_call(kernel, in_specs=in_specs, out_specs=[in_vmem] * len(out_s...  8.9 us
    pallas_call x2, Pallas kernels, output_part(): pl.pallas_call(functools.partial(output_kernel, count, rows, start), in_s...  3.34 us
  transfers between devices with their start and end apart: 16, of which 12 were waited for; matrix products, arithmetic and copies ran while one was open for 9% of the time, Pallas kernels for 4%

profile of v8, /device:TPU:0, one launch (start us, length us, event | category | flops | bytes accessed | tf_op | source)
XLA Modules:
  0.0 57.7 jit_solution(2030943761034977699)
XLA Ops:
  0.0 7.6 %shard_map.64 = (bf16[64,5248]{1,0:T(8,128)(2,1)S(1)}, f32[64,5248]{1,0:T(8,128)S(1)}, bf16[128,1024]{1,0:T(8,128)(2,1)S(1)}, bf16[4,1024,1024]{2,1,0:T(8,128)(2,1)S(1)}) custom-call(s32[1]{0:T(128)} %bitcast.me_ref, bf16[128,1024]{1,0:T(8,128)(2,1)} %acts_ref.1, bf16[1024]{0:T(1024)(128)(2,1)} %gain_ref.1, bf16[1024,9216]{1,0:T(8,128)(2,1)} %w_ref.1), custom_call_target="tpu_custom_call" | custom-call | flops 1342177280 | bytes 12500992 | tf_op jit(solution)/shard_map/pallas_call | solution.py:144
  7.6 0.5 collective-permute-start
  8.2 1.3 %shard_map.65 = (bf16[64,4096]{1,0:T(8,128)(2,1)S(1)}, f32[64,4096]{1,0:T(8,128)S(1)}) custom-call(bf16[128,1024]{1,0:T(8,128)(2,1)S(1)} %get-tuple-element.18.scaled, bf16[4,1024,1024]{2,1,0:T(8,128)(2,1)S(1)} %get-tuple-element.19.weights), custom_call_target="tpu_custom_call" | custom-call | flops 1073741824 | bytes 9961472 | tf_op jit(solution)/shard_map/pallas_call | solution.py:144
  9.4 0.0 copy-start
  9.4 0.1 collective-permute-start.4
  9.6 0.3 collective-permute-done
  9.9 0.1 add_convert_fusion
  10.0 2.7 %collective-permute-start.1 = (bf16[32,5248]{1,0:T(8,128)(2,1)S(1)}, bf16[32,5248]{1,0:T(8,128)(2,1)S(1)}, u32[]{:S(2)}, u32[]{:S(2)}) collective-permute-start(bf16[32,5248]{1,0:T(8,128)(2,1)S(1)} %add_convert_fusion), channel_id=1, source_target_pairs={{0,3},{1,4},{2,7},{3,0},{4,1},{5,6},{6,5},{7,2},{8,13},{9,10},{10,... | collective-permute-start | bytes 1007624 | tf_op jit(solution)/shard_map/ppermute | solution.py:299
  12.7 0.0 collective-permute-done.4
  12.7 0.1 add_convert_fusion.1
  12.7 1.5 %collective-permute-start.5 = (bf16[32,4096]{1,0:T(8,128)(2,1)S(1)}, bf16[32,4096]{1,0:T(8,128)(2,1)S(1)}, u32[]{:S(2)}, u32[]{:S(2)}) collective-permute-start(bf16[32,4096]{1,0:T(8,128)(2,1)S(1)} %add_convert_fusion.1), channel_id=1, source_target_pairs={{0,3},{1,4},{2,7},{3,0},{4,1},{5,6},{6,5},{7,2},{8,13},{9,10},{10,... | collective-permute-start | bytes 786440 | tf_op jit(solution)/shard_map/ppermute | solution.py:299
  14.2 0.0 copy-done
  14.2 0.5 copy.9
  14.7 0.0 copy-done.1
  14.7 0.0 slice-start.2
  14.7 0.5 copy.11
  15.2 2.3 %collective-permute-done.1 = bf16[32,5248]{1,0:T(8,128)(2,1)S(1)} collective-permute-done((bf16[32,5248]{1,0:T(8,128)(2,1)S(1)}, bf16[32,5248]{1,0:T(8,128)(2,1)S(1)}, u32[]{:S(2)}, u32[]{:S(2)}) %collective-permute-start.1) | collective-permute-done | bytes 335904 | tf_op jit(solution)/shard_map/ppermute | solution.py:299
  17.5 0.1 add_convert_fusion.2
  17.6 2.2 %collective-permute-start.2 = (bf16[16,5248]{1,0:T(8,128)(2,1)S(1)}, bf16[16,5248]{1,0:T(8,128)(2,1)S(1)}, u32[]{:S(2)}, u32[]{:S(2)}) collective-permute-start(bf16[16,5248]{1,0:T(8,128)(2,1)S(1)} %add_convert_fusion.2), channel_id=1, source_target_pairs={{0,5},{1,8},{2,11},{3,6},{4,13},{5,0},{6,3},{7,14},{8,1},{9,12},{1... | collective-permute-start | bytes 503816 | tf_op jit(solution)/shard_map/ppermute | solution.py:299
  19.7 0.6 %collective-permute-done.5 = bf16[32,4096]{1,0:T(8,128)(2,1)S(1)} collective-permute-done((bf16[32,4096]{1,0:T(8,128)(2,1)S(1)}, bf16[32,4096]{1,0:T(8,128)(2,1)S(1)}, u32[]{:S(2)}, u32[]{:S(2)}) %collective-permute-start.5) | collective-permute-done | bytes 262176 | tf_op jit(solution)/shard_map/ppermute | solution.py:299
  20.4 1.9 %collective-permute-start.6 = (bf16[16,4096]{1,0:T(8,128)(2,1)S(1)}, bf16[16,4096]{1,0:T(8,128)(2,1)S(1)}, u32[]{:S(2)}, u32[]{:S(2)}) collective-permute-start(bf16[16,4096]{1,0:T(8,128)(2,1)S(1)} %add_convert_fusion.3), channel_id=1, source_target_pairs={{0,5},{1,2},{2,1},{3,6},{4,7},{5,0},{6,3},{7,4},{8,11},{9,12},{10,... | collective-permute-start | bytes 393224 | tf_op jit(solution)/shard_map/ppermute | solution.py:299
  22.2 1.9 %collective-permute-done.2 = bf16[16,5248]{1,0:T(8,128)(2,1)S(1)} collective-permute-done((bf16[16,5248]{1,0:T(8,128)(2,1)S(1)}, bf16[16,5248]{1,0:T(8,128)(2,1)S(1)}, u32[]{:S(2)}, u32[]{:S(2)}) %collective-permute-start.2) | collective-permute-done | bytes 167968 | tf_op jit(solution)/shard_map/ppermute | solution.py:299
  24.1 2.9 %collective-permute-start.3 = (bf16[8,5248]{1,0:T(8,128)(2,1)S(1)}, bf16[8,5248]{1,0:T(8,128)(2,1)S(1)}, u32[]{:S(2)}, u32[]{:S(2)}) collective-permute-start(bf16[8,5248]{1,0:T(8,128)(2,1)S(1)} %add_convert_fusion.4), channel_id=1, source_target_pairs={{0,9},{1,2},{2,1},{3,10},{4,7},{5,12},{6,15},{7,4},{8,11},{9,0},{1... | collective-permute-start | bytes 251912 | tf_op jit(solution)/shard_map/ppermute | solution.py:299
  27.1 0.0 collective-permute-done.6
  27.1 1.1 %collective-permute-start.7 = (bf16[8,4096]{1,0:T(8,128)(2,1)S(1)}, bf16[8,4096]{1,0:T(8,128)(2,1)S(1)}, u32[]{:S(2)}, u32[]{:S(2)}) collective-permute-start(bf16[8,4096]{1,0:T(8,128)(2,1)S(1)} %add_convert_fusion.6), channel_id=1, source_target_pairs={{0,9},{1,8},{2,11},{3,10},{4,13},{5,12},{6,15},{7,14},{8,1},{9,0},... | collective-permute-start | bytes 196616 | tf_op jit(solution)/shard_map/ppermute | solution.py:299
  28.2 1.0 %collective-permute-done.3 = bf16[8,5248]{1,0:T(8,128)(2,1)S(1)} collective-permute-done((bf16[8,5248]{1,0:T(8,128)(2,1)S(1)}, bf16[8,5248]{1,0:T(8,128)(2,1)S(1)}, u32[]{:S(2)}, u32[]{:S(2)}) %collective-permute-start.3) | collective-permute-done | bytes 84000 | tf_op jit(solution)/shard_map/ppermute | solution.py:299
  29.2 0.1 convert_add_fusion
  29.3 0.1 slice_reduce_fusion
  29.4 0.1 slice_multiply_fusion.1
  29.5 0.1 fusion.8
  29.6 0.1 add_convert_fusion.8
  29.6 0.1 fusion.16
  29.7 0.1 subtract_convert_fusion.1
  29.9 0.2 multiply_reduce_fusion.1
  30.1 0.5 fusion.25
  30.6 0.2 fusion.6
  30.9 0.0 slice-start.3
  30.9 0.3 fusion
  31.3 2.7 %collective-permute-start.9 = (bf16[8,4096]{1,0:T(8,128)(2,1)S(1)}, bf16[8,4096]{1,0:T(8,128)(2,1)S(1)}, u32[]{:S(2)}, u32[]{:S(2)}) collective-permute-start(bf16[8,4096]{1,0:T(8,128)(2,1)S(1)} %bitcast.43), channel_id=1, source_target_pairs={{0,9},{1,8},{2,11},{3,10},{4,13},{5,12},{6,15},{7,14},{8,1},{9,0},... | collective-permute-start | bytes 196616 | tf_op jit(solution)/shard_map/ppermute | solution.py:299
  34.0 0.0 collective-permute-done.7
  34.0 0.1 multiply_bitcast_fusion
  34.1 0.1 subtract_convert_fusion
  34.3 0.5 fusion.26
  34.8 0.2 multiply_reduce_fusion
  35.0 0.2 fusion.7
  35.3 0.3 fusion.1
  35.7 0.1 collective-permute-start.8
  35.7 0.5 collective-permute-done.9
  36.2 5.5 %collective-permute-start.11 = (bf16[16,4096]{1,0:T(8,128)(2,1)S(1)}, bf16[16,4096]{1,0:T(8,128)(2,1)S(1)}, u32[]{:S(2)}, u32[]{:S(2)}) collective-permute-start(bf16[16,4096]{1,0:T(8,128)(2,1)S(1)} %get-tuple-element.39), channel_id=1, source_target_pairs={{0,3},{1,4},{2,7},{3,0},{4,1},{5,6},{6,5},{7,2},{8,13},{9,10},{10,... | collective-permute-start | bytes 393224 | tf_op jit(solution)/shard_map/ppermute | solution.py:299
  41.8 0.5 collective-permute-done.8
  42.3 1.6 %collective-permute-start.10 = (bf16[16,4096]{1,0:T(8,128)(2,1)S(1)}, bf16[16,4096]{1,0:T(8,128)(2,1)S(1)}, u32[]{:S(2)}, u32[]{:S(2)}) collective-permute-start(bf16[16,4096]{1,0:T(8,128)(2,1)S(1)} %pad_maximum_fusion.1), channel_id=1, source_target_pairs={{0,3},{1,4},{2,7},{3,0},{4,1},{5,6},{6,5},{7,2},{8,13},{9,10},{10,... | collective-permute-start | bytes 393224 | tf_op jit(solution)/shard_map/ppermute | solution.py:299
  43.9 0.5 collective-permute-done.11
  44.4 0.1 collective-permute-start.14
  44.5 3.3 %collective-permute-done.10 = bf16[16,4096]{1,0:T(8,128)(2,1)S(1)} collective-permute-done((bf16[16,4096]{1,0:T(8,128)(2,1)S(1)}, bf16[16,4096]{1,0:T(8,128)(2,1)S(1)}, u32[]{:S(2)}, u32[]{:S(2)}) %collective-permute-start.10) | collective-permute-done | bytes 131104 | tf_op jit(solution)/shard_map/ppermute | solution.py:299
  47.8 0.1 collective-permute-start.12
  47.9 2.4 %collective-permute-done.14 = bf16[32,4096]{1,0:T(8,128)(2,1)S(1)} collective-permute-done((bf16[32,4096]{1,0:T(8,128)(2,1)S(1)}, bf16[32,4096]{1,0:T(8,128)(2,1)S(1)}, u32[]{:S(2)}, u32[]{:S(2)}) %collective-permute-start.14) | collective-permute-done | bytes 262176 | tf_op jit(solution)/shard_map/ppermute | solution.py:299
  50.3 0.1 collective-permute-start.15
  50.4 3.3 %collective-permute-done.12 = bf16[32,4096]{1,0:T(8,128)(2,1)S(1)} collective-permute-done((bf16[32,4096]{1,0:T(8,128)(2,1)S(1)}, bf16[32,4096]{1,0:T(8,128)(2,1)S(1)}, u32[]{:S(2)}, u32[]{:S(2)}) %collective-permute-start.12) | collective-permute-done | bytes 262176 | tf_op jit(solution)/shard_map/ppermute | solution.py:299
  53.7 0.1 collective-permute-start.13
  53.8 0.0 collective-permute-done.15.other_ref
  53.8 0.0 slice-done
  53.8 1.3 %shard_map.66.refs_0_ = f32[128,1024]{1,0:T(8,128)S(1)} custom-call(s32[1]{0:T(128)} %bitcast.me_ref, bf16[64,4096]{1,0:T(8,128)(2,1)S(1)} %constant_dynamic-update-slice_fusion.7.mine_ref, bf16[64,4096]{1,0:T(8,128)(2,1)S(1)} %collective-permute-done.15.other_ref, bf16[8192,1024]{1,0:T(8,128)(2,1)S(1)} %bitcast.30), custom_call_target="tpu_custom_call" | custom-call | flops 1073741824 | bytes 9699328 | tf_op jit(solution)/shard_map/pallas_call | solution.py:221
  55.1 0.5 collective-permute-done.13.other_ref
  55.7 2.0 %shard_map.67 = bf16[128,1024]{1,0:T(8,128)(2,1)} custom-call(s32[1]{0:T(128)} %bitcast.me_ref, bf16[64,4096]{1,0:T(8,128)(2,1)S(1)} %constant_dynamic-update-slice_fusion.5.mine_ref, bf16[64,4096]{1,0:T(8,128)(2,1)S(1)} %collective-permute-done.13.other_ref, bf16[8192,1024]{1,0:T(8,128)(2,1)S(1)} %bitcast.30, f32[128,1024]{1,0:T(8,128)S(1)} %shard_map.66.refs_0_), custom_call_target="tpu_custom_call" | custom-call | flops 1073741824 | bytes 9699328 | tf_op jit(solution)/shard_map/pallas_call | solution.py:221
  (37 shorter events, 0.6 us)
Async XLA Ops:
  7.6 2.3 %collective-permute-start = (bf16[64,5248]{1,0:T(8,128)(2,1)S(1)}, bf16[64,5248]{1,0:T(8,128)(2,1)S(1)}, u32[]{:S(2)}, u32[]{:S(2)}) collective-permute-start(bf16[64,5248]{1,0:T(8,128)(2,1)S(1)} %get-tuple-element.22), channel_id=1, source_target_pairs={{0,1},{1,0},{2,3},{3,2},{4,5},{5,4},{6,7},{7,6},{8,9},{9,8},{10,11... | collective-permute-start | bytes 2015240 | tf_op jit(solution)/shard_map/ppermute | solution.py:299
  8.2 6.5 %copy-start.1 = (bf16[8,256,4,128]{3,2,1,0:T(4,128)(2,1)S(1)}, bf16[8,256,4,128]{3,2,1,0:T(4,128)(2,1)}, u32[]{:S(2)}) copy-start(bf16[8,256,4,128]{3,2,1,0:T(4,128)(2,1)} %param.11) | copy-start | bytes 6291460
  8.2 45.6 %slice-start = ((s8[16777216]{0:T(1024)(128)(4,1)}), s8[4194304]{0:T(1024)(128)(4,1)S(1)}, s32[]{:S(2)}) async-start(s8[16777216]{0:T(1024)(128)(4,1)} %bitcast.29), calls=%async_computation | async-start | bytes 8388608
  9.4 4.8 %copy-start = (bf16[8,256,4,128]{3,2,1,0:T(4,128)(2,1)S(1)}, bf16[8,256,4,128]{3,2,1,0:T(4,128)(2,1)}, u32[]{:S(2)}) copy-start(bf16[8,256,4,128]{3,2,1,0:T(4,128)(2,1)} %param.10) | copy-start | bytes 6291460
  9.4 3.2 %collective-permute-start.4 = (bf16[64,4096]{1,0:T(8,128)(2,1)S(1)}, bf16[64,4096]{1,0:T(8,128)(2,1)S(1)}, u32[]{:S(2)}, u32[]{:S(2)}) collective-permute-start(bf16[64,4096]{1,0:T(8,128)(2,1)S(1)} %get-tuple-element.23), channel_id=1, source_target_pairs={{0,1},{1,0},{2,3},{3,2},{4,5},{5,4},{6,7},{7,6},{8,9},{9,8},{10,11... | collective-permute-start | bytes 1572872 | tf_op jit(solution)/shard_map/ppermute | solution.py:299
  9.9 43.9 %slice-start.1 = ((s8[16777216]{0:T(1024)(128)(4,1)}), s8[4194304]{0:T(1024)(128)(4,1)S(1)}, s32[]{:S(2)}) async-start(s8[16777216]{0:T(1024)(128)(4,1)} %bitcast.29), calls=%async_computation.1 | async-start | bytes 8388608
  10.0 7.5 %collective-permute-start.1 = (bf16[32,5248]{1,0:T(8,128)(2,1)S(1)}, bf16[32,5248]{1,0:T(8,128)(2,1)S(1)}, u32[]{:S(2)}, u32[]{:S(2)}) collective-permute-start(bf16[32,5248]{1,0:T(8,128)(2,1)S(1)} %add_convert_fusion), channel_id=1, source_target_pairs={{0,3},{1,4},{2,7},{3,0},{4,1},{5,6},{6,5},{7,2},{8,13},{9,10},{10,... | collective-permute-start | bytes 1007624 | tf_op jit(solution)/shard_map/ppermute | solution.py:299
  12.7 7.6 %collective-permute-start.5 = (bf16[32,4096]{1,0:T(8,128)(2,1)S(1)}, bf16[32,4096]{1,0:T(8,128)(2,1)S(1)}, u32[]{:S(2)}, u32[]{:S(2)}) collective-permute-start(bf16[32,4096]{1,0:T(8,128)(2,1)S(1)} %add_convert_fusion.1), channel_id=1, source_target_pairs={{0,3},{1,4},{2,7},{3,0},{4,1},{5,6},{6,5},{7,2},{8,13},{9,10},{10,... | collective-permute-start | bytes 786440 | tf_op jit(solution)/shard_map/ppermute | solution.py:299
  14.7 39.1 %slice-start.2 = ((s8[16777216]{0:T(1024)(128)(4,1)}), s8[4194304]{0:T(1024)(128)(4,1)S(1)}, s32[]{:S(2)}) async-start(s8[16777216]{0:T(1024)(128)(4,1)} %bitcast.29), calls=%async_computation.2 | async-start | bytes 8388608
  17.6 6.5 %collective-permute-start.2 = (bf16[16,5248]{1,0:T(8,128)(2,1)S(1)}, bf16[16,5248]{1,0:T(8,128)(2,1)S(1)}, u32[]{:S(2)}, u32[]{:S(2)}) collective-permute-start(bf16[16,5248]{1,0:T(8,128)(2,1)S(1)} %add_convert_fusion.2), channel_id=1, source_target_pairs={{0,5},{1,8},{2,11},{3,6},{4,13},{5,0},{6,3},{7,14},{8,1},{9,12},{1... | collective-permute-start | bytes 503816 | tf_op jit(solution)/shard_map/ppermute | solution.py:299
  20.4 6.7 %collective-permute-start.6 = (bf16[16,4096]{1,0:T(8,128)(2,1)S(1)}, bf16[16,4096]{1,0:T(8,128)(2,1)S(1)}, u32[]{:S(2)}, u32[]{:S(2)}) collective-permute-start(bf16[16,4096]{1,0:T(8,128)(2,1)S(1)} %add_convert_fusion.3), channel_id=1, source_target_pairs={{0,5},{1,2},{2,1},{3,6},{4,7},{5,0},{6,3},{7,4},{8,11},{9,12},{10,... | collective-permute-start | bytes 393224 | tf_op jit(solution)/shard_map/ppermute | solution.py:299
  24.1 5.1 %collective-permute-start.3 = (bf16[8,5248]{1,0:T(8,128)(2,1)S(1)}, bf16[8,5248]{1,0:T(8,128)(2,1)S(1)}, u32[]{:S(2)}, u32[]{:S(2)}) collective-permute-start(bf16[8,5248]{1,0:T(8,128)(2,1)S(1)} %add_convert_fusion.4), channel_id=1, source_target_pairs={{0,9},{1,2},{2,1},{3,10},{4,7},{5,12},{6,15},{7,4},{8,11},{9,0},{1... | collective-permute-start | bytes 251912 | tf_op jit(solution)/shard_map/ppermute | solution.py:299
  27.1 6.9 %collective-permute-start.7 = (bf16[8,4096]{1,0:T(8,128)(2,1)S(1)}, bf16[8,4096]{1,0:T(8,128)(2,1)S(1)}, u32[]{:S(2)}, u32[]{:S(2)}) collective-permute-start(bf16[8,4096]{1,0:T(8,128)(2,1)S(1)} %add_convert_fusion.6), channel_id=1, source_target_pairs={{0,9},{1,8},{2,11},{3,10},{4,13},{5,12},{6,15},{7,14},{8,1},{9,0},... | collective-permute-start | bytes 196616 | tf_op jit(solution)/shard_map/ppermute | solution.py:299
  30.9 22.9 %slice-start.3 = ((s8[16777216]{0:T(1024)(128)(4,1)}), s8[4194304]{0:T(1024)(128)(4,1)S(1)}, s32[]{:S(2)}) async-start(s8[16777216]{0:T(1024)(128)(4,1)} %bitcast.29), calls=%async_computation.3 | async-start | bytes 8388608
  31.3 4.9 %collective-permute-start.9 = (bf16[8,4096]{1,0:T(8,128)(2,1)S(1)}, bf16[8,4096]{1,0:T(8,128)(2,1)S(1)}, u32[]{:S(2)}, u32[]{:S(2)}) collective-permute-start(bf16[8,4096]{1,0:T(8,128)(2,1)S(1)} %bitcast.43), channel_id=1, source_target_pairs={{0,9},{1,8},{2,11},{3,10},{4,13},{5,12},{6,15},{7,14},{8,1},{9,0},... | collective-permute-start | bytes 196616 | tf_op jit(solution)/shard_map/ppermute | solution.py:299
  35.7 6.6 %collective-permute-start.8 = (bf16[8,4096]{1,0:T(8,128)(2,1)S(1)}, bf16[8,4096]{1,0:T(8,128)(2,1)S(1)}, u32[]{:S(2)}, u32[]{:S(2)}) collective-permute-start(bf16[8,4096]{1,0:T(8,128)(2,1)S(1)} %bitcast.39), channel_id=1, source_target_pairs={{0,9},{1,8},{2,11},{3,10},{4,13},{5,12},{6,15},{7,14},{8,1},{9,0},... | collective-permute-start | bytes 196616 | tf_op jit(solution)/shard_map/ppermute | solution.py:299
  36.2 8.2 %collective-permute-start.11 = (bf16[16,4096]{1,0:T(8,128)(2,1)S(1)}, bf16[16,4096]{1,0:T(8,128)(2,1)S(1)}, u32[]{:S(2)}, u32[]{:S(2)}) collective-permute-start(bf16[16,4096]{1,0:T(8,128)(2,1)S(1)} %get-tuple-element.39), channel_id=1, source_target_pairs={{0,3},{1,4},{2,7},{3,0},{4,1},{5,6},{6,5},{7,2},{8,13},{9,10},{10,... | collective-permute-start | bytes 393224 | tf_op jit(solution)/shard_map/ppermute | solution.py:299
  42.3 5.5 %collective-permute-start.10 = (bf16[16,4096]{1,0:T(8,128)(2,1)S(1)}, bf16[16,4096]{1,0:T(8,128)(2,1)S(1)}, u32[]{:S(2)}, u32[]{:S(2)}) collective-permute-start(bf16[16,4096]{1,0:T(8,128)(2,1)S(1)} %pad_maximum_fusion.1), channel_id=1, source_target_pairs={{0,3},{1,4},{2,7},{3,0},{4,1},{5,6},{6,5},{7,2},{8,13},{9,10},{10,... | collective-permute-start | bytes 393224 | tf_op jit(solution)/shard_map/ppermute | solution.py:299
  44.4 5.9 %collective-permute-start.14 = (bf16[32,4096]{1,0:T(8,128)(2,1)S(1)}, bf16[32,4096]{1,0:T(8,128)(2,1)S(1)}, u32[]{:S(2)}, u32[]{:S(2)}) collective-permute-start(bf16[32,4096]{1,0:T(8,128)(2,1)S(1)} %get-tuple-element.36), channel_id=1, source_target_pairs={{0,5},{1,2},{2,1},{3,6},{4,7},{5,0},{6,3},{7,4},{8,11},{9,12},{10,... | collective-permute-start | bytes 786440 | tf_op jit(solution)/shard_map/ppermute | solution.py:299
  47.8 5.9 %collective-permute-start.12 = (bf16[32,4096]{1,0:T(8,128)(2,1)S(1)}, bf16[32,4096]{1,0:T(8,128)(2,1)S(1)}, u32[]{:S(2)}, u32[]{:S(2)}) collective-permute-start(bf16[32,4096]{1,0:T(8,128)(2,1)S(1)} %pad_maximum_fusion), channel_id=1, source_target_pairs={{0,5},{1,2},{2,1},{3,6},{4,7},{5,0},{6,3},{7,4},{8,11},{9,12},{10,... | collective-permute-start | bytes 786440 | tf_op jit(solution)/shard_map/ppermute | solution.py:299
  50.3 3.5 %collective-permute-start.15 = (bf16[64,4096]{1,0:T(8,128)(2,1)S(1)}, bf16[64,4096]{1,0:T(8,128)(2,1)S(1)}, u32[]{:S(2)}, u32[]{:S(2)}) collective-permute-start(bf16[64,4096]{1,0:T(8,128)(2,1)S(1)} %constant_dynamic-update-slice_fusion.7.mine_ref), channel_id=1, source_target_pairs={{0,1},{1,0},{2,3},{3,2},{4,5},{5,4},{6,7},{7,6},{8,9},{9,8},{10,11... | collective-permute-start | bytes 1572872 | tf_op jit(solution)/shard_map/ppermute | solution.py:299
  53.7 2.0 %collective-permute-start.13 = (bf16[64,4096]{1,0:T(8,128)(2,1)S(1)}, bf16[64,4096]{1,0:T(8,128)(2,1)S(1)}, u32[]{:S(2)}, u32[]{:S(2)}) collective-permute-start(bf16[64,4096]{1,0:T(8,128)(2,1)S(1)} %constant_dynamic-update-slice_fusion.5.mine_ref), channel_id=1, source_target_pairs={{0,1},{1,0},{2,3},{3,2},{4,5},{5,4},{6,7},{7,6},{8,9},{9,8},{10,11... | collective-permute-start | bytes 1572872 | tf_op jit(solution)/shard_map/ppermute | solution.py:299
